TPU v7x, 512 devices: a whole 4x4x16 slice. The times are simulated.
512 devices in a mesh: layer: 4 (over y), row: 4 (over x), col: 32 (over z, core).
Axes of the slice: x: 4, y: 4, z: 16, core: 2. Of those that a mesh axis runs over, the one named last changes fastest.
Arguments:
- leaf_rhs: bfloat16 [1024, 128, 256], P(('layer', 'row', 'col')), may hold values from -6 to 6
- leaf_lower_inv: bfloat16 [1024, 128, 128], P(('layer', 'row', 'col'))
- leaf_upper_inv: bfloat16 [1024, 128, 128], P(('layer', 'row', 'col'))
- leaf_lower: bfloat16 [1024, 4, 128, 128], P(('layer', 'row', 'col')), may hold values from -0.125 to 0.125
- leaf_upper: bfloat16 [1024, 4, 128, 128], P(('layer', 'row', 'col')), may hold values from -0.25 to 0.25
- targets: int32 [1024, 4], P(('layer', 'row', 'col')), may hold values from 0 to 63, as said below
- sep_rhs: float32 [256, 128, 256], P(('row', 'col')), may hold values from -6 to 6
- sep_lower_inv: float32 [256, 128, 128], P(('row', 'col')), as said below
- sep_upper_inv: float32 [256, 128, 128], P(('row', 'col')), as said below
- sep_lower_link: float32 [256, 128, 128], P(('row', 'col'))
- sep_upper_link: float32 [256, 128, 128], P(('row', 'col'))
Outputs:
- leaf_solution: bfloat16 [1024, 128, 256], P(('layer', 'row', 'col'))
- sep_solution: float32 [256, 128, 256], P(('row', 'col'))
Inputs may be any that keep to these rules, and one draw needn't show every extreme that they name: Each leaf names 4 different separators of its own grid row; separators t and u with t // 2 == u // 2 are owned by the same col index, and among the targets of one device's 2 leaves at most one separator of each such owner appears. `sep_lower_inv`: diagonally dominant blocks. `sep_upper_inv`: diagonally dominant blocks.
All inputs are finite; a program needn't handle non-finite values.
Results may differ from a plain program's by a relative error of at most 0.007.
Values may be sent and summed in bfloat16 or wider, within the bound.
No kernel may reach another device: no remote copies, remote signals or barrier semaphores. Data moves between devices by JAX's collectives and lax.ppermute only.
A program may use at most 128 MiB of HBM per device.

v0:
```python
import jax
import jax.numpy as jnp
from jax import lax
from jax.sharding import PartitionSpec as P

highest = lax.Precision.HIGHEST


def entering(value, axis, combine, identity, reverse):
    devices, place = (lax.axis_size(axis), lax.axis_index(axis))
    everything = jax.tree.map(lambda part: lax.all_gather(part, axis), value)
    start = jax.tree.map(
        lambda part, zero: jnp.broadcast_to(jnp.asarray(zero, part.dtype), part.shape),
        value,
        identity,
    )

    def turn(k, before):
        at = devices - 1 - k if reverse else k
        reached = at > place if reverse else at < place
        new = combine(before, jax.tree.map(lambda part: part[at], everything))
        return jax.tree.map(lambda a, b: jnp.where(reached, a, b), new, before)

    return lax.fori_loop(0, devices, turn, start)


def compose(earlier_map, later_map):
    return (
        jnp.dot(later_map[0], earlier_map[0], precision=highest),
        jnp.dot(later_map[0], earlier_map[1], precision=highest) + later_map[1],
    )


def on_device(
    leaf_rhs,
    leaf_lower_inv,
    leaf_upper_inv,
    leaf_lower,
    leaf_upper,
    targets,
    sep_rhs,
    sep_lower_inv,
    sep_upper_inv,
    sep_lower_link,
    sep_upper_link,
):
    sep_count = sep_rhs.shape[0]
    blocksize = sep_rhs.shape[1]
    col_count = lax.axis_size("col")
    forward_leaf = jnp.einsum(
        "kab,kbr->kar", leaf_lower_inv, leaf_rhs, preferred_element_type=jnp.float32
    ).astype(jnp.bfloat16)
    owners = targets // sep_count
    within = targets % sep_count
    owner_match = owners[:, :, None] == jnp.arange(col_count, dtype=jnp.int32)[None, None, :]
    owner_onehot = owner_match.astype(jnp.bfloat16)
    spread_lower = jnp.einsum(
        "kic,kiab->kcab", owner_onehot, leaf_lower, preferred_element_type=jnp.bfloat16
    )
    slot_sums = jnp.einsum(
        "kcab,kbr->car", spread_lower, forward_leaf, preferred_element_type=jnp.float32
    )
    slots = slot_sums.astype(jnp.bfloat16)
    local_index = jnp.max(jnp.where(owner_match, within[:, :, None], 0), axis=(0, 1))
    placed = local_index[:, None] == jnp.arange(sep_count, dtype=jnp.int32)[None, :]
    by_owner = jnp.where(
        placed[:, :, None, None], slots[:, None, :, :], jnp.zeros((), jnp.bfloat16)
    )
    received = lax.all_to_all(by_owner, "col", split_axis=0, concat_axis=0, tiled=True)
    col_total = jnp.sum(received.astype(jnp.float32), axis=0)
    layer_total = lax.psum(col_total, "layer")
    right_side = sep_rhs - layer_total
    columns = right_side.shape[2]
    identity_map = (
        jnp.eye(blocksize, dtype=jnp.float32),
        jnp.zeros((blocksize, columns), jnp.float32),
    )
    local_down = identity_map
    for position in range(sep_count):
        inverse = sep_lower_inv[position]
        step_map = (
            -jnp.dot(inverse, sep_lower_link[position], precision=highest),
            jnp.dot(inverse, right_side[position], precision=highest),
        )
        local_down = compose(local_down, step_map)
    prefix = entering(local_down, ("row", "col"), compose, identity_map, False)
    previous = prefix[1]
    chain_rows = []
    for position in range(sep_count):
        previous = jnp.dot(
            sep_lower_inv[position],
            right_side[position] - jnp.dot(sep_lower_link[position], previous, precision=highest),
            precision=highest,
        )
        chain_rows.append(previous)
    local_up = identity_map
    for position in reversed(range(sep_count)):
        inverse = sep_upper_inv[position]
        step_map = (
            -jnp.dot(inverse, sep_upper_link[position], precision=highest),
            jnp.dot(inverse, chain_rows[position], precision=highest),
        )
        local_up = compose(local_up, step_map)
    suffix = entering(local_up, ("row", "col"), compose, identity_map, True)
    following = suffix[1]
    solved_rows = [None] * sep_count
    for position in reversed(range(sep_count)):
        following = jnp.dot(
            sep_upper_inv[position],
            chain_rows[position] - jnp.dot(sep_upper_link[position], following, precision=highest),
            precision=highest,
        )
        solved_rows[position] = following
    sep_part = jnp.stack(solved_rows)
    solved_low = sep_part.astype(jnp.bfloat16)
    gathered = lax.all_gather(solved_low, "col", axis=0, tiled=True)
    picked = gathered[targets]
    back_updates = jnp.einsum(
        "kiab,kibr->kar", leaf_upper, picked, preferred_element_type=jnp.float32
    )
    residual = (forward_leaf.astype(jnp.float32) - back_updates).astype(jnp.bfloat16)
    leaf_solution = jnp.einsum(
        "kab,kbr->kar", leaf_upper_inv, residual, preferred_element_type=jnp.float32
    ).astype(jnp.bfloat16)
    return (leaf_solution, sep_part)


def solution(mesh):
    return jax.shard_map(
        on_device,
        mesh=mesh,
        in_specs=(
            P(("layer", "row", "col"), None, None),
            P(("layer", "row", "col"), None, None),
            P(("layer", "row", "col"), None, None),
            P(("layer", "row", "col"), None, None, None),
            P(("layer", "row", "col"), None, None, None),
            P(("layer", "row", "col"), None),
            P(("row", "col"), None, None),
            P(("row", "col"), None, None),
            P(("row", "col"), None, None),
            P(("row", "col"), None, None),
            P(("row", "col"), None, None),
        ),
        out_specs=(P(("layer", "row", "col"), None, None), P(("row", "col"), None, None)),
        check_vma=False,
    )
```

profile of v0, /device:TPU:1, one launch (start us, length us, event | category | flops | bytes accessed | tf_op | source)
XLA Modules:
  0.0 1091.5 jit_solution(10009844366539806647)
XLA Ops:
  11.0 1.4 bitcast_convert_fusion
  12.4 2.3 broadcast_select_fusion
  14.7 16.9 %all-to-all-start = ((bf16[32,2,128,256]{3,2,1,0:T(8,128)(2,1)}), bf16[32,2,128,256]{3,2,1,0:T(8,128)(2,1)}, u32[]{:S(2)}, u32[]{:S(2)}) async-start(bf16[32,2,128,256]{3,2,1,0:T(8,128)(2,1)} %broadcast_select_fusion), calls=%async_computation | async-start | bytes 8388608 | tf_op jit(solution)/shard_map/all_to_all | solution.py:69
  32.2 182.7 %all-to-all-done = bf16[32,2,128,256]{3,2,1,0:T(8,128)(2,1)} async-done(((bf16[32,2,128,256]{3,2,1,0:T(8,128)(2,1)}), bf16[32,2,128,256]{3,2,1,0:T(8,128)(2,1)}, u32[]{:S(2)}, u32[]{:S(2)}) %all-to-all-start) | async-done | bytes 4194336 | tf_op jit(solution)/shard_map/all_to_all | solution.py:69
  214.9 2.9 convert_reduce_fusion
  220.1 52.8 %all-reduce.2.cloned.1.call-done = f32[2,128,256]{1,2,0:T(8,128)} async-done(((f32[2,128,256]{1,2,0:T(8,128)}), f32[2,128,256]{1,2,0:T(8,128)}) %all-reduce.2.cloned.1.call-update) | async-done | bytes 262160 | tf_op jit(solution)/shard_map/psum | solution.py:71
  277.3 92.9 %all-gather.12.cloned.1.call-done = f32[16384,128]{1,0:T(8,128)} async-done(((f32[128,128]{1,0:T(8,128)}), f32[16384,128]{1,0:T(8,128)}) %all-gather.12.cloned.1.call-update) | async-done | bytes 8388624 | tf_op jit(solution)/shard_map/all_gather | solution.py:11
  370.2 157.6 %all-gather.14.cloned.1.call-done = f32[16384,256]{1,0:T(8,128)} async-done(((f32[128,256]{1,0:T(8,128)}), f32[16384,256]{1,0:T(8,128)}) %all-gather.14.cloned.1.call-update) | async-done | bytes 16777232 | tf_op jit(solution)/shard_map/all_gather | solution.py:11
  527.9 162.0 %while.30 = (s32[]{:T(128)}, f32[128,256]{1,0:T(8,128)S(1)}, s32[]{:T(128)}, f32[128,128,128]{2,1,0:T(8,128)}, f32[128,128,256]{2,1,0:T(8,128)}, /*index=5*/s32[]{:T(128)}, s32[]{:T(128)}) while((s32[]{:T(128)}, f32[128,256]{1,0:T(8,128)S(1)}, s32[]{:T(128)}, f32[128,128,128]{2,1,0:T(8,128)}, f32[128,128,256]{2,1,0:T(8,128)}, ...), condition=%wide.region_4.5_spmd.clone, body=%wide.region_3.4_spmd.clone.sunk | while | flops 50462724 | bytes 854623 | solution.py:24
  534.2 1.2 fusion.124
  546.8 1.2 fusion.124
  548.1 1.2 fusion.124
  549.3 1.2 fusion.124
  553.1 1.2 fusion.124
  559.4 1.2 fusion.124
  565.8 1.2 fusion.124
  577.1 1.2 fusion.124
  580.9 1.2 fusion.124
  583.4 1.2 fusion.124
  594.8 1.2 fusion.124
  607.4 1.2 fusion.124
  612.5 1.2 fusion.124
  617.6 1.3 fusion.124
  618.9 1.2 fusion.124
  620.2 1.2 fusion.124
  621.4 1.3 fusion.124
  622.8 1.2 fusion.124
  629.1 1.2 fusion.124
  630.4 1.2 fusion.124
  632.9 1.3 fusion.124
  634.2 1.2 fusion.124
  636.7 1.2 fusion.124
  638.0 1.2 fusion.124
  645.6 1.2 fusion.124
  646.9 1.2 fusion.124
  648.1 1.2 fusion.124
  649.4 1.2 fusion.124
  651.9 1.2 fusion.124
  653.2 1.2 fusion.124
  660.8 1.2 fusion.124
  662.1 1.3 fusion.124
  665.9 1.2 fusion.124
  669.7 1.2 fusion.124
  692.7 153.7 %all-gather.18.cloned.1.call-done = f32[16384,256]{1,0:T(8,128)} async-done(((f32[128,256]{1,0:T(8,128)}), f32[16384,256]{1,0:T(8,128)}) %all-gather.18.cloned.1.call-update) | async-done | bytes 16777232 | tf_op jit(solution)/shard_map/all_gather | solution.py:11
  846.4 162.5 %while.31 = (s32[]{:T(128)}, f32[128,256]{1,0:T(8,128)S(1)}, s32[]{:T(128)}, f32[128,128,128]{2,1,0:T(8,128)}, f32[128,128,256]{2,1,0:T(8,128)}, /*index=5*/s32[]{:T(128)}, s32[]{:T(128)}, s32[]{:T(128)}, s32[]{:T(128)}) while((s32[]{:T(128)}, f32[128,256]{1,0:T(8,128)S(1)}, s32[]{:T(128)}, f32[128,128,128]{2,1,0:T(8,128)}, ...), condition=%wide.region_6.7_spmd.clone, body=%wide.region_5.6_spmd.clone.sunk | while | flops 50462728 | bytes 854685 | solution.py:24
  846.4 1.2 fusion.127
  1012.0 67.9 %all-gather.10.cloned.1.call-done = bf16[64,128,256]{2,1,0:T(8,128)(2,1)} async-done(((bf16[2,128,256]{2,1,0:T(8,128)(2,1)}), bf16[64,128,256]{2,1,0:T(8,128)(2,1)}) %all-gather.10.cloned.1.call-update) | async-done | bytes 4194320 | tf_op jit(solution)/shard_map/all_gather | solution.py:116
  1079.9 2.8 gather_fusion
  (550 shorter events, 288.0 us)
Async XLA Ops:
  8.0 1.0 copy-start
  14.7 17.0 %copy-start.2 = (f32[2,128,128]{2,1,0:T(8,128)S(1)}, f32[2,128,128]{2,1,0:T(8,128)}, u32[]{:S(2)}) copy-start(f32[2,128,128]{2,1,0:T(8,128)} %param.22) | copy-start | bytes 393220
  14.7 17.0 %copy-start.4 = (f32[2,128,128]{2,1,0:T(8,128)S(1)}, f32[2,128,128]{2,1,0:T(8,128)}, u32[]{:S(2)}) copy-start(f32[2,128,128]{2,1,0:T(8,128)} %param.24) | copy-start | bytes 393220
  14.7 200.2 %all-to-all-start = ((bf16[32,2,128,256]{3,2,1,0:T(8,128)(2,1)}), bf16[32,2,128,256]{3,2,1,0:T(8,128)(2,1)}, u32[]{:S(2)}, u32[]{:S(2)}) async-start(bf16[32,2,128,256]{3,2,1,0:T(8,128)(2,1)} %broadcast_select_fusion), calls=%async_computation | async-start | bytes 8388608 | tf_op jit(solution)/shard_map/all_to_all | solution.py:69
  31.7 188.1 %copy-start.7 = (f32[2,128,256]{2,1,0:T(8,128)S(1)}, f32[2,128,256]{2,1,0:T(8,128)}, u32[]{:S(2)}) copy-start(f32[2,128,256]{2,1,0:T(8,128)} %param.21) | copy-start | bytes 786436
  31.7 241.3 %all-reduce.2.cloned.1.call-start = ((), (), s32[]{:S(2)}) async-start(), calls=%async_computation.1 | async-start | bytes 524288 | tf_op jit(solution)/shard_map/psum | solution.py:71
  32.2 243.4 %copy-start.3 = (f32[2,128,128]{2,1,0:T(8,128)S(1)}, f32[2,128,128]{2,1,0:T(8,128)}, u32[]{:S(2)}) copy-start(f32[2,128,128]{2,1,0:T(8,128)} %param.23) | copy-start | bytes 393220
  32.2 243.3 %copy-start.5 = (f32[2,128,128]{2,1,0:T(8,128)S(1)}, f32[2,128,128]{2,1,0:T(8,128)}, u32[]{:S(2)}) copy-start(f32[2,128,128]{2,1,0:T(8,128)} %param.25) | copy-start | bytes 393220
  218.7 151.6 %all-gather.12.cloned.1.call-start = ((), (), s32[]{:S(2)}) async-start(), calls=%async_computation.3 | async-start | bytes 8454144 | tf_op jit(solution)/shard_map/all_gather | solution.py:11
  219.8 308.1 %all-gather.14.cloned.1.call-start = ((), (), s32[]{:S(2)}) async-start(), calls=%async_computation.4 | async-start | bytes 16908288 | tf_op jit(solution)/shard_map/all_gather | solution.py:11
  275.5 417.3 %all-gather.16.cloned.1.call-start = ((), (), s32[]{:S(2)}) async-start(), calls=%async_computation.5 | async-start | bytes 8454144 | tf_op jit(solution)/shard_map/all_gather | solution.py:11
  277.0 569.4 %all-gather.18.cloned.1.call-start = ((), (), s32[]{:S(2)}) async-start(), calls=%async_computation.6 | async-start | bytes 16908288 | tf_op jit(solution)/shard_map/all_gather | solution.py:11
  692.6 390.0 %copy-start.6 = (bf16[2,4,128,128]{3,2,1,0:T(8,128)(2,1)S(1)}, bf16[2,4,128,128]{3,2,1,0:T(8,128)(2,1)}, u32[]{:S(2)}) copy-start(bf16[2,4,128,128]{3,2,1,0:T(8,128)(2,1)} %param.19) | copy-start | bytes 786436
  692.6 390.0 %copy-start.8 = (bf16[2,128,128]{2,1,0:T(8,128)(2,1)S(1)}, bf16[2,128,128]{2,1,0:T(8,128)(2,1)}, u32[]{:S(2)}) copy-start(bf16[2,128,128]{2,1,0:T(8,128)(2,1)} %param.17) | copy-start | bytes 196612
  692.7 387.2 %all-gather.10.cloned.1.call-start = ((), (), s32[]{:S(2)}) async-start(), calls=%async_computation.2 | async-start | bytes 4325376 | tf_op jit(solution)/shard_map/all_gather | solution.py:116
  846.4 237.5 %copy-start.1 = (bf16[2,4,128,128]{3,2,1,0:T(8,128)(2,1)S(1)}, bf16[2,4,128,128]{3,2,1,0:T(8,128)(2,1)}, u32[]{:S(2)}) copy-start(bf16[2,4,128,128]{3,2,1,0:T(8,128)(2,1)} %param.18) | copy-start | bytes 786436
Sparse Core Ops, SparseCore 0:
  218.8 54.1 all-reduce.1
  1011.2 68.6 all-gather.9
Sparse Core Ops, SparseCore 1:
  222.8 147.4 all-gather.11
  374.3 153.5 all-gather.13
  531.9 142.7 all-gather.15
  692.7 153.6 all-gather.17
where the time goes:
time: 1100 us; the launch traced here: 1090 us
  waiting for transfers between devices  708 us (64%)
  matrix products  324 us (29%)
  starting transfers between devices  17.2 us (2%)
  between operations  16.1 us (1%)
    all_gather x4, waiting for transfers between devices, entering(): everything = jax.tree.map(lambda part: lax.all_gather(part, axis), value)  404 us
    dot_general x260, matrix products, compose(): jnp.dot(later_map[0], earlier_map[1], precision=highest) + later_map[1]  312 us
    all_to_all x1, waiting for transfers between devices, on_device(): lax.all_to_all(by_owner, 'col', split_axis=0, concat_axis=0, tiled=True)  183 us
    all_gather x1, waiting for transfers between devices, on_device(): gathered = lax.all_gather(solved_low, 'col', axis=0, tiled=True)  67.9 us
    psum x1, waiting for transfers between devices, on_device(): layer_total = lax.psum(col_total, 'layer')  52.8 us
  transfers between devices with their start and end apart: 7, of which 6 were waited for; matrix products, arithmetic and copies ran while one was open for 15% of the time, Pallas kernels for 0%

commit v1 on v0

v1 whole, which is shorter than its diff:
```python
import jax
import jax.numpy as jnp
from jax import lax
from jax.experimental import pallas as pl
from jax.experimental.pallas import tpu as pltpu
from jax.sharding import Mesh
from jax.sharding import PartitionSpec as P

f32 = jnp.float32
bf16 = jnp.bfloat16

B = 128
VMEM_LIMIT = 40 * 1024 * 1024


def dot(a, b):
    return jnp.dot(a, b, preferred_element_type=f32)


def dot_nt(a, b):
    return lax.dot_general(a, b, (((1,), (1,)), ((), ())), preferred_element_type=f32)


def split(x):
    high = x.astype(bf16)
    return high, (x - high.astype(f32)).astype(bf16)


def mm(a, b):
    a_high, a_low = split(a)
    b_high, b_low = split(b)
    return dot(a_high, b_high) + (dot(a_low, b_high) + dot(a_high, b_low))


def call(kernel, outs, scratch=(), name=None, smem=()):
    def run(*operands):
        return pl.pallas_call(
            kernel,
            out_shape=outs,
            in_specs=[
                pl.BlockSpec(memory_space=pltpu.SMEM if k in smem else pltpu.VMEM)
                for k in range(len(operands))
            ],
            out_specs=jax.tree.map(lambda _: pl.BlockSpec(memory_space=pltpu.VMEM), outs),
            scratch_shapes=list(scratch),
            compiler_params=pltpu.CompilerParams(vmem_limit_bytes=VMEM_LIMIT),
            name=name,
        )(*operands)

    return run


def shaped(shape, dtype):
    return jax.ShapeDtypeStruct(shape, dtype)


def leaf_forward(rhs_ref, inv_ref, lower_ref, tgt_ref, out_ref):
    groups, width = out_ref.shape[0], 256 // out_ref.shape[0]
    for k in range(2):
        forward = dot(inv_ref[k], rhs_ref[k]).T.astype(bf16)
        for j in range(groups):
            out_ref[j, (8 + k) * width : (9 + k) * width] = forward[j * width : (j + 1) * width]
        for i in range(4):
            update = dot_nt(forward, lower_ref[k, i]).astype(bf16)
            slot = 4 * k + i
            for j in range(groups):
                out_ref[j, slot * width : (slot + 1) * width] = update[j * width : (j + 1) * width]
    for j in range(groups):
        out_ref[j, 10 * width :] = tgt_ref[...]


def scatter_updates(place_ref, got_ref, out_ref, total):
    width = out_ref.shape[-2]
    total[...] = jnp.zeros_like(total)
    for j in range(got_ref.shape[0]):
        for slot in range(8):
            s = place_ref[j, slot]
            total[s] = total[s] + got_ref[j, slot * width : (slot + 1) * width].astype(f32)
    out_ref[...] = total[...].reshape(out_ref.shape).astype(bf16)


def sep_prepare(at_ref, rhs_ref, li_ref, ll_ref, ui_ref, ul_ref, out_ref, turned):
    width = out_ref.shape[2] - 4 * B
    for s in range(2):
        turned[s] = rhs_ref[s].T
        li, ui = li_ref[s], ui_ref[s]
        blocks = (-mm(li, ll_ref[s]).T, -mm(ui, ul_ref[s]).T, li.T, ui.T)
        for c in range(2):
            for k in range(4):
                out_ref[c, s, k * B : (k + 1) * B] = blocks[k]
            first = pl.multiple_of((2 * at_ref[0] + c) * width, width)
            out_ref[c, s, 4 * B :] = turned[s, pl.ds(first, width)]


def chip_maps(sep_ref, pqr_ref, wy_ref):
    def block(s, k):
        return sep_ref[s // 2, s % 2, k * B : (k + 1) * B]

    reach = [block(0, 0)]
    for s in range(1, 4):
        reach.append(mm(reach[-1], block(s, 0)))
    w = mm(reach[3], block(3, 3))
    y = block(3, 1)
    wy = jnp.concatenate([w, y], axis=0)
    wy_ref[:, 3 * B :] = wy
    for s in (2, 1, 0):
        wy = mm(wy, block(s, 1))
        wy = jnp.concatenate([wy[:B] + mm(reach[s], block(s, 3)), wy[B:]], axis=0)
        wy_ref[:, s * B : (s + 1) * B] = wy
    for n in range(pqr_ref.shape[0]):
        pqr_ref[n, 0] = reach[3]
        pqr_ref[n, 1] = wy[B:]
        pqr_ref[n, 2] = wy[:B]


def chip_solve(got_ref, sep_ref, bg_ref, local_ref):
    total = jnp.sum(got_ref[...].astype(f32), axis=0)

    def block(s, k):
        return sep_ref[s // 2, s % 2, k * B : (k + 1) * B]

    base = [
        mm(sep_ref[s // 2, s % 2, 4 * B :] - total[s], block(s, 2)) for s in range(4)
    ]
    f = base[0]
    forward = [f]
    for s in range(1, 4):
        f = mm(f, block(s, 0)) + base[s]
        forward.append(f)
    bent = [mm(forward[s], block(s, 3)) for s in range(4)]
    u = bent[3]
    local_ref[3] = u
    for s in (2, 1, 0):
        u = mm(u, block(s, 1)) + bent[s]
        local_ref[s] = u
    for n in range(bg_ref.shape[0]):
        bg_ref[n, 0] = f
        bg_ref[n, 1] = u


def level_maps(axis):
    def kernel(at_ref, maps_ref, pqr_ref, xyz_ref, keep):
        count = maps_ref.shape[0]
        identity = (
            lax.broadcasted_iota(jnp.int32, (B, B), 0) == lax.broadcasted_iota(jnp.int32, (B, B), 1)
        ).astype(f32)
        x = identity
        keep[0, 0] = x
        xs = [x]
        for q in range(count):
            x = maps_ref[0, 0] if q == 0 else mm(x, maps_ref[q, 0])
            xs.append(x)
            if q + 1 < count:
                keep[q + 1, 0] = x
        zy = jnp.concatenate([jnp.zeros((B, B), f32), identity], axis=0)
        for q in reversed(range(count)):
            keep[q, 1] = zy[B:]
            keep[q, 2] = zy[:B]
            if q == count - 1:
                zy = jnp.concatenate([mm(xs[q], maps_ref[q, 2]), maps_ref[q, 1]], axis=0)
            else:
                turned = maps_ref[0, 2] if q == 0 else mm(xs[q], maps_ref[q, 2])
                zy = mm(zy, maps_ref[q, 1])
                zy = jnp.concatenate([zy[:B] + turned, zy[B:]], axis=0)
        xyz_ref[...] = keep[at_ref[axis]]
        for n in range(pqr_ref.shape[0]):
            pqr_ref[n, 0] = xs[count]
            pqr_ref[n, 1] = zy[B:]
            pqr_ref[n, 2] = zy[:B]

    return kernel


def level_chain(maps_ref, bg_ref, keep):
    count = maps_ref.shape[0]
    f = jnp.zeros(bg_ref.shape[2:], f32)
    entering = []
    for q in range(count):
        keep[q, 0] = f
        entering.append(f)
        f = bg_ref[0, 0] if q == 0 else mm(f, maps_ref[q, 0]) + bg_ref[q, 0]
    u = jnp.zeros_like(f)
    for q in reversed(range(count)):
        keep[q, 1] = u
        turned = bg_ref[q, 1]
        if q > 0:
            turned = turned + mm(entering[q], maps_ref[q, 2])
        u = turned if q == count - 1 else mm(u, maps_ref[q, 1]) + turned
    return f, u


def level_solve(axis):
    def kernel(at_ref, maps_ref, bg_ref, out_ref, own_ref, keep):
        f, u = level_chain(maps_ref, bg_ref, keep)
        own_ref[...] = keep[at_ref[axis]]
        for n in range(out_ref.shape[0]):
            out_ref[n, 0] = f
            out_ref[n, 1] = u

    return kernel


def top_solve(at_ref, maps_ref, bg_ref, xyz_hi_ref, own_hi_ref, xyz_lo_ref, own_lo_ref, wy_ref, local_ref,
              sep_ref, low_ref, keep):
    level_chain(maps_ref, bg_ref, keep)
    place = at_ref[3]
    f, u = keep[place, 0], keep[place, 1]
    for xyz, own in ((xyz_hi_ref, own_hi_ref), (xyz_lo_ref, own_lo_ref)):
        f, u = (
            mm(f, xyz[0]) + own[0],
            mm(u, xyz[1]) + mm(f, xyz[2]) + own[1],
        )
    reached = mm(jnp.concatenate([f, u], axis=1), wy_ref[...])
    for s in range(4):
        value = local_ref[s] + reached[:, s * B : (s + 1) * B]
        for n in range(sep_ref.shape[0] // 2):
            sep_ref[2 * n + s // 2, s % 2] = value
        low = value.astype(bf16)
        for n in range(low_ref.shape[0]):
            low_ref[n, s] = low


def leaf_backward(place_ref, solved_ref, got_ref, upper_ref, inv_ref, out_ref):
    width = out_ref.shape[2]
    for j in range(out_ref.shape[0]):
        for k in range(2):
            total = jnp.zeros((width, B), f32)
            for i in range(4):
                total = total + dot_nt(solved_ref[place_ref[j, 4 * k + i]], upper_ref[j, k, i])
            forward = got_ref[j, (8 + k) * width : (9 + k) * width].astype(f32)
            out_ref[j, k] = dot_nt((forward - total).astype(bf16), inv_ref[j, k]).astype(bf16)


def turn_back(got_ref, out_ref):
    width = got_ref.shape[2]
    for s in range(out_ref.shape[0]):
        for j in range(got_ref.shape[0]):
            part = got_ref[j, s].astype(f32)
            out_ref[s, :, j * width : (j + 1) * width] = part.T.astype(out_ref.dtype)


def exchange(value, axes):
    return lax.all_to_all(value, axes, split_axis=0, concat_axis=0, tiled=True)


def on_device(
    leaf_rhs,
    leaf_lower_inv,
    leaf_upper_inv,
    leaf_lower,
    leaf_upper,
    targets,
    sep_rhs,
    sep_lower_inv,
    sep_upper_inv,
    sep_lower_link,
    sep_upper_link,
):
    across = ("layer", "core")
    layers, rows = lax.axis_size("layer"), lax.axis_size("row")
    highs, lows = lax.axis_size("zh"), lax.axis_size("zl")
    groups = 2 * layers
    width = 256 // groups
    chips = highs * lows
    at = jnp.stack(
        [lax.axis_index(name) for name in ("layer", "zl", "zh", "row")]
    ).astype(jnp.int32)

    mine = call(
        sep_prepare,
        shaped((2, 2, 4 * B + width, B), f32),
        [pltpu.VMEM((2, 256, B), f32)],
        "sep_prepare",
        (0,),
    )(at, sep_rhs, sep_lower_inv, sep_lower_link, sep_upper_inv, sep_upper_link)
    seps = exchange(mine, "core")
    pqr, wy = call(
        chip_maps,
        (shaped((lows, 3, B, B), f32), shaped((2 * B, 4 * B), f32)),
        name="chip_maps",
    )(seps)

    sent_targets = jnp.zeros((16, B), bf16).at[0, :8].set(targets.reshape(8).astype(bf16))
    sent = call(
        leaf_forward, shaped((groups, 10 * width + 16, B), bf16), name="leaf_forward"
    )(leaf_rhs, leaf_lower_inv, leaf_lower, sent_targets)
    upper = lax.all_gather(leaf_upper, across)
    upper_inv = lax.all_gather(leaf_upper_inv, across)
    got = exchange(sent, across)
    place = got[:, 10 * width, :8].astype(jnp.int32)
    sums = call(
        scatter_updates,
        shaped((chips, 4, width, B), bf16),
        [pltpu.VMEM((4 * chips, width, B), f32)],
        "scatter_updates",
        (0,),
    )(place, got)

    lo_maps = exchange(pqr, "zl")
    pqr_hi, xyz_lo = call(
        level_maps(1),
        (shaped((highs, 3, B, B), f32), shaped((3, B, B), f32)),
        [pltpu.VMEM((lows, 3, B, B), f32)],
        "maps_lo",
        (0,),
    )(at, lo_maps)
    hi_maps = exchange(pqr_hi, "zh")
    pqr_top, xyz_hi = call(
        level_maps(2),
        (shaped((rows, 3, B, B), f32), shaped((3, B, B), f32)),
        [pltpu.VMEM((highs, 3, B, B), f32)],
        "maps_hi",
        (0,),
    )(at, hi_maps)
    top_maps = exchange(pqr_top, "row")

    summed = exchange(sums, ("zh", "zl"))
    pair = (2, width, B)
    bg, local = call(
        chip_solve,
        (shaped((lows,) + pair, f32), shaped((4, width, B), f32)),
        name="chip_solve",
    )(summed, seps)
    bg, own_lo = call(
        level_solve(1),
        (shaped((highs,) + pair, f32), shaped(pair, f32)),
        [pltpu.VMEM((lows,) + pair, f32)],
        "solve_lo",
        (0,),
    )(at, lo_maps, exchange(bg, "zl"))
    bg, own_hi = call(
        level_solve(2),
        (shaped((rows,) + pair, f32), shaped(pair, f32)),
        [pltpu.VMEM((highs,) + pair, f32)],
        "solve_hi",
        (0,),
    )(at, hi_maps, exchange(bg, "zh"))
    solved, solved_low = call(
        top_solve,
        (shaped((groups, 2, width, B), f32), shaped((chips, 4, width, B), bf16)),
        [pltpu.VMEM((rows,) + pair, f32)],
        "top_solve",
        (0,),
    )(at, top_maps, exchange(bg, "row"), xyz_hi, own_hi, xyz_lo, own_lo, wy, local)

    low = exchange(solved_low, ("zh", "zl")).reshape(4 * chips, width, B)
    sep_part = call(turn_back, shaped((2, B, 256), f32), name="turn_sep")(exchange(solved, across))
    back = call(
        leaf_backward, shaped((groups, 2, width, B), bf16), name="leaf_backward", smem=(0,)
    )(place, low, got, upper, upper_inv)
    leaf_part = call(turn_back, shaped((2, B, 256), bf16), name="turn_leaf")(exchange(back, across))
    return (leaf_part, sep_part)


def solution(mesh):
    layers, rows, cols = (mesh.shape[name] for name in ("layer", "row", "col"))
    lows = 4
    fine = Mesh(
        mesh.devices.reshape(layers, rows, cols // (2 * lows), lows, 2),
        ("layer", "row", "zh", "zl", "core"),
    )
    leaf = ("layer", "row", "zh", "zl", "core")
    sep = ("row", "zh", "zl", "core")
    return jax.shard_map(
        on_device,
        mesh=fine,
        in_specs=(P(leaf),) * 6 + (P(sep),) * 5,
        out_specs=(P(leaf), P(sep)),
        check_vma=False,
    )
```

time: 1100 us -> 279 us (0.25)
  waiting for transfers between devices: 708 us -> 101 us
  matrix products: 324 us -> 0 us
  blocking collectives: 0 us -> 64.2 us
  starting transfers between devices: 17.2 us -> 65.1 us
  Pallas kernels: 0 us -> 26.6 us
    all_gather x5 -> x1, waiting for transfers between devices: 472 us -> 0.01 us  [on_device(): upper = lax.all_gather(leaf_upper, across)]
    dot_general x284 -> x0, matrix products: 324 us -> none  [the longest x260 312 us: compose(): jnp.dot(later_map[0], earlier_map[1], precision=highest) + later_map[1]]
    all_to_all x1 -> x9, waiting for transfers between devices: 183 us -> 100 us  [exchange(): return lax.all_to_all(value, axes, split_axis=0, concat_axis=0, tiled=True)]
    psum x1 -> x0, waiting for transfers between devices: 52.8 us -> none  [on_device(): layer_total = lax.psum(col_total, 'layer')]
    all_to_all x0 -> x3, blocking collectives: none -> 49.1 us  [exchange(): return lax.all_to_all(value, axes, split_axis=0, concat_axis=0, tiled=True)]
    all_to_all x1 -> x9, starting transfers between devices: 16.9 us -> 65 us  [exchange(): return lax.all_to_all(value, axes, split_axis=0, concat_axis=0, tiled=True)]
    pallas_call x0 -> x13, Pallas kernels: none -> 26.6 us  [run(): pl.pallas_call(kernel, out_shape=outs, in_specs=[pl.BlockSpec(memory_spac...]
    all_gather x0 -> x1, blocking collectives: none -> 15.2 us  [on_device(): upper_inv = lax.all_gather(leaf_upper_inv, across)]
  transfers between devices with their start and end apart: 7 -> 10, of which waited for: 6 -> 8; matrix products, arithmetic and copies ran while one was open for 15% -> 0% of each run, Pallas kernels for 0% -> 8%
where the time goes in v1:
time: 279 us; the launch traced here: 278 us
  waiting for transfers between devices  101 us (36%)
  starting transfers between devices  65.1 us (23%)
  blocking collectives  64.2 us (23%)
  Pallas kernels  26.6 us (10%)
  between operations  14.1 us (5%)
  local copies, waits for them, and re-layouts  6.09 us (2%)
    all_to_all x9, waiting for transfers between devices, exchange(): return lax.all_to_all(value, axes, split_axis=0, concat_axis=0, tiled=True)  100 us
    all_to_all x9, starting transfers between devices, exchange(): return lax.all_to_all(value, axes, split_axis=0, concat_axis=0, tiled=True)  65 us
    all_to_all x3, blocking collectives, exchange(): return lax.all_to_all(value, axes, split_axis=0, concat_axis=0, tiled=True)  49.1 us
    pallas_call x13, Pallas kernels, run(): pl.pallas_call(kernel, out_shape=outs, in_specs=[pl.BlockSpec(memory_spac...  26.6 us
    all_gather x1, blocking collectives, on_device(): upper_inv = lax.all_gather(leaf_upper_inv, across)  15.2 us
    unnamed x26, local copies, waits for them, and re-layouts  5.99 us
  transfers between devices with their start and end apart: 10, of which 8 were waited for; matrix products, arithmetic and copies ran while one was open for 0% of the time, Pallas kernels for 8%

profile of v1, /device:TPU:1, one launch (start us, length us, event | category | flops | bytes accessed | tf_op | source)
XLA Modules:
  0.0 278.1 jit_solution(361650959647904679)
XLA Ops:
  7.2 0.7 convert_element_type.16
  7.8 0.1 convert_element_type.17
  7.9 0.9 copy-done.4
  8.9 0.9 copy-done.6
  9.8 0.8 copy-done.11
  10.6 0.0 copy-start.10
  10.7 1.6 leaf_forward.1
  12.2 10.3 %all-to-all-start = ((bf16[8,336,128]{2,1,0:T(8,128)(2,1)}), bf16[8,336,128]{2,1,0:T(8,128)(2,1)S(1)}, u32[]{:S(2)}, u32[]{:S(2)}) async-start(bf16[8,336,128]{2,1,0:T(8,128)(2,1)} %leaf_forward.1), calls=%async_computation | async-start | bytes 1376256 | tf_op jit(solution)/shard_map/all_to_all | solution.py:243
  22.6 0.1 pad_add_fusion.at_ref
  22.6 0.0 copy-done.5
  22.7 1.9 sep_prepare.1
  24.6 9.2 %all-to-all-done.got_ref = bf16[8,336,128]{2,1,0:T(8,128)(2,1)S(1)} async-done(((bf16[8,336,128]{2,1,0:T(8,128)(2,1)}), bf16[8,336,128]{2,1,0:T(8,128)(2,1)S(1)}, u32[]{:S(2)}, u32[]{:S(2)}) %all-to-all-start) | async-done | bytes 688160 | tf_op jit(solution)/shard_map/all_to_all | solution.py:243
  33.8 4.5 %all-to-all-start.1 = ((f32[2,2,544,128]{3,2,1,0:T(8,128)}), f32[2,2,544,128]{3,2,1,0:T(8,128)S(1)}, u32[]{:S(2)}, u32[]{:S(2)}) async-start(f32[2,2,544,128]{3,2,1,0:T(8,128)} %sep_prepare.1), calls=%async_computation.1 | async-start | bytes 2228224 | tf_op jit(solution)/shard_map/all_to_all | solution.py:243
  38.3 1.7 scatter_updates.1
  40.0 0.1 all-to-all-done.1.sep_ref
  40.1 10.5 %all-to-all-start.5 = ((bf16[16,4,32,128]{3,2,1,0:T(8,128)(2,1)}), bf16[16,4,32,128]{3,2,1,0:T(8,128)(2,1)S(1)}, u32[]{:S(2)}, u32[]{:S(2)}) async-start(bf16[16,4,32,128]{3,2,1,0:T(8,128)(2,1)} %scatter_updates.1), calls=%async_computation.5 | async-start | bytes 1048576 | tf_op jit(solution)/shard_map/all_to_all | solution.py:243
  50.6 1.4 chip_maps.1
  52.0 0.9 copy-done.1
  52.9 0.8 copy-done.2
  53.7 19.7 %all-to-all-done.5.got_ref = bf16[16,4,32,128]{3,2,1,0:T(8,128)(2,1)S(1)} async-done(((bf16[16,4,32,128]{3,2,1,0:T(8,128)(2,1)}), bf16[16,4,32,128]{3,2,1,0:T(8,128)(2,1)S(1)}, u32[]{:S(2)}, u32[]{:S(2)}) %all-to-all-start.5) | async-done | bytes 524320 | tf_op jit(solution)/shard_map/all_to_all | solution.py:243
  73.4 8.2 %all-to-all-start.2 = ((f32[4,3,128,128]{3,2,1,0:T(8,128)}), f32[4,3,128,128]{3,2,1,0:T(8,128)S(1)}, u32[]{:S(2)}, u32[]{:S(2)}) async-start(f32[4,3,128,128]{3,2,1,0:T(8,128)} %copy-done.1), calls=%async_computation.2 | async-start | bytes 1572864 | tf_op jit(solution)/shard_map/all_to_all | solution.py:243
  81.6 1.2 chip_solve.1
  82.8 18.1 %all-to-all-done.2.maps_ref = f32[4,3,128,128]{3,2,1,0:T(8,128)S(1)} async-done(((f32[4,3,128,128]{3,2,1,0:T(8,128)}), f32[4,3,128,128]{3,2,1,0:T(8,128)S(1)}, u32[]{:S(2)}, u32[]{:S(2)}) %all-to-all-start.2) | async-done | bytes 786464 | tf_op jit(solution)/shard_map/all_to_all | solution.py:243
  100.9 7.1 %all_to_all.60.bg_ref = f32[4,2,32,128]{3,2,1,0:T(8,128)S(1)} all-to-all(f32[4,2,32,128]{3,2,1,0:T(8,128)S(1)} %get-tuple-element.31), channel_id=1, replica_groups=mesh['layer'=4,'row'=4,'zh'=4,'zl'=4,'core'=2] {'zl'}, dimensions={0} | all-to-all | bytes 262144 | tf_op jit(solution)/shard_map/all_to_all | solution.py:243
  108.0 2.1 solve_lo.1
  110.1 8.3 %all-to-all-start.7 = ((f32[4,2,32,128]{3,2,1,0:T(8,128)}), f32[4,2,32,128]{3,2,1,0:T(8,128)S(1)}, u32[]{:S(2)}, u32[]{:S(2)}) async-start(f32[4,2,32,128]{3,2,1,0:T(8,128)} %get-tuple-element.32), calls=%async_computation.7 | async-start | bytes 262144 | tf_op jit(solution)/shard_map/all_to_all | solution.py:243
  118.4 2.5 maps_lo.1
  120.9 9.6 %all-to-all-done.7.bg_ref = f32[4,2,32,128]{3,2,1,0:T(8,128)S(1)} async-done(((f32[4,2,32,128]{3,2,1,0:T(8,128)}), f32[4,2,32,128]{3,2,1,0:T(8,128)S(1)}, u32[]{:S(2)}, u32[]{:S(2)}) %all-to-all-start.7) | async-done | bytes 131104 | tf_op jit(solution)/shard_map/all_to_all | solution.py:243
  130.5 3.5 %all-to-all-start.3 = ((f32[4,3,128,128]{3,2,1,0:T(8,128)}), f32[4,3,128,128]{3,2,1,0:T(8,128)S(1)}, u32[]{:S(2)}, u32[]{:S(2)}) async-start(f32[4,3,128,128]{3,2,1,0:T(8,128)} %get-tuple-element.29), calls=%async_computation.3 | async-start | bytes 1572864 | tf_op jit(solution)/shard_map/all_to_all | solution.py:243
  134.0 0.0 all-gather.4.cloned.1.call-start
  134.1 0.7 all-gather.4.cloned.1.call-update
  134.8 36.5 %all-to-all-done.3.maps_ref = f32[4,3,128,128]{3,2,1,0:T(8,128)S(1)} async-done(((f32[4,3,128,128]{3,2,1,0:T(8,128)}), f32[4,3,128,128]{3,2,1,0:T(8,128)S(1)}, u32[]{:S(2)}, u32[]{:S(2)}) %all-to-all-start.3) | async-done | bytes 786464 | tf_op jit(solution)/shard_map/all_to_all | solution.py:243
  171.3 2.1 solve_hi.1
  173.4 4.0 %all-to-all-start.8 = ((f32[4,2,32,128]{3,2,1,0:T(8,128)}), f32[4,2,32,128]{3,2,1,0:T(8,128)S(1)}, u32[]{:S(2)}, u32[]{:S(2)}) async-start(f32[4,2,32,128]{3,2,1,0:T(8,128)} %get-tuple-element.33), calls=%async_computation.8 | async-start | bytes 262144 | tf_op jit(solution)/shard_map/all_to_all | solution.py:243
  177.4 1.6 maps_hi.1
  179.0 3.2 %all-to-all-done.8.bg_ref = f32[4,2,32,128]{3,2,1,0:T(8,128)S(1)} async-done(((f32[4,2,32,128]{3,2,1,0:T(8,128)}), f32[4,2,32,128]{3,2,1,0:T(8,128)S(1)}, u32[]{:S(2)}, u32[]{:S(2)}) %all-to-all-start.8) | async-done | bytes 131104 | tf_op jit(solution)/shard_map/all_to_all | solution.py:243
  182.2 10.7 %all_to_all.61.maps_ref = f32[4,3,128,128]{3,2,1,0:T(8,128)S(1)} all-to-all(f32[4,3,128,128]{3,2,1,0:T(8,128)S(1)} %get-tuple-element.30), channel_id=1, replica_groups=mesh['layer'=4,'row'=4,'zh'=4,'zl'=4,'core'=2] {'row'}, dimensions={0} | all-to-all | bytes 1572864 | tf_op jit(solution)/shard_map/all_to_all | solution.py:243
  193.0 2.7 top_solve.1
  195.7 31.2 %all_to_all.62 = bf16[16,4,32,128]{3,2,1,0:T(8,128)(2,1)S(1)} all-to-all(bf16[16,4,32,128]{3,2,1,0:T(8,128)(2,1)S(1)} %get-tuple-element.40), channel_id=1, replica_groups=mesh['layer'=4,'row'=4,'zh'=4,'zl'=4,'core'=2] {'zh','zl'}, dimensions={0} | all-to-all | bytes 1048576 | tf_op jit(solution)/shard_map/all_to_all | solution.py:243
  226.9 12.3 %all-to-all-start.11 = ((f32[8,2,32,128]{3,2,1,0:T(8,128)}), f32[8,2,32,128]{3,2,1,0:T(8,128)S(1)}, u32[]{:S(2)}, u32[]{:S(2)}) async-start(f32[8,2,32,128]{3,2,1,0:T(8,128)} %get-tuple-element.41), calls=%async_computation.11 | async-start | bytes 524288 | tf_op jit(solution)/shard_map/all_to_all | solution.py:243
  239.2 15.2 %all-gather.1 = bf16[16,128,128]{2,1,0:T(8,128)(2,1)S(1)} all-gather(bf16[2,128,128]{2,1,0:T(8,128)(2,1)S(1)} %copy-done.12), channel_id=3, replica_groups=mesh['layer'=4,'row'=4,'zh'=4,'zl'=4,'core'=2] {'layer','core'}, dimensions={0}, use_global_device_ids=true | all-gather | bytes 589824 | tf_op jit(solution)/shard_map/all_gather | solution.py:288
  254.4 1.6 copy-done
  256.0 5.4 %leaf_backward.1 = bf16[8,2,32,128]{3,2,1,0:T(8,128)(2,1)} custom-call(s32[8,8]{1,0:T(8,128)S(1)} %bitcast.12, bf16[64,32,128]{2,1,0:T(8,128)(2,1)S(1)} %bitcast.8, bf16[8,336,128]{2,1,0:T(8,128)(2,1)S(1)} %all-to-all-done.got_ref, bf16[8,2,4,128,128]{4,3,2,1,0:T(8,128)(2,1)S(1)} %bitcast.10, bf16[8,2,128,128]{3,2,1,0:T(8,128)(2,1)S(1)} %bitcast.9), custom_call_target="tpu_custom_call" | custom-call | tf_op jit(solution)/shard_map/leaf_backward/pallas_call | solution.py:37
  261.4 0.0 all-to-all-done.11.got_ref
  261.4 3.4 %all-to-all-start.10 = ((bf16[8,2,32,128]{3,2,1,0:T(8,128)(2,1)}), bf16[8,2,32,128]{3,2,1,0:T(8,128)(2,1)S(1)}, u32[]{:S(2)}, u32[]{:S(2)}) async-start(bf16[8,2,32,128]{3,2,1,0:T(8,128)(2,1)} %leaf_backward.1), calls=%async_computation.10 | async-start | bytes 262144 | tf_op jit(solution)/shard_map/all_to_all | solution.py:243
  264.8 1.3 turn_sep.1
  266.1 4.0 %all-to-all-done.10.got_ref = bf16[8,2,32,128]{3,2,1,0:T(8,128)(2,1)S(1)} async-done(((bf16[8,2,32,128]{3,2,1,0:T(8,128)(2,1)}), bf16[8,2,32,128]{3,2,1,0:T(8,128)(2,1)S(1)}, u32[]{:S(2)}, u32[]{:S(2)}) %all-to-all-start.10) | async-done | bytes 131104 | tf_op jit(solution)/shard_map/all_to_all | solution.py:243
  270.1 1.1 turn_leaf.1
  (21 shorter events, 0.0 us)
Async XLA Ops:
  7.9 0.9 copy-start.4
  8.9 0.9 copy-start.6
  9.8 0.8 copy-start.11
  10.6 12.0 %copy-start.5 = (f32[2,128,256]{2,1,0:T(8,128)S(1)}, f32[2,128,256]{2,1,0:T(8,128)}, u32[]{:S(2)}) copy-start(f32[2,128,256]{2,1,0:T(8,128)} %rhs_ref.3) | copy-start | bytes 786436
  10.6 12.0 %copy-start.7 = (f32[2,128,128]{2,1,0:T(8,128)S(1)}, f32[2,128,128]{2,1,0:T(8,128)}, u32[]{:S(2)}) copy-start(f32[2,128,128]{2,1,0:T(8,128)} %li_ref.1) | copy-start | bytes 393220
  10.6 12.0 %copy-start.8 = (f32[2,128,128]{2,1,0:T(8,128)S(1)}, f32[2,128,128]{2,1,0:T(8,128)}, u32[]{:S(2)}) copy-start(f32[2,128,128]{2,1,0:T(8,128)} %ll_ref.1) | copy-start | bytes 393220
  10.6 12.0 %copy-start.9 = (f32[2,128,128]{2,1,0:T(8,128)S(1)}, f32[2,128,128]{2,1,0:T(8,128)}, u32[]{:S(2)}) copy-start(f32[2,128,128]{2,1,0:T(8,128)} %ui_ref.1) | copy-start | bytes 393220
  10.6 12.0 %copy-start.10 = (f32[2,128,128]{2,1,0:T(8,128)S(1)}, f32[2,128,128]{2,1,0:T(8,128)}, u32[]{:S(2)}) copy-start(f32[2,128,128]{2,1,0:T(8,128)} %ul_ref.1) | copy-start | bytes 393220
  12.2 21.6 %all-to-all-start = ((bf16[8,336,128]{2,1,0:T(8,128)(2,1)}), bf16[8,336,128]{2,1,0:T(8,128)(2,1)S(1)}, u32[]{:S(2)}, u32[]{:S(2)}) async-start(bf16[8,336,128]{2,1,0:T(8,128)(2,1)} %leaf_forward.1), calls=%async_computation | async-start | bytes 1376256 | tf_op jit(solution)/shard_map/all_to_all | solution.py:243
  33.8 6.2 %all-to-all-start.1 = ((f32[2,2,544,128]{3,2,1,0:T(8,128)}), f32[2,2,544,128]{3,2,1,0:T(8,128)S(1)}, u32[]{:S(2)}, u32[]{:S(2)}) async-start(f32[2,2,544,128]{3,2,1,0:T(8,128)} %sep_prepare.1), calls=%async_computation.1 | async-start | bytes 2228224 | tf_op jit(solution)/shard_map/all_to_all | solution.py:243
  40.1 33.3 %all-to-all-start.5 = ((bf16[16,4,32,128]{3,2,1,0:T(8,128)(2,1)}), bf16[16,4,32,128]{3,2,1,0:T(8,128)(2,1)S(1)}, u32[]{:S(2)}, u32[]{:S(2)}) async-start(bf16[16,4,32,128]{3,2,1,0:T(8,128)(2,1)} %scatter_updates.1), calls=%async_computation.5 | async-start | bytes 1048576 | tf_op jit(solution)/shard_map/all_to_all | solution.py:243
  52.0 0.9 copy-start.1
  52.9 0.8 copy-start.2
  73.4 27.5 %all-to-all-start.2 = ((f32[4,3,128,128]{3,2,1,0:T(8,128)}), f32[4,3,128,128]{3,2,1,0:T(8,128)S(1)}, u32[]{:S(2)}, u32[]{:S(2)}) async-start(f32[4,3,128,128]{3,2,1,0:T(8,128)} %copy-done.1), calls=%async_computation.2 | async-start | bytes 1572864 | tf_op jit(solution)/shard_map/all_to_all | solution.py:243
  110.1 20.4 %all-to-all-start.7 = ((f32[4,2,32,128]{3,2,1,0:T(8,128)}), f32[4,2,32,128]{3,2,1,0:T(8,128)S(1)}, u32[]{:S(2)}, u32[]{:S(2)}) async-start(f32[4,2,32,128]{3,2,1,0:T(8,128)} %get-tuple-element.32), calls=%async_computation.7 | async-start | bytes 262144 | tf_op jit(solution)/shard_map/all_to_all | solution.py:243
  130.5 40.8 %all-to-all-start.3 = ((f32[4,3,128,128]{3,2,1,0:T(8,128)}), f32[4,3,128,128]{3,2,1,0:T(8,128)S(1)}, u32[]{:S(2)}, u32[]{:S(2)}) async-start(f32[4,3,128,128]{3,2,1,0:T(8,128)} %get-tuple-element.29), calls=%async_computation.3 | async-start | bytes 1572864 | tf_op jit(solution)/shard_map/all_to_all | solution.py:243
  134.0 120.3 %all-gather.4.cloned.1.call-start = ((), (), s32[]{:S(2)}) async-start(), calls=%async_computation.12 | async-start | bytes 2359296 | tf_op jit(solution)/shard_map/all_gather | solution.py:287
  173.4 8.8 %all-to-all-start.8 = ((f32[4,2,32,128]{3,2,1,0:T(8,128)}), f32[4,2,32,128]{3,2,1,0:T(8,128)S(1)}, u32[]{:S(2)}, u32[]{:S(2)}) async-start(f32[4,2,32,128]{3,2,1,0:T(8,128)} %get-tuple-element.33), calls=%async_computation.8 | async-start | bytes 262144 | tf_op jit(solution)/shard_map/all_to_all | solution.py:243
  177.4 15.6 %copy-start.3 = (f32[256,512]{1,0:T(8,128)S(1)}, f32[256,512]{1,0:T(8,128)}, u32[]{:S(2)}) copy-start(f32[256,512]{1,0:T(8,128)} %copy-done.2) | copy-start | bytes 1572868
  195.7 43.5 %copy-start.12 = (bf16[2,128,128]{2,1,0:T(8,128)(2,1)S(1)}, bf16[2,128,128]{2,1,0:T(8,128)(2,1)}, u32[]{:S(2)}) copy-start(bf16[2,128,128]{2,1,0:T(8,128)(2,1)} %param.15) | copy-start | bytes 196612
  226.9 34.5 %all-to-all-start.11 = ((f32[8,2,32,128]{3,2,1,0:T(8,128)}), f32[8,2,32,128]{3,2,1,0:T(8,128)S(1)}, u32[]{:S(2)}, u32[]{:S(2)}) async-start(f32[8,2,32,128]{3,2,1,0:T(8,128)} %get-tuple-element.41), calls=%async_computation.11 | async-start | bytes 524288 | tf_op jit(solution)/shard_map/all_to_all | solution.py:243
  254.4 1.6 copy-start
  261.4 8.7 %all-to-all-start.10 = ((bf16[8,2,32,128]{3,2,1,0:T(8,128)(2,1)}), bf16[8,2,32,128]{3,2,1,0:T(8,128)(2,1)S(1)}, u32[]{:S(2)}, u32[]{:S(2)}) async-start(bf16[8,2,32,128]{3,2,1,0:T(8,128)(2,1)} %leaf_backward.1), calls=%async_computation.10 | async-start | bytes 262144 | tf_op jit(solution)/shard_map/all_to_all | solution.py:243
Sparse Core Ops, SparseCore 0:
  137.0 36.7 all-gather.3

commit v2 on v1

v2 whole, which is shorter than its diff:
```python
import jax
import jax.numpy as jnp
from jax import lax
from jax.experimental import pallas as pl
from jax.experimental.pallas import tpu as pltpu
from jax.sharding import Mesh
from jax.sharding import PartitionSpec as P

f32 = jnp.float32
bf16 = jnp.bfloat16

B = 128
VMEM_LIMIT = 16 * 1024 * 1024


def dot(a, b):
    return jnp.dot(a, b, preferred_element_type=f32)


def dot_nt(a, b):
    return lax.dot_general(a, b, (((1,), (1,)), ((), ())), preferred_element_type=f32)


def split(x):
    high = x.astype(bf16)
    return high, (x - high.astype(f32)).astype(bf16)


def mm(a, b):
    a_high, a_low = split(a)
    b_high, b_low = split(b)
    return dot(a_high, b_high) + (dot(a_low, b_high) + dot(a_high, b_low))


def call(kernel, outs, scratch=(), name=None, smem=(), hbm=(), after=(), limit=VMEM_LIMIT):
    def run(*operands):
        count = len(operands)

        def body(*refs):
            kernel(*refs[:count], *refs[count + len(after) :])

        def space(k):
            return pltpu.SMEM if k in smem else pltpu.HBM if k in hbm else pltpu.VMEM

        return pl.pallas_call(
            body,
            out_shape=outs,
            in_specs=[pl.BlockSpec(memory_space=space(k)) for k in range(count)]
            + [pl.BlockSpec(memory_space=pl.ANY)] * len(after),
            out_specs=jax.tree.map(lambda _: pl.BlockSpec(memory_space=pltpu.VMEM), outs),
            scratch_shapes=list(scratch),
            compiler_params=pltpu.CompilerParams(vmem_limit_bytes=limit),
            name=name,
        )(*operands, *after)

    return run


def landing(arrays):
    return [pltpu.VMEM(x.shape, x.dtype) for x in arrays] + [pltpu.SemaphoreType.DMA((len(arrays),))]


def start_copies(sources, targets, sems):
    copies = [
        pltpu.make_async_copy(source, target, sems.at[k])
        for k, (source, target) in enumerate(zip(sources, targets))
    ]
    for copy in copies:
        copy.start()
    return copies


def shaped(shape, dtype):
    return jax.ShapeDtypeStruct(shape, dtype)


def scatter_updates(place_ref, got_ref, out_ref, total):
    width = out_ref.shape[-2]
    total[...] = jnp.zeros_like(total)
    for j in range(got_ref.shape[0]):
        for slot in range(8):
            s = place_ref[j, slot]
            total[s] = total[s] + got_ref[j, slot * width : (slot + 1) * width].astype(f32)
    out_ref[...] = total[...].reshape(out_ref.shape).astype(bf16)


def begin(at_ref, tgt_ref, *refs):
    sources, (mine_ref, other_ref, sent_ref), rest = refs[:8], refs[8:11], refs[11:]
    landed, sems, turned = rest[:8], rest[8], rest[9]
    copies = start_copies(sources, landed, sems)
    li_ref, ll_ref, ui_ref, ul_ref, rhs_ref, leaf_ref, inv_ref, lower_ref = landed
    groups = sent_ref.shape[0]
    width = 256 // groups
    for copy in copies[:5]:
        copy.wait()
    for s in range(2):
        turned[s] = rhs_ref[s].T
        li, ui = li_ref[s], ui_ref[s]
        blocks = (-mm(li, ll_ref[s]).T, -mm(ui, ul_ref[s]).T, li.T, ui.T)
        for ref, core in ((mine_ref, at_ref[4]), (other_ref, 1 - at_ref[4])):
            for k in range(4):
                ref[s, k * B : (k + 1) * B] = blocks[k]
            first = pl.multiple_of((2 * at_ref[0] + core) * width, width)
            ref[s, 4 * B :] = turned[s, pl.ds(first, width)]
    for copy in copies[5:]:
        copy.wait()
    for k in range(2):
        forward = dot(inv_ref[k], leaf_ref[k]).T.astype(bf16)
        for j in range(groups):
            sent_ref[j, (8 + k) * width : (9 + k) * width] = forward[j * width : (j + 1) * width]
        for i in range(4):
            update = dot_nt(forward, lower_ref[k, i]).astype(bf16)
            slot = 4 * k + i
            for j in range(groups):
                sent_ref[j, slot * width : (slot + 1) * width] = update[j * width : (j + 1) * width]
    lane = lax.broadcasted_iota(jnp.int32, (16, B), 1)
    places = jnp.zeros((16, B), jnp.int32)
    for slot in range(8):
        places = jnp.where(lane == slot, tgt_ref[slot // 4, slot % 4], places)
    for j in range(groups):
        sent_ref[j, 10 * width :] = places.astype(f32).astype(bf16)


def chip_maps(at_ref, mine_ref, other_ref, sep_ref, half_ref, wy_ref, whole):
    sep_ref[at_ref[4]] = mine_ref[...]
    sep_ref[1 - at_ref[4]] = other_ref[...]

    def block(s, k):
        return sep_ref[s // 2, s % 2, k * B : (k + 1) * B]

    reach = [block(0, 0)]
    for s in range(1, 4):
        reach.append(mm(reach[-1], block(s, 0)))
    w = mm(reach[3], block(3, 3))
    y = block(3, 1)
    wy = jnp.concatenate([w, y], axis=0)
    wy_ref[:, 3 * B :] = wy
    for s in (2, 1, 0):
        wy = mm(wy, block(s, 1))
        wy = jnp.concatenate([wy[:B] + mm(reach[s], block(s, 3)), wy[B:]], axis=0)
        wy_ref[:, s * B : (s + 1) * B] = wy
    whole[0] = reach[3]
    whole[1] = wy[B:]
    whole[2] = wy[:B]
    half_ref[...] = whole[:, pl.ds(pl.multiple_of(at_ref[4] * (B // 2), B // 2), B // 2)]


def chip_solve(got_ref, sep_ref, bg_ref, local_ref):
    total = jnp.sum(got_ref[...].astype(f32), axis=0)

    def block(s, k):
        return sep_ref[s // 2, s % 2, k * B : (k + 1) * B]

    base = [
        mm(sep_ref[s // 2, s % 2, 4 * B :] - total[s], block(s, 2)) for s in range(4)
    ]
    f = base[0]
    forward = [f]
    for s in range(1, 4):
        f = mm(f, block(s, 0)) + base[s]
        forward.append(f)
    bent = [mm(forward[s], block(s, 3)) for s in range(4)]
    u = bent[3]
    local_ref[3] = u
    for s in (2, 1, 0):
        u = mm(u, block(s, 1)) + bent[s]
        local_ref[s] = u
    for n in range(bg_ref.shape[0]):
        bg_ref[n, 0] = f.astype(bf16)
        bg_ref[n, 1] = u.astype(bf16)


def compose(maps):
    count = len(maps)
    reach = [None, maps[0][0]]
    for q in range(1, count):
        reach.append(mm(reach[-1], maps[q][0]))
    turned = [maps[0][2]] + [mm(reach[q], maps[q][2]) for q in range(1, count)]
    zy = jnp.concatenate([turned[-1], maps[-1][1]], axis=0)
    entries = [None] * count
    for q in reversed(range(count - 1)):
        entries[q] = zy
        zy = mm(zy, maps[q][1])
        zy = jnp.concatenate([zy[:B] + turned[q], zy[B:]], axis=0)
    return (reach[count], zy[B:], zy[:B]), reach[:count], entries


def keep_entries(keep, first, reach, entries):
    identity = (
        lax.broadcasted_iota(jnp.int32, (B, B), 0) == lax.broadcasted_iota(jnp.int32, (B, B), 1)
    ).astype(f32)
    for q in range(len(reach)):
        keep[first + q, 0] = identity if reach[q] is None else reach[q]
        keep[first + q, 1] = identity if entries[q] is None else entries[q][B:]
        keep[first + q, 2] = jnp.zeros((B, B), f32) if entries[q] is None else entries[q][:B]


def both(maps_ref, place, m):
    return jnp.concatenate([maps_ref[2 * place, m], maps_ref[2 * place + 1, m]], axis=0)


def col_maps(at_ref, maps_ref, quad_ref, pqr_ref, xyz_ref, keep):
    quads = []
    for h in range(4):
        maps = [[both(maps_ref, 4 * h + q, m) for m in range(3)] for q in range(4)]
        quad, reach, entries = compose(maps)
        keep_entries(keep, 4 * h, reach, entries)
        for m in range(3):
            quad_ref[h, m] = quad[m]
        quads.append(quad)
    whole, reach, entries = compose(quads)
    keep_entries(keep, 16, reach, entries)
    for m in range(3):
        pqr_ref[m] = whole[m]
    high, low = 16 + at_ref[2], 4 * at_ref[2] + at_ref[1]
    for m in range(3):
        xyz_ref[0, m] = keep[low, m]
    xyz_ref[1, 0] = mm(keep[high, 0], keep[low, 0])
    xyz_ref[1, 1] = mm(keep[high, 1], keep[low, 1])
    xyz_ref[1, 2] = mm(keep[high, 2], keep[low, 1]) + mm(keep[high, 0], keep[low, 2])


def chain(maps, bgs, keep, first):
    count = len(maps)
    f = bgs[0][0]
    entering = [None, f]
    for q in range(1, count):
        f = mm(f, maps[q][0]) + bgs[q][0]
        entering.append(f)
    turned = [bgs[0][1]] + [mm(entering[q], maps[q][2]) + bgs[q][1] for q in range(1, count)]
    keep[first, 0] = jnp.zeros_like(f)
    keep[first + count - 1, 1] = jnp.zeros_like(f)
    for q in range(1, count):
        keep[first + q, 0] = entering[q]
    u = turned[-1]
    for q in reversed(range(count - 1)):
        keep[first + q, 1] = u
        u = mm(u, maps[q][1]) + turned[q]
    return f, u


def col_solve(at_ref, maps_ref, quad_ref, bg_ref, xyz_ref, pqr_ref, out_ref, own_ref, keep):
    width = bg_ref.shape[2]
    quads = []
    for h in range(4):
        places = range(4 * h, 4 * h + 4)
        maps = [[both(maps_ref, p, m) for m in range(3)] for p in places]
        bgs = [[bg_ref[p, m].astype(f32) for m in range(2)] for p in places]
        quads.append(chain(maps, bgs, keep, 4 * h))
    maps = [[quad_ref[h, m] for m in range(3)] for h in range(4)]
    f, u = chain(maps, quads, keep, 16)
    for n in range(out_ref.shape[0]):
        for m in range(3):
            out_ref[n, m * B : (m + 1) * B] = pqr_ref[m]
        out_ref[n, 3 * B : 3 * B + width] = f
        out_ref[n, 3 * B + width :] = u
    high, low = 16 + at_ref[2], 4 * at_ref[2] + at_ref[1]
    f, u = keep[high, 0], keep[high, 1]
    own_ref[0] = mm(f, xyz_ref[0, 0]) + keep[low, 0]
    own_ref[1] = mm(u, xyz_ref[0, 1]) + mm(f, xyz_ref[0, 2]) + keep[low, 1]


def top_solve(at_ref, got_ref, xyz_ref, own_ref, wy_ref, local_ref, sep_ref, low_ref, keep):
    width = own_ref.shape[1]
    count = got_ref.shape[0]
    maps = [[got_ref[q, m * B : (m + 1) * B] for m in range(3)] for q in range(count)]
    bgs = [
        [got_ref[q, 3 * B + m * width : 3 * B + (m + 1) * width] for m in range(2)] for q in range(count)
    ]
    chain(maps, bgs, keep, 0)
    f, u = keep[at_ref[3], 0], keep[at_ref[3], 1]
    f, u = (
        mm(f, xyz_ref[1, 0]) + own_ref[0],
        mm(u, xyz_ref[1, 1]) + mm(f, xyz_ref[1, 2]) + own_ref[1],
    )
    reached = mm(jnp.concatenate([f, u], axis=1), wy_ref[...])
    for s in range(4):
        value = local_ref[s] + reached[:, s * B : (s + 1) * B]
        high, rest = split(value)
        sep_ref[s // 2, s % 2, 0] = high
        sep_ref[s // 2, s % 2, 1] = rest
        for n in range(low_ref.shape[0]):
            low_ref[n, s] = high


def leaf_backward(place_ref, solved_ref, got_ref, upper_ref, sep_ref, out_ref):
    width = out_ref.shape[2]
    for j in range(out_ref.shape[0]):
        for k in range(2):
            total = jnp.zeros((width, B), f32)
            for i in range(4):
                total = total + dot_nt(solved_ref[place_ref[j, 4 * k + i]], upper_ref[j, k, i])
            forward = got_ref[j, (8 + k) * width : (9 + k) * width].astype(f32)
            out_ref[j, k] = dot_nt((forward - total).astype(bf16), upper_ref[j, k, 4]).astype(bf16)
            out_ref[j, 2 + 2 * k] = sep_ref[j % 2, k, 0]
            out_ref[j, 3 + 2 * k] = sep_ref[j % 2, k, 1]


def turn_back(got_ref, leaf_ref, sep_ref):
    width = got_ref.shape[2]
    for j in range(got_ref.shape[0]):
        lanes = pl.ds(j * width, width)
        for k in range(2):
            leaf_ref[k, :, lanes] = got_ref[j, k].astype(f32).T.astype(bf16)
            value = got_ref[j, 2 + 2 * k].astype(f32) + got_ref[j, 3 + 2 * k].astype(f32)
            sep_ref[k, :, lanes] = value.T


def exchange(value, axes):
    return lax.all_to_all(value, axes, split_axis=0, concat_axis=0, tiled=True)


def on_device(
    leaf_rhs,
    leaf_lower_inv,
    leaf_upper_inv,
    leaf_lower,
    leaf_upper,
    targets,
    sep_rhs,
    sep_lower_inv,
    sep_upper_inv,
    sep_lower_link,
    sep_upper_link,
):
    across = ("layer", "core")
    layers, rows = lax.axis_size("layer"), lax.axis_size("row")
    highs, lows = lax.axis_size("zh"), lax.axis_size("zl")
    groups = 2 * layers
    width = 256 // groups
    chips = highs * lows
    at = jnp.stack(
        [lax.axis_index(name) for name in ("layer", "zl", "zh", "row", "core")]
    ).astype(jnp.int32)

    along = ("zh", "zl")
    pair = (2, width, B)

    sources = (
        sep_lower_inv,
        sep_lower_link,
        sep_upper_inv,
        sep_upper_link,
        sep_rhs,
        leaf_rhs,
        leaf_lower_inv,
        leaf_lower,
    )
    blocks = shaped((2, 4 * B + width, B), f32)
    mine, others, sent = call(
        begin,
        (blocks, blocks, shaped((groups, 10 * width + 16, B), bf16)),
        landing(sources) + [pltpu.VMEM((2, 256, B), f32)],
        "begin",
        smem=(0, 1),
        hbm=range(2, 10),
        limit=60 * 1024 * 1024,
    )(at, targets, *sources)
    theirs = lax.ppermute(others, "core", [(0, 1), (1, 0)])
    got = exchange(sent, across)
    place = got[:, 10 * width, :8].astype(jnp.int32)
    seps, half, wy = call(
        chip_maps,
        (shaped((2, 2, 4 * B + width, B), f32), shaped((3, B // 2, B), f32), shaped((2 * B, 4 * B), f32)),
        [pltpu.VMEM((3, B, B), f32)],
        "chip_maps",
        smem=(0,),
    )(at, mine, theirs)
    maps = lax.all_gather(half, along + ("core",))
    upper = lax.all_gather(jnp.concatenate([leaf_upper, leaf_upper_inv[:, None]], axis=1), across)

    sums = call(
        scatter_updates,
        shaped((chips, 4, width, B), bf16),
        [pltpu.VMEM((4 * chips, width, B), f32)],
        "scatter_updates",
        (0,),
        after=(half,),
    )(place, got)
    bg, local = call(
        chip_solve,
        (shaped((chips,) + pair, bf16), shaped((4, width, B), f32)),
        name="chip_solve",
    )(exchange(sums, along), seps)
    quads, pqr, xyz = call(
        col_maps,
        (shaped((4, 3, B, B), f32), shaped((3, B, B), f32), shaped((2, 3, B, B), f32)),
        [pltpu.VMEM((20, 3, B, B), f32)],
        "col_maps",
        (0,),
    )(at, maps)
    sent_on, own = call(
        col_solve,
        (shaped((rows, 3 * B + 2 * width, B), f32), shaped(pair, f32)),
        [pltpu.VMEM((20,) + pair, f32)],
        "col_solve",
        (0,),
    )(at, maps, quads, exchange(bg, along), xyz, pqr)
    solved, solved_low = call(
        top_solve,
        (shaped((2, 2, 2, width, B), bf16), shaped((chips, 4, width, B), bf16)),
        [pltpu.VMEM((rows,) + pair, f32)],
        "top_solve",
        (0,),
    )(at, exchange(sent_on, "row"), xyz, own, wy, local)

    low = exchange(solved_low, along).reshape(4 * chips, width, B)
    back = call(
        leaf_backward, shaped((groups, 6, width, B), bf16), name="leaf_backward", smem=(0,)
    )(place, low, got, upper, solved)
    return call(turn_back, (shaped((2, B, 256), bf16), shaped((2, B, 256), f32)), name="turn_back")(
        exchange(back, across)
    )


def solution(mesh):
    layers, rows, cols = (mesh.shape[name] for name in ("layer", "row", "col"))
    lows = 4
    fine = Mesh(
        mesh.devices.reshape(layers, rows, cols // (2 * lows), lows, 2),
        ("layer", "row", "zh", "zl", "core"),
    )
    leaf = ("layer", "row", "zh", "zl", "core")
    sep = ("row", "zh", "zl", "core")
    return jax.shard_map(
        on_device,
        mesh=fine,
        in_specs=(P(leaf),) * 6 + (P(sep),) * 5,
        out_specs=(P(leaf), P(sep)),
        check_vma=False,
    )
```

time: 279 us -> 219 us (0.78)
  waiting for transfers between devices: 101 us -> 68.2 us
  starting transfers between devices: 65.1 us -> 42.1 us
  blocking collectives: 64.2 us -> 51.5 us
  local copies, waits for them, and re-layouts: 6.09 us -> 11.9 us
    all_to_all x9 -> x3, waiting for transfers between devices: 100 us -> 48.6 us  [exchange(): return lax.all_to_all(value, axes, split_axis=0, concat_axis=0, tiled=True)]
    all_to_all x9 -> x3, starting transfers between devices: 65 us -> 33.2 us  [exchange(): return lax.all_to_all(value, axes, split_axis=0, concat_axis=0, tiled=True)]
    all_gather x1 -> x2, waiting for transfers between devices: 0.01 us -> 17.9 us  [the longest x1 17.8 us: on_device(): maps = lax.all_gather(half, along + ('core',))]
    all_gather x1 -> x0, blocking collectives: 15.2 us -> none  [on_device(): upper_inv = lax.all_gather(leaf_upper_inv, across)]
    ppermute x0 -> x1, starting transfers between devices: none -> 8.78 us  [on_device(): theirs = lax.ppermute(others, 'core', [(0, 1), (1, 0)])]
    unnamed x26 -> x36, local copies, waits for them, and re-layouts: 5.99 us -> 11.2 us
    pallas_call x13 -> x9, Pallas kernels: 26.6 us -> 29.1 us  [run(): pl.pallas_call(body, out_shape=outs, in_specs=[pl.BlockSpec(memory_space=...]
  transfers between devices with their start and end apart: 10 -> 6, of which waited for: 8 -> 4; matrix products, arithmetic and copies ran while one was open for 0% -> 0% of each run, Pallas kernels for 8% -> 7%
where the time goes in v2:
time: 219 us; the launch traced here: 218 us
  waiting for transfers between devices  68.2 us (31%)
  blocking collectives  51.5 us (24%)
  starting transfers between devices  42.1 us (19%)
  Pallas kernels  29.1 us (13%)
  between operations  14.1 us (6%)
  local copies, waits for them, and re-layouts  11.9 us (5%)
    all_to_all x3, blocking collectives, exchange(): return lax.all_to_all(value, axes, split_axis=0, concat_axis=0, tiled=True)  51.5 us
    all_to_all x3, waiting for transfers between devices, exchange(): return lax.all_to_all(value, axes, split_axis=0, concat_axis=0, tiled=True)  48.6 us
    all_to_all x3, starting transfers between devices, exchange(): return lax.all_to_all(value, axes, split_axis=0, concat_axis=0, tiled=True)  33.2 us
    pallas_call x9, Pallas kernels, run(): pl.pallas_call(body, out_shape=outs, in_specs=[pl.BlockSpec(memory_space=...  29.1 us
    all_gather x1, waiting for transfers between devices, on_device(): maps = lax.all_gather(half, along + ('core',))  17.8 us
    unnamed x36, local copies, waits for them, and re-layouts  11.2 us
    ppermute x1, starting transfers between devices, on_device(): theirs = lax.ppermute(others, 'core', [(0, 1), (1, 0)])  8.78 us
  transfers between devices with their start and end apart: 6, of which 4 were waited for; matrix products, arithmetic and copies ran while one was open for 0% of the time, Pallas kernels for 7%

profile of v2, /device:TPU:1, one launch (start us, length us, event | category | flops | bytes accessed | tf_op | source)
XLA Modules:
  0.0 217.7 jit_solution(13484084326546042903)
XLA Ops:
  7.2 0.0 all-gather.5.cloned.1.call-start
  7.2 0.6 stack.23.refs_0_
  7.8 0.0 copy-start.16
  7.8 4.0 %begin.1 = (f32[2,544,128]{2,1,0:T(8,128)}, f32[2,544,128]{2,1,0:T(8,128)}, bf16[8,336,128]{2,1,0:T(8,128)(2,1)}) custom-call(s32[5]{0:T(128)} %stack.23.refs_0_, s32[2,4]{1,0:T(2,128)} %refs_1_.1, f32[2,128,128]{2,1,0:T(8,128)} %refs_2_.1, f32[2,128,128]{2,1,0:T(8,128)} %refs_3_.1, f32[2,128,128]{2,1,0:T(8,128)} %refs_4_.1, f32[2,128,128]{2,1,0:T(8,128)} %refs_5_.1, ...), custom_call_target="tpu_custom_call" | custom-call | tf_op jit(solution)/shard_map/begin/pallas_call | solution.py:45
  11.9 8.8 %collective-permute-start = (f32[2,544,128]{2,1,0:T(8,128)}, f32[2,544,128]{2,1,0:T(8,128)S(1)}, u32[]{:S(2)}, u32[]{:S(2)}) collective-permute-start(f32[2,544,128]{2,1,0:T(8,128)} %get-tuple-element.19), channel_id=1, source_target_pairs={{0,1},{1,0},{2,3},{3,2},{4,5},{5,4},{6,7},{7,6},{8,9},{9,8},{10,11... | collective-permute-start | bytes 1671176 | tf_op jit(solution)/shard_map/ppermute | solution.py:359
  20.7 1.8 collective-permute-done.refs_2_
  22.5 1.1 copy-done.7
  23.5 0.6 copy-done.14
  24.2 2.6 %chip_maps.1 = (f32[2,2,544,128]{3,2,1,0:T(8,128)S(1)}, f32[3,64,128]{2,1,0:T(8,128)}, f32[256,512]{1,0:T(8,128)S(1)}) custom-call(s32[5]{0:T(128)S(1)} %copy-done.14, f32[2,544,128]{2,1,0:T(8,128)S(1)} %copy-done.7, f32[2,544,128]{2,1,0:T(8,128)S(1)} %collective-permute-done.refs_2_), custom_call_target="tpu_custom_call" | custom-call | tf_op jit(solution)/shard_map/chip_maps/pallas_call | solution.py:45
  26.8 0.8 copy-done.8
  27.6 0.0 all-gather.5.cloned.1.call-update
  27.6 15.1 %all_to_all.30.refs_1_.refs_2_ = bf16[8,336,128]{2,1,0:T(8,128)(2,1)S(1)} all-to-all(bf16[8,336,128]{2,1,0:T(8,128)(2,1)} %get-tuple-element.17), channel_id=1, replica_groups=mesh['layer'=4,'row'=4,'zh'=4,'zl'=4,'core'=2] {'layer','core'}, dimensions={0} | all-to-all | bytes 1376256 | tf_op jit(solution)/shard_map/all_to_all | solution.py:310
  42.7 1.7 scatter_updates.1
  44.4 0.8 copy-done.2
  45.3 10.6 %all-to-all-start.1 = ((bf16[16,4,32,128]{3,2,1,0:T(8,128)(2,1)}), bf16[16,4,32,128]{3,2,1,0:T(8,128)(2,1)S(1)}, u32[]{:S(2)}, u32[]{:S(2)}) async-start(bf16[16,4,32,128]{3,2,1,0:T(8,128)(2,1)} %scatter_updates.1), calls=%async_computation.1 | async-start | bytes 1048576 | tf_op jit(solution)/shard_map/all_to_all | solution.py:310
  55.8 0.0 all-gather.7.cloned.1.call-start
  55.9 0.0 copy-done.16
  55.9 0.0 copy-done.17
  55.9 0.8 pad_maximum_fusion
  56.7 0.0 all-gather.7.cloned.1.call-update
  56.7 25.8 %all-to-all-done.1.refs_0_ = bf16[16,4,32,128]{3,2,1,0:T(8,128)(2,1)S(1)} async-done(((bf16[16,4,32,128]{3,2,1,0:T(8,128)(2,1)}), bf16[16,4,32,128]{3,2,1,0:T(8,128)(2,1)S(1)}, u32[]{:S(2)}, u32[]{:S(2)}) %all-to-all-start.1) | async-done | bytes 524320 | tf_op jit(solution)/shard_map/all_to_all | solution.py:310
  82.5 2.0 chip_solve.1
  84.4 0.6 copy-done.12
  85.1 13.5 %all-to-all-start.2 = ((bf16[16,2,32,128]{3,2,1,0:T(8,128)(2,1)}), bf16[16,2,32,128]{3,2,1,0:T(8,128)(2,1)}, u32[]{:S(2)}, u32[]{:S(2)}) async-start(bf16[16,2,32,128]{3,2,1,0:T(8,128)(2,1)} %get-tuple-element.23), calls=%async_computation.2 | async-start | bytes 524288 | tf_op jit(solution)/shard_map/all_to_all | solution.py:310
  98.5 17.8 %all-gather.5.cloned.1.call-done = f32[96,64,128]{2,1,0:T(8,128)} async-done(((f32[3,64,128]{2,1,0:T(8,128)}), f32[96,64,128]{2,1,0:T(8,128)}) %all-gather.5.cloned.1.call-update) | async-done | bytes 3145744 | tf_op jit(solution)/shard_map/all_gather | solution.py:369
  116.4 0.0 copy-done.15
  116.4 1.9 copy-done
  118.3 4.8 %col_maps.1 = (f32[4,3,128,128]{3,2,1,0:T(8,128)S(1)}, f32[3,128,128]{2,1,0:T(8,128)S(1)}, f32[2,3,128,128]{3,2,1,0:T(8,128)S(1)}) custom-call(s32[5]{0:T(128)S(1)} %copy-done.15, f32[32,3,64,128]{3,2,1,0:T(8,128)S(1)} %bitcast.10), custom_call_target="tpu_custom_call" | custom-call | tf_op jit(solution)/shard_map/col_maps/pallas_call | solution.py:45
  123.1 0.0 copy-start.5
  123.1 0.9 copy-done.5
  123.9 0.7 copy-done.10
  124.6 0.0 all-to-all-done.2.refs_3_
  124.6 0.0 copy-done.1
  124.6 1.1 copy-done.6
  125.8 0.9 copy-done.11
  126.7 5.0 %col_solve.1 = (f32[4,448,128]{2,1,0:T(8,128)S(1)}, f32[2,32,128]{2,1,0:T(8,128)S(1)}) custom-call(s32[5]{0:T(128)S(1)} %copy-done.15, f32[32,3,64,128]{3,2,1,0:T(8,128)S(1)} %bitcast.11, f32[4,3,128,128]{3,2,1,0:T(8,128)S(1)} %copy-done.6, bf16[16,2,32,128]{3,2,1,0:T(8,128)(2,1)} %all-to-all-done.2.refs_3_, ...), custom_call_target="tpu_custom_call" | custom-call | tf_op jit(solution)/shard_map/col_solve/pallas_call | solution.py:45
  131.7 17.2 %all_to_all.31.refs_1_ = f32[4,448,128]{2,1,0:T(8,128)S(1)} all-to-all(f32[4,448,128]{2,1,0:T(8,128)S(1)} %get-tuple-element.26), channel_id=1, replica_groups=mesh['layer'=4,'row'=4,'zh'=4,'zl'=4,'core'=2] {'row'}, dimensions={0} | all-to-all | bytes 1835008 | tf_op jit(solution)/shard_map/all_to_all | solution.py:310
  148.8 0.0 copy-done.9
  148.8 0.0 copy-done.13
  148.8 2.6 %top_solve.1 = (bf16[2,2,2,32,128]{4,3,2,1,0:T(8,128)(2,1)S(1)}, bf16[16,4,32,128]{3,2,1,0:T(8,128)(2,1)}) custom-call(s32[5]{0:T(128)S(1)} %copy-done.15, f32[4,448,128]{2,1,0:T(8,128)S(1)} %all_to_all.31.refs_1_, f32[2,3,128,128]{3,2,1,0:T(8,128)S(1)} %get-tuple-element.24.refs_4_.refs_2_, f32[2,32,128]{2,1,0:T(8,128)S(1)} %get-tuple-element.27.refs_3_, ...), custom_call_target="tpu_custom_call" | custom-call | tf_op jit(solution)/shard_map/top_solve/pallas_call | solution.py:45
  151.5 9.2 %all-to-all-start.4 = ((bf16[16,4,32,128]{3,2,1,0:T(8,128)(2,1)}), bf16[16,4,32,128]{3,2,1,0:T(8,128)(2,1)S(1)}, u32[]{:S(2)}, u32[]{:S(2)}) async-start(bf16[16,4,32,128]{3,2,1,0:T(8,128)(2,1)} %get-tuple-element.30), calls=%async_computation.4 | async-start | bytes 1048576 | tf_op jit(solution)/shard_map/all_to_all | solution.py:310
  160.6 0.0 all-gather.7.cloned.1.call-done
  160.7 22.8 %all-to-all-done.4 = bf16[16,4,32,128]{3,2,1,0:T(8,128)(2,1)S(1)} async-done(((bf16[16,4,32,128]{3,2,1,0:T(8,128)(2,1)}), bf16[16,4,32,128]{3,2,1,0:T(8,128)(2,1)S(1)}, u32[]{:S(2)}, u32[]{:S(2)}) %all-to-all-start.4) | async-done | bytes 524320 | tf_op jit(solution)/shard_map/all_to_all | solution.py:310
  183.5 0.0 copy-done.3
  183.5 1.7 copy-done.4
  185.2 4.7 %leaf_backward.1 = bf16[8,6,32,128]{3,2,1,0:T(8,128)(2,1)S(1)} custom-call(s32[8,8]{1,0:T(8,128)S(1)} %bitcast.15, bf16[64,32,128]{2,1,0:T(8,128)(2,1)S(1)} %bitcast.13, bf16[8,336,128]{2,1,0:T(8,128)(2,1)S(1)} %copy-done.3, bf16[8,2,5,128,128]{4,3,2,1,0:T(8,128)(2,1)S(1)} %bitcast.12, bf16[2,2,2,32,128]{4,3,2,1,0:T(8,128)(2,1)S(1)} %get-tuple-element.31.refs_4_), custom_call_target="tpu_custom_call" | custom-call | tf_op jit(solution)/shard_map/leaf_backward/pallas_call | solution.py:45
  190.0 19.3 %all_to_all.32.refs_0_ = bf16[8,6,32,128]{3,2,1,0:T(8,128)(2,1)S(1)} all-to-all(bf16[8,6,32,128]{3,2,1,0:T(8,128)(2,1)S(1)} %leaf_backward.1), channel_id=1, replica_groups=mesh['layer'=4,'row'=4,'zh'=4,'zl'=4,'core'=2] {'layer','core'}, dimensions={0} | all-to-all | bytes 786432 | tf_op jit(solution)/shard_map/all_to_all | solution.py:310
  209.3 1.7 turn_back.1
  (17 shorter events, 0.0 us)
Async XLA Ops:
  7.2 109.2 %all-gather.5.cloned.1.call-start = ((), (), s32[]{:S(2)}) async-start(), calls=%async_computation.6 | async-start | bytes 3244032 | tf_op jit(solution)/shard_map/all_gather | solution.py:369
  7.8 48.0 %copy-start.16 = (bf16[2,4,128,128]{3,2,1,0:T(8,128)(2,1)S(1)}, bf16[2,4,128,128]{3,2,1,0:T(8,128)(2,1)}, u32[]{:S(2)}) copy-start(bf16[2,4,128,128]{3,2,1,0:T(8,128)(2,1)} %param.15) | copy-start | bytes 786436
  7.8 48.1 %copy-start.17 = (bf16[2,128,128]{2,1,0:T(8,128)(2,1)S(1)}, bf16[2,128,128]{2,1,0:T(8,128)(2,1)}, u32[]{:S(2)}) copy-start(bf16[2,128,128]{2,1,0:T(8,128)(2,1)} %param.13) | copy-start | bytes 196612
  11.9 10.6 %collective-permute-start = (f32[2,544,128]{2,1,0:T(8,128)}, f32[2,544,128]{2,1,0:T(8,128)S(1)}, u32[]{:S(2)}, u32[]{:S(2)}) collective-permute-start(f32[2,544,128]{2,1,0:T(8,128)} %get-tuple-element.19), channel_id=1, source_target_pairs={{0,1},{1,0},{2,3},{3,2},{4,5},{5,4},{6,7},{7,6},{8,9},{9,8},{10,11... | collective-permute-start | bytes 1671176 | tf_op jit(solution)/shard_map/ppermute | solution.py:359
  22.5 1.1 copy-start.7
  23.5 0.6 copy-start.14
  26.8 0.8 copy-start.8
  42.7 73.7 %copy-start.15 = (s32[5]{0:T(128)S(1)}, s32[5]{0:T(128)}, u32[]{:S(2)}) copy-start(s32[5]{0:T(128)} %stack.23.refs_0_) | copy-start | bytes 64
  44.4 0.8 copy-start.2
  45.3 37.2 %all-to-all-start.1 = ((bf16[16,4,32,128]{3,2,1,0:T(8,128)(2,1)}), bf16[16,4,32,128]{3,2,1,0:T(8,128)(2,1)S(1)}, u32[]{:S(2)}, u32[]{:S(2)}) async-start(bf16[16,4,32,128]{3,2,1,0:T(8,128)(2,1)} %scatter_updates.1), calls=%async_computation.1 | async-start | bytes 1048576 | tf_op jit(solution)/shard_map/all_to_all | solution.py:310
  55.8 104.8 %all-gather.7.cloned.1.call-start = ((), (), s32[]{:S(2)}) async-start(), calls=%async_computation.7 | async-start | bytes 2949120 | tf_op jit(solution)/shard_map/all_gather | solution.py:370
  84.4 0.6 copy-start.12
  85.1 39.6 %all-to-all-start.2 = ((bf16[16,2,32,128]{3,2,1,0:T(8,128)(2,1)}), bf16[16,2,32,128]{3,2,1,0:T(8,128)(2,1)}, u32[]{:S(2)}, u32[]{:S(2)}) async-start(bf16[16,2,32,128]{3,2,1,0:T(8,128)(2,1)} %get-tuple-element.23), calls=%async_computation.2 | async-start | bytes 524288 | tf_op jit(solution)/shard_map/all_to_all | solution.py:310
  116.4 1.9 copy-start
  118.3 6.3 %copy-start.1 = (f32[96,64,128]{2,1,0:T(8,128)S(1)}, f32[96,64,128]{2,1,0:T(8,128)}, u32[]{:S(2)}) copy-start(f32[96,64,128]{2,1,0:T(8,128)} %all-gather.5.cloned.1.call-done) | copy-start | bytes 9437188
  123.1 0.9 copy-start.5
  123.9 0.7 copy-start.10
  124.6 1.1 copy-start.6
  125.8 0.9 copy-start.11
  126.7 22.1 %copy-start.9 = (f32[256,512]{1,0:T(8,128)S(1)}, f32[256,512]{1,0:T(8,128)}, u32[]{:S(2)}) copy-start(f32[256,512]{1,0:T(8,128)} %copy-done.8) | copy-start | bytes 1572868
  126.7 22.1 %copy-start.13 = (f32[4,32,128]{2,1,0:T(8,128)S(1)}, f32[4,32,128]{2,1,0:T(8,128)}, u32[]{:S(2)}) copy-start(f32[4,32,128]{2,1,0:T(8,128)} %copy-done.12) | copy-start | bytes 196612
  131.7 51.8 %copy-start.3 = (bf16[8,336,128]{2,1,0:T(8,128)(2,1)S(1)}, bf16[8,336,128]{2,1,0:T(8,128)(2,1)}, u32[]{:S(2)}) copy-start(bf16[8,336,128]{2,1,0:T(8,128)(2,1)} %copy-done.2) | copy-start | bytes 2064388
  151.5 32.0 %all-to-all-start.4 = ((bf16[16,4,32,128]{3,2,1,0:T(8,128)(2,1)}), bf16[16,4,32,128]{3,2,1,0:T(8,128)(2,1)S(1)}, u32[]{:S(2)}, u32[]{:S(2)}) async-start(bf16[16,4,32,128]{3,2,1,0:T(8,128)(2,1)} %get-tuple-element.30), calls=%async_computation.4 | async-start | bytes 1048576 | tf_op jit(solution)/shard_map/all_to_all | solution.py:310
  183.5 1.7 copy-start.4
Sparse Core Ops, SparseCore 0:
  27.7 88.6 all-gather.4
  118.5 32.7 all-gather.6

commit v3 on v2

v3 whole, which is shorter than its diff:
```python
import jax
import jax.numpy as jnp
from jax import lax
from jax.experimental import pallas as pl
from jax.experimental.pallas import tpu as pltpu
from jax.sharding import Mesh
from jax.sharding import PartitionSpec as P

f32 = jnp.float32
bf16 = jnp.bfloat16

B = 128
VMEM_LIMIT = 16 * 1024 * 1024
VMEM_ALL = 60 * 1024 * 1024


def dot(a, b):
    return jnp.dot(a, b, preferred_element_type=f32)


def dot_nt(a, b):
    return lax.dot_general(a, b, (((1,), (1,)), ((), ())), preferred_element_type=f32)


def split(x):
    high = x.astype(bf16)
    return high, (x - high.astype(f32)).astype(bf16)


def mm(a, b):
    a_high, a_low = split(a)
    b_high, b_low = split(b)
    if b.shape == (B, B):
        wide = jnp.concatenate([b_high, b_low], axis=1)
        parts = dot(jnp.concatenate([a_high, a_low], axis=1), jnp.concatenate([wide, wide], axis=0))
        return parts[:, :B] + parts[:, B:]
    return dot(a_high, b_high) + (dot(a_low, b_high) + dot(a_high, b_low))


def call(kernel, outs, scratch=(), name=None, smem=(), hbm=(), after=(), limit=VMEM_LIMIT):
    def run(*operands):
        count = len(operands)

        def body(*refs):
            kernel(*refs[:count], *refs[count + len(after) :])

        def space(k):
            return pltpu.SMEM if k in smem else pltpu.HBM if k in hbm else pltpu.VMEM

        return pl.pallas_call(
            body,
            out_shape=outs,
            in_specs=[pl.BlockSpec(memory_space=space(k)) for k in range(count)]
            + [pl.BlockSpec(memory_space=pl.ANY)] * len(after),
            out_specs=jax.tree.map(lambda _: pl.BlockSpec(memory_space=pltpu.VMEM), outs),
            scratch_shapes=list(scratch),
            compiler_params=pltpu.CompilerParams(vmem_limit_bytes=limit),
            name=name,
        )(*operands, *after)

    return run


def landing(arrays):
    return [pltpu.VMEM(x.shape, x.dtype) for x in arrays] + [pltpu.SemaphoreType.DMA((len(arrays),))]


def start_copies(sources, targets, sems):
    copies = [
        pltpu.make_async_copy(source, target, sems.at[k])
        for k, (source, target) in enumerate(zip(sources, targets))
    ]
    for copy in copies:
        copy.start()
    return copies


def shaped(shape, dtype):
    return jax.ShapeDtypeStruct(shape, dtype)


def scatter_updates(place_ref, got_ref, out_ref, forward_ref, total):
    width = out_ref.shape[-2]
    total[...] = jnp.zeros_like(total)
    for j in range(got_ref.shape[0]):
        for slot in range(8):
            s = place_ref[j, slot]
            total[s] = total[s] + got_ref[j, slot * width : (slot + 1) * width].astype(f32)
    out_ref[...] = total[...].reshape(out_ref.shape).astype(bf16)
    for k in range(2):
        forward_ref[:, k] = got_ref[:, (8 + k) * width : (9 + k) * width]


def leaf_forward(tgt_ref, *refs):
    sources, sent_ref, landed, sems = refs[:3], refs[3], refs[4:7], refs[7]
    copies = start_copies(sources, landed, sems)
    rhs_ref, inv_ref, lower_ref = landed
    groups = sent_ref.shape[0]
    width = 256 // groups
    lane = lax.broadcasted_iota(jnp.int32, (16, B), 1)
    places = jnp.zeros((16, B), jnp.int32)
    for slot in range(8):
        places = jnp.where(lane == slot, tgt_ref[slot // 4, slot % 4], places)
    for j in range(groups):
        sent_ref[j, 10 * width :] = places.astype(f32).astype(bf16)
    copies[0].wait()
    copies[1].wait()
    forwards = []
    for k in range(2):
        forward = dot(inv_ref[k], rhs_ref[k]).T.astype(bf16)
        forwards.append(forward)
        for j in range(groups):
            sent_ref[j, (8 + k) * width : (9 + k) * width] = forward[j * width : (j + 1) * width]
    copies[2].wait()
    for k in range(2):
        for i in range(4):
            update = dot_nt(forwards[k], lower_ref[k, i]).astype(bf16)
            slot = 4 * k + i
            for j in range(groups):
                sent_ref[j, slot * width : (slot + 1) * width] = update[j * width : (j + 1) * width]


def sep_prepare(at_ref, *refs):
    sources, (mine_ref, other_ref), landed, sems, turned = refs[:5], refs[5:7], refs[7:12], refs[12], refs[13]
    copies = start_copies(sources, landed, sems)
    li_ref, ll_ref, ui_ref, ul_ref, rhs_ref = landed
    width = mine_ref.shape[1] - 4 * B
    for copy in copies:
        copy.wait()
    for s in range(2):
        turned[s] = rhs_ref[s].T
        li, ui = li_ref[s], ui_ref[s]
        blocks = (-mm(li, ll_ref[s]).T, -mm(ui, ul_ref[s]).T, li.T, ui.T)
        for ref, core in ((mine_ref, at_ref[4]), (other_ref, 1 - at_ref[4])):
            for k in range(4):
                ref[s, k * B : (k + 1) * B] = blocks[k]
            first = pl.multiple_of((2 * at_ref[0] + core) * width, width)
            ref[s, 4 * B :] = turned[s, pl.ds(first, width)]


def map_parts(maps):
    return split(maps[0]) + split(maps[1]) + (maps[2].astype(bf16),)


def send_half(at_ref, maps, half_ref, whole):
    for m, part in enumerate(map_parts(maps)):
        whole[m] = part
    half_ref[...] = whole[:, pl.ds(pl.multiple_of(at_ref[4] * (B // 2), B // 2), B // 2)]


def chip_maps(at_ref, mine_ref, other_ref, sep_ref, half_ref, wy_ref, whole):
    sep_ref[at_ref[4]] = mine_ref[...]
    sep_ref[1 - at_ref[4]] = other_ref[...]

    def block(s, k):
        return sep_ref[s // 2, s % 2, k * B : (k + 1) * B]

    reach = [block(0, 0)]
    for s in range(1, 4):
        reach.append(mm(reach[-1], block(s, 0)))
    w = mm(reach[3], block(3, 3))
    y = block(3, 1)
    wy = jnp.concatenate([w, y], axis=0)
    wy_ref[:, 3 * B :] = wy
    for s in (2, 1, 0):
        wy = mm(wy, block(s, 1))
        wy = jnp.concatenate([wy[:B] + mm(reach[s], block(s, 3)), wy[B:]], axis=0)
        wy_ref[:, s * B : (s + 1) * B] = wy
    send_half(at_ref, (reach[3], wy[B:], wy[:B]), half_ref, whole)


def chip_solve(got_ref, sep_ref, bg_ref, local_ref):
    total = jnp.sum(got_ref[...].astype(f32), axis=0)

    def block(s, k):
        return sep_ref[s // 2, s % 2, k * B : (k + 1) * B]

    base = [
        mm(sep_ref[s // 2, s % 2, 4 * B :] - total[s], block(s, 2)) for s in range(4)
    ]
    f = base[0]
    forward = [f]
    for s in range(1, 4):
        f = mm(f, block(s, 0)) + base[s]
        forward.append(f)
    bent = [mm(forward[s], block(s, 3)) for s in range(4)]
    u = bent[3]
    local_ref[3] = u
    for s in (2, 1, 0):
        u = mm(u, block(s, 1)) + bent[s]
        local_ref[s] = u
    for n in range(bg_ref.shape[0]):
        bg_ref[n, 0] = f.astype(bf16)
        bg_ref[n, 1] = u.astype(bf16)


def mm_parts(a, high, low):
    a_high, a_low = split(a)
    wide = jnp.concatenate([high, low], axis=1)
    parts = dot(jnp.concatenate([a_high, a_low], axis=1), jnp.concatenate([wide, wide], axis=0))
    return parts[:, :B] + parts[:, B:]


def mm_two(a, b_high, b_low, c_high, c_low):
    a_high, a_low = split(a)
    high = jnp.concatenate([b_high, c_high], axis=1)
    both = dot(jnp.concatenate([a_high, a_low], axis=1), jnp.concatenate([high, high], axis=0))
    if c_low is None:
        return both[:, :B] + dot(a_high, b_low), both[:, B:]
    both = both + dot(a_high, jnp.concatenate([b_low, c_low], axis=1))
    return both[:, :B], both[:, B:]


def compose(maps, sides):
    count = len(maps)
    whole = [sum(part.astype(f32) for part in m if part is not None) for m in maps[0]]
    none = jnp.zeros((B, B), f32)
    rows = jnp.concatenate([whole[0], sides[0][0]], axis=0)
    bent = [jnp.concatenate([whole[2], sides[0][1]], axis=0)]
    entering = [None, rows]
    for q in range(1, count):
        rows, turned = mm_two(rows, *maps[q][0], *maps[q][2])
        rows = rows + jnp.concatenate([none, sides[q][0]], axis=0)
        bent.append(turned + jnp.concatenate([none, sides[q][1]], axis=0))
        entering.append(rows)
    last = sum(part.astype(f32) for part in maps[-1][1])
    back = jnp.concatenate([bent[-1], last], axis=0)
    leaving = [None] * count
    for q in reversed(range(count - 1)):
        leaving[q] = back
        back = mm_parts(back, *maps[q][1])
        size = bent[q].shape[0]
        back = jnp.concatenate([back[:size] + bent[q], back[size:]], axis=0)
    size = bent[0].shape[0]
    whole = (rows[:B], back[size:], back[:B])
    return whole, (rows[B:], back[B:size]), entering[:count], leaving


def keep_entries(keep_maps, keep, first, entering, leaving, width):
    identity = (
        lax.broadcasted_iota(jnp.int32, (B, B), 0) == lax.broadcasted_iota(jnp.int32, (B, B), 1)
    ).astype(f32)
    none, nothing = jnp.zeros((B, B), f32), jnp.zeros((width, B), f32)
    for q in range(len(entering)):
        f, u = entering[q], leaving[q]
        keep_maps[first + q, 0] = identity if f is None else f[:B]
        keep[first + q, 0] = nothing if f is None else f[B:]
        keep_maps[first + q, 1] = identity if u is None else u[B + width :]
        keep_maps[first + q, 2] = none if u is None else u[:B]
        keep[first + q, 1] = nothing if u is None else u[B : B + width]


def row_solve(at_ref, maps_hbm, bg_ref, out_ref, xyz_ref, own_ref, maps_ref, sems, keep_maps, keep):
    width = bg_ref.shape[2]
    quads = [pl.ds(8 * h, 8) for h in range(4)]
    copies = start_copies([maps_hbm.at[q] for q in quads], [maps_ref.at[q] for q in quads], sems)
    quad_maps, quad_sides = [], []
    for h in range(4):
        copies[h].wait()
        maps, sides = [], []
        for p in range(4 * h, 4 * h + 4):
            part = [
                jnp.concatenate([maps_ref[2 * p, m], maps_ref[2 * p + 1, m]], axis=0) for m in range(5)
            ]
            maps.append((part[:2], part[2:4], (part[4], None)))
            sides.append([bg_ref[p, m].astype(f32) for m in range(2)])
        quad, side, entering, leaving = compose(maps, sides)
        keep_entries(keep_maps, keep, 4 * h, entering, leaving, width)
        quad_maps.append([split(m) for m in quad])
        quad_sides.append(side)
    row, side, entering, leaving = compose(quad_maps, quad_sides)
    keep_entries(keep_maps, keep, 16, entering, leaving, width)
    sent = map_parts(row)
    sides = split(side[0]) + split(side[1])
    for n in range(out_ref.shape[0]):
        for m in range(5):
            out_ref[n, m * B : (m + 1) * B] = sent[m]
        for m in range(4):
            out_ref[n, 5 * B + m * width : 5 * B + (m + 1) * width] = sides[m]
    high, low = 16 + at_ref[2], 4 * at_ref[2] + at_ref[1]
    x, y, z = (keep_maps[low, m] for m in range(3))
    f = mm(jnp.concatenate([keep_maps[high, 0], keep[high, 0]], axis=0), x)
    u = mm(jnp.concatenate([keep_maps[high, 2], keep_maps[high, 1], keep[high, 1]], axis=0), y)
    z = mm(jnp.concatenate([keep_maps[high, 0], keep[high, 0]], axis=0), z)
    xyz_ref[0] = f[:B]
    xyz_ref[1] = u[B : 2 * B]
    xyz_ref[2] = u[:B] + z[:B]
    own_ref[0] = f[B:] + keep[low, 0]
    own_ref[1] = u[2 * B :] + z[B:] + keep[low, 1]


def chain(maps, bgs, keep):
    count = len(maps)
    f = bgs[0][0]
    entering = [None, f]
    for q in range(1, count - 1):
        f = mm(f, maps[q][0]) + bgs[q][0]
        entering.append(f)
    turned = [None] + [mm(entering[q], maps[q][2]) + bgs[q][1] for q in range(1, count)]
    keep[0, 0] = jnp.zeros_like(f)
    keep[count - 1, 1] = jnp.zeros_like(f)
    for q in range(1, count):
        keep[q, 0] = entering[q]
    u = turned[-1]
    for q in reversed(range(count - 1)):
        keep[q, 1] = u
        if q > 0:
            u = mm(u, maps[q][1]) + turned[q]


def top_solve(at_ref, got_ref, xyz_ref, own_ref, wy_ref, local_ref, sep_ref, low_ref, keep):
    width = own_ref.shape[1]
    count = got_ref.shape[0]
    maps, bgs = [], []
    for q in range(count):
        part = [got_ref[q, m * B : (m + 1) * B].astype(f32) for m in range(5)]
        maps.append([part[0] + part[1], part[2] + part[3], part[4]])
        side = [
            got_ref[q, 5 * B + m * width : 5 * B + (m + 1) * width].astype(f32) for m in range(4)
        ]
        bgs.append([side[0] + side[1], side[2] + side[3]])
    chain(maps, bgs, keep)
    f, u = keep[at_ref[3], 0], keep[at_ref[3], 1]
    f, u = (
        mm(f, xyz_ref[0]) + own_ref[0],
        mm(u, xyz_ref[1]) + mm(f, xyz_ref[2]) + own_ref[1],
    )
    reached = mm(jnp.concatenate([f, u], axis=1), wy_ref[...])
    for s in range(4):
        value = local_ref[s] + reached[:, s * B : (s + 1) * B]
        sep_ref[s] = value
        low = value.astype(bf16)
        for n in range(low_ref.shape[0]):
            low_ref[n, s] = low


def join_upper(upper_ref, inv_ref, out_ref):
    for k in range(2):
        for i in range(4):
            out_ref[k, i * B : (i + 1) * B] = upper_ref[k, i].astype(f32).T.astype(bf16)
        out_ref[k, 4 * B :] = inv_ref[k].astype(f32).T.astype(bf16)


def leaf_backward(place_ref, solved_ref, forward_ref, upper_ref, out_ref):
    for j in range(out_ref.shape[0]):
        for k in range(2):
            solved = [solved_ref[place_ref[j, 4 * k + i]] for i in range(4)]
            total = dot(jnp.concatenate(solved, axis=1), upper_ref[j, k, : 4 * B])
            residual = (forward_ref[j, k].astype(f32) - total).astype(bf16)
            out_ref[j, k] = dot(residual, upper_ref[j, k, 4 * B :]).astype(bf16)


def turn_leaf(got_ref, out_ref):
    width = got_ref.shape[2]
    for k in range(2):
        whole = jnp.concatenate([got_ref[j, k] for j in range(got_ref.shape[0])], axis=0)
        out_ref[k] = whole.astype(f32).T.astype(bf16)


def turn_sep(at_ref, got_ref, out_ref):
    for k in range(2):
        s = 2 * at_ref[4] + k
        whole = jnp.concatenate([got_ref[j, s] for j in range(got_ref.shape[0])], axis=0)
        out_ref[k] = whole.T


def exchange(value, axes):
    return lax.all_to_all(value, axes, split_axis=0, concat_axis=0, tiled=True)


def on_device(
    leaf_rhs,
    leaf_lower_inv,
    leaf_upper_inv,
    leaf_lower,
    leaf_upper,
    targets,
    sep_rhs,
    sep_lower_inv,
    sep_upper_inv,
    sep_lower_link,
    sep_upper_link,
):
    across = ("layer", "core")
    layers, rows = lax.axis_size("layer"), lax.axis_size("row")
    highs, lows = lax.axis_size("zh"), lax.axis_size("zl")
    groups = 2 * layers
    width = 256 // groups
    chips = highs * lows
    at = jnp.stack(
        [lax.axis_index(name) for name in ("layer", "zl", "zh", "row", "core")]
    ).astype(jnp.int32)

    along = ("zh", "zl")
    pair = (2, width, B)

    sources = (sep_lower_inv, sep_lower_link, sep_upper_inv, sep_upper_link, sep_rhs)
    blocks = shaped((2, 4 * B + width, B), f32)
    half_maps = shaped((5, B // 2, B), bf16)
    maps = shaped((3, B, B), f32)
    mine, others = call(
        sep_prepare,
        (blocks, blocks),
        landing(sources) + [pltpu.VMEM((2, 256, B), f32)],
        "sep_prepare",
        smem=(0,),
        hbm=range(1, 6),
        limit=VMEM_ALL,
    )(at, *sources)
    theirs = lax.ppermute(others, "core", [(0, 1), (1, 0)])

    sources = (leaf_rhs, leaf_lower_inv, leaf_lower)
    sent = call(
        leaf_forward,
        shaped((groups, 10 * width + 16, B), bf16),
        landing(sources),
        "leaf_forward",
        smem=(0,),
        hbm=(1, 2, 3),
        limit=VMEM_ALL,
        after=(mine,),
    )(targets, *sources)
    seps, half, wy = call(
        chip_maps,
        (shaped((2, 2, 4 * B + width, B), f32), half_maps, shaped((2 * B, 4 * B), f32)),
        [pltpu.VMEM((5, B, B), bf16)],
        "chip_maps",
        smem=(0,),
        limit=VMEM_ALL,
        after=(sent,),
    )(at, mine, theirs)
    by_chip = lax.all_gather(half, along + ("core",)).reshape((2 * chips,) + half_maps.shape)

    got = exchange(sent, across)
    place = got[:, 10 * width, :8].astype(jnp.int32)
    sums, forward = call(
        scatter_updates,
        (shaped((chips, 4, width, B), bf16), shaped((groups, 2, width, B), bf16)),
        [pltpu.VMEM((4 * chips, width, B), f32)],
        "scatter_updates",
        smem=(0,),
        after=(half,),
    )(place, got)

    bg, local = call(
        chip_solve, (shaped((chips,) + pair, bf16), shaped((4, width, B), f32)), name="chip_solve"
    )(exchange(sums, along), seps)
    sent_on, xyz, own = call(
        row_solve,
        (shaped((rows, 5 * B + 4 * width, B), bf16), maps, shaped(pair, f32)),
        [
            pltpu.VMEM((2 * chips,) + half_maps.shape, bf16),
            pltpu.SemaphoreType.DMA((4,)),
            pltpu.VMEM((20, 3, B, B), f32),
            pltpu.VMEM((20,) + pair, f32),
        ],
        "row_solve",
        smem=(0,),
        hbm=(1,),
        limit=VMEM_ALL,
    )(at, by_chip, exchange(bg, along))
    solved, solved_low = call(
        top_solve,
        (shaped((4, width, B), f32), shaped((chips, 4, width, B), bf16)),
        [pltpu.VMEM((rows,) + pair, f32)],
        "top_solve",
        smem=(0,),
        limit=VMEM_ALL,
    )(at, exchange(sent_on, "row"), xyz, own, wy, local)

    joined = call(
        join_upper, shaped((2, 5 * B, B), bf16), name="join_upper", after=(sums,), limit=VMEM_ALL
    )(leaf_upper, leaf_upper_inv)
    upper = lax.all_gather(joined, across).reshape((groups, 2, 5 * B, B))
    low = exchange(solved_low, along).reshape(4 * chips, width, B)
    sep_all = lax.all_gather(solved, across).reshape((groups, 4, width, B))
    sep_part = call(turn_sep, shaped((2, B, 256), f32), name="turn_sep", smem=(0,))(at, sep_all)
    back = call(
        leaf_backward,
        shaped((groups, 2, width, B), bf16),
        name="leaf_backward",
        smem=(0,),
        after=(sep_part,),
    )(place, low, forward, upper)
    leaf_part = call(turn_leaf, shaped((2, B, 256), bf16), name="turn_leaf")(exchange(back, across))
    return (leaf_part, sep_part)


def solution(mesh):
    layers, rows, cols = (mesh.shape[name] for name in ("layer", "row", "col"))
    lows = 4
    fine = Mesh(
        mesh.devices.reshape(layers, rows, cols // (2 * lows), lows, 2),
        ("layer", "row", "zh", "zl", "core"),
    )
    leaf = ("layer", "row", "zh", "zl", "core")
    sep = ("row", "zh", "zl", "core")
    return jax.shard_map(
        on_device,
        mesh=fine,
        in_specs=(P(leaf),) * 6 + (P(sep),) * 5,
        out_specs=(P(leaf), P(sep)),
        check_vma=False,
    )
```

time: 219 us -> 202 us (0.922)
  blocking collectives: 51.5 us -> 89.8 us
  waiting for transfers between devices: 68.2 us -> 32.4 us
  starting transfers between devices: 42.1 us -> 29.6 us
  local copies, waits for them, and re-layouts: 11.9 us -> 5.65 us
    all_to_all x3 -> x4, blocking collectives: 51.5 us -> 73.6 us  [exchange(): return lax.all_to_all(value, axes, split_axis=0, concat_axis=0, tiled=True)]
    all_to_all x3 -> x2, waiting for transfers between devices: 48.6 us -> 29.6 us  [exchange(): return lax.all_to_all(value, axes, split_axis=0, concat_axis=0, tiled=True)]
    all_gather x0 -> x1, blocking collectives: none -> 16.2 us  [on_device(): sep_all = lax.all_gather(solved, across).reshape((groups, 4, width, B))]
    all_gather x2, waiting for transfers between devices: 17.9 us -> 2.8 us  [the longest x1 2.79 us: on_device(): lax.all_gather(half, along + ('core',))]
    all_to_all x3 -> x2, starting transfers between devices: 33.2 us -> 20.8 us  [exchange(): return lax.all_to_all(value, axes, split_axis=0, concat_axis=0, tiled=True)]
    unnamed x36 -> x14, local copies, waits for them, and re-layouts: 11.2 us -> 4.99 us
    pallas_call x9 -> x11, Pallas kernels: 29.1 us -> 29.7 us  [run(): pl.pallas_call(body, out_shape=outs, in_specs=[pl.BlockSpec(memory_space=...]
  transfers between devices with their start and end apart: 6 -> 5, of which waited for: 4 -> 3; matrix products, arithmetic and copies ran while one was open for 0% -> 0% of each run, Pallas kernels for 7% -> 10%
where the time goes in v3:
time: 202 us; the launch traced here: 201 us
  blocking collectives  89.8 us (44%)
  waiting for transfers between devices  32.4 us (16%)
  Pallas kernels  29.7 us (15%)
  starting transfers between devices  29.6 us (15%)
  between operations  14.1 us (7%)
  local copies, waits for them, and re-layouts  5.65 us (3%)
    all_to_all x4, blocking collectives, exchange(): return lax.all_to_all(value, axes, split_axis=0, concat_axis=0, tiled=True)  73.6 us
    pallas_call x11, Pallas kernels, run(): pl.pallas_call(body, out_shape=outs, in_specs=[pl.BlockSpec(memory_space=...  29.7 us
    all_to_all x2, waiting for transfers between devices, exchange(): return lax.all_to_all(value, axes, split_axis=0, concat_axis=0, tiled=True)  29.6 us
    all_to_all x2, starting transfers between devices, exchange(): return lax.all_to_all(value, axes, split_axis=0, concat_axis=0, tiled=True)  20.8 us
    all_gather x1, blocking collectives, on_device(): sep_all = lax.all_gather(solved, across).reshape((groups, 4, width, B))  16.2 us
    ppermute x1, starting transfers between devices, on_device(): theirs = lax.ppermute(others, 'core', [(0, 1), (1, 0)])  8.79 us
    unnamed x14, local copies, waits for them, and re-layouts  4.99 us
  transfers between devices with their start and end apart: 5, of which 3 were waited for; matrix products, arithmetic and copies ran while one was open for 0% of the time, Pallas kernels for 10%

profile of v3, /device:TPU:1, one launch (start us, length us, event | category | flops | bytes accessed | tf_op | source)
XLA Modules:
  0.0 201.4 jit_solution(871343070189887669)
XLA Ops:
  7.2 0.0 all-gather.6.cloned.1.call-start
  7.2 0.7 stack.23.refs_0_
  7.9 3.3 %sep_prepare.1 = (f32[2,544,128]{2,1,0:T(8,128)}, f32[2,544,128]{2,1,0:T(8,128)}) custom-call(s32[5]{0:T(128)} %stack.23.refs_0_, f32[2,128,128]{2,1,0:T(8,128)} %refs_1_.3, f32[2,128,128]{2,1,0:T(8,128)} %refs_2_.2, f32[2,128,128]{2,1,0:T(8,128)} %refs_3_.2, f32[2,128,128]{2,1,0:T(8,128)} %refs_4_.1, f32[2,128,256]{2,1,0:T(8,128)} %refs_5_.1), custom_call_target="tpu_custom_call" | custom-call | tf_op jit(solution)/shard_map/sep_prepare/pallas_call | solution.py:50
  11.2 8.8 %collective-permute-start = (f32[2,544,128]{2,1,0:T(8,128)}, f32[2,544,128]{2,1,0:T(8,128)S(1)}, u32[]{:S(2)}, u32[]{:S(2)}) collective-permute-start(f32[2,544,128]{2,1,0:T(8,128)} %get-tuple-element.17), channel_id=1, source_target_pairs={{0,1},{1,0},{2,3},{3,2},{4,5},{5,4},{6,7},{7,6},{8,9},{9,8},{10,11... | collective-permute-start | bytes 1671176 | tf_op jit(solution)/shard_map/ppermute | solution.py:410
  20.0 3.0 %leaf_forward.1.refs_3_ = bf16[8,336,128]{2,1,0:T(8,128)(2,1)} custom-call(s32[2,4]{1,0:T(2,128)} %refs_0_.2, bf16[2,128,256]{2,1,0:T(8,128)(2,1)} %refs_1_.4, bf16[2,128,128]{2,1,0:T(8,128)(2,1)} %refs_2_.3, bf16[2,4,128,128]{3,2,1,0:T(8,128)(2,1)} %refs_3_.3, f32[2,544,128]{2,1,0:T(8,128)} %get-tuple-element.16.refs_4_.refs_1_), custom_call_target="tpu_custom_call" | custom-call | tf_op jit(solution)/shard_map/leaf_forward/pallas_call | solution.py:50
  23.0 0.0 collective-permute-done.refs_2_
  23.0 0.0 copy-start.6
  23.0 0.8 copy-done.6
  23.8 3.1 %chip_maps.1 = (f32[2,2,544,128]{3,2,1,0:T(8,128)}, bf16[5,64,128]{2,1,0:T(8,128)(2,1)}, f32[256,512]{1,0:T(8,128)}) custom-call(s32[5]{0:T(128)} %stack.23.refs_0_, f32[2,544,128]{2,1,0:T(8,128)} %get-tuple-element.16.refs_4_.refs_1_, f32[2,544,128]{2,1,0:T(8,128)} %copy-done.6, bf16[8,336,128]{2,1,0:T(8,128)(2,1)} %leaf_forward.1.refs_3_), custom_call_target="tpu_custom_call" | custom-call | tf_op jit(solution)/shard_map/chip_maps/pallas_call | solution.py:50
  27.0 0.0 copy-start.1
  27.0 0.0 all-gather.6.cloned.1.call-update
  27.0 14.8 %all_to_all.30.refs_1_ = bf16[8,336,128]{2,1,0:T(8,128)(2,1)S(1)} all-to-all(bf16[8,336,128]{2,1,0:T(8,128)(2,1)} %leaf_forward.1.refs_3_), channel_id=1, replica_groups=mesh['layer'=4,'row'=4,'zh'=4,'zl'=4,'core'=2] {'layer','core'}, dimensions={0} | all-to-all | bytes 1376256 | tf_op jit(solution)/shard_map/all_to_all | solution.py:368
  41.8 0.0 copy-start.3
  41.8 0.9 copy-done.3
  42.7 1.7 scatter_updates.1
  44.4 10.7 %all-to-all-start.1 = ((bf16[16,4,32,128]{3,2,1,0:T(8,128)(2,1)}), bf16[16,4,32,128]{3,2,1,0:T(8,128)(2,1)S(1)}, u32[]{:S(2)}, u32[]{:S(2)}) async-start(bf16[16,4,32,128]{3,2,1,0:T(8,128)(2,1)} %get-tuple-element.19.refs_2_), calls=%async_computation.1 | async-start | bytes 1048576 | tf_op jit(solution)/shard_map/all_to_all | solution.py:368
  55.1 0.0 all-gather.8.cloned.1.call-start
  55.2 1.9 join_upper.1
  57.0 0.0 all-gather.8.cloned.1.call-update
  57.0 25.0 %all-to-all-done.1.refs_0_ = bf16[16,4,32,128]{3,2,1,0:T(8,128)(2,1)S(1)} async-done(((bf16[16,4,32,128]{3,2,1,0:T(8,128)(2,1)}), bf16[16,4,32,128]{3,2,1,0:T(8,128)(2,1)S(1)}, u32[]{:S(2)}, u32[]{:S(2)}) %all-to-all-start.1) | async-done | bytes 524320 | tf_op jit(solution)/shard_map/all_to_all | solution.py:368
  82.1 0.0 copy-done.1
  82.1 1.0 chip_solve.1
  83.1 0.0 copy-start.4
  83.1 0.6 copy-done.4
  83.7 27.0 %all_to_all.31.refs_2_ = bf16[16,2,32,128]{3,2,1,0:T(8,128)(2,1)} all-to-all(bf16[16,2,32,128]{3,2,1,0:T(8,128)(2,1)S(1)} %get-tuple-element.21), channel_id=1, replica_groups=mesh['layer'=4,'row'=4,'zh'=4,'zl'=4,'core'=2] {'zh','zl'}, dimensions={0} | all-to-all | bytes 524288 | tf_op jit(solution)/shard_map/all_to_all | solution.py:368
  110.7 2.8 %all-gather.6.cloned.1.call-done = bf16[160,64,128]{2,1,0:T(8,128)(2,1)} async-done(((bf16[5,64,128]{2,1,0:T(8,128)(2,1)}), bf16[160,64,128]{2,1,0:T(8,128)(2,1)}) %all-gather.6.cloned.1.call-update) | async-done | bytes 2621456 | tf_op jit(solution)/shard_map/all_gather | solution.py:432
  113.5 7.3 %row_solve.1 = (bf16[4,768,128]{2,1,0:T(8,128)(2,1)}, f32[3,128,128]{2,1,0:T(8,128)}, f32[2,32,128]{2,1,0:T(8,128)}) custom-call(s32[5]{0:T(128)} %stack.23.refs_0_, bf16[32,5,64,128]{3,2,1,0:T(8,128)(2,1)} %bitcast.15, bf16[16,2,32,128]{3,2,1,0:T(8,128)(2,1)} %all_to_all.31.refs_2_), custom_call_target="tpu_custom_call" | custom-call | tf_op jit(solution)/shard_map/row_solve/pallas_call | solution.py:50
  120.8 0.0 copy-start.5
  120.8 13.5 %all_to_all.32.refs_1_ = bf16[4,768,128]{2,1,0:T(8,128)(2,1)} all-to-all(bf16[4,768,128]{2,1,0:T(8,128)(2,1)} %get-tuple-element.22), channel_id=1, replica_groups=mesh['layer'=4,'row'=4,'zh'=4,'zl'=4,'core'=2] {'row'}, dimensions={0} | all-to-all | bytes 1572864 | tf_op jit(solution)/shard_map/all_to_all | solution.py:368
  134.3 3.3 %top_solve.1 = (f32[4,32,128]{2,1,0:T(8,128)}, bf16[16,4,32,128]{3,2,1,0:T(8,128)(2,1)}) custom-call(s32[5]{0:T(128)} %stack.23.refs_0_, bf16[4,768,128]{2,1,0:T(8,128)(2,1)} %all_to_all.32.refs_1_, f32[3,128,128]{2,1,0:T(8,128)} %get-tuple-element.23.refs_2_, f32[2,32,128]{2,1,0:T(8,128)} %get-tuple-element.24.refs_3_, ...), custom_call_target="tpu_custom_call" | custom-call | tf_op jit(solution)/shard_map/top_solve/pallas_call | solution.py:50
  137.5 10.1 %all-to-all-start.4 = ((bf16[16,4,32,128]{3,2,1,0:T(8,128)(2,1)}), bf16[16,4,32,128]{3,2,1,0:T(8,128)(2,1)S(1)}, u32[]{:S(2)}, u32[]{:S(2)}) async-start(bf16[16,4,32,128]{3,2,1,0:T(8,128)(2,1)} %get-tuple-element.27), calls=%async_computation.4 | async-start | bytes 1048576 | tf_op jit(solution)/shard_map/all_to_all | solution.py:368
  147.7 16.2 %all-gather.2 = f32[32,32,128]{2,1,0:T(8,128)S(1)} all-gather(f32[4,32,128]{2,1,0:T(8,128)} %get-tuple-element.29), channel_id=4, replica_groups=mesh['layer'=4,'row'=4,'zh'=4,'zl'=4,'core'=2] {'layer','core'}, dimensions={0}, use_global_device_ids=true | all-gather | bytes 589824 | tf_op jit(solution)/shard_map/all_gather | solution.py:476
  163.9 0.0 copy-done.5
  163.9 1.4 turn_sep.1.refs_4_
  165.2 0.0 all-gather.8.cloned.1.call-done
  165.2 4.5 %all-to-all-done.4 = bf16[16,4,32,128]{3,2,1,0:T(8,128)(2,1)S(1)} async-done(((bf16[16,4,32,128]{3,2,1,0:T(8,128)(2,1)}), bf16[16,4,32,128]{3,2,1,0:T(8,128)(2,1)S(1)}, u32[]{:S(2)}, u32[]{:S(2)}) %all-to-all-start.4) | async-done | bytes 524320 | tf_op jit(solution)/shard_map/all_to_all | solution.py:368
  169.8 0.0 copy-start
  169.8 1.7 copy-done
  171.5 0.0 copy-start.2
  171.5 0.9 copy-done.2
  172.5 3.0 %leaf_backward.1 = bf16[8,2,32,128]{3,2,1,0:T(8,128)(2,1)S(1)} custom-call(s32[8,8]{1,0:T(8,128)S(1)} %bitcast.14, bf16[64,32,128]{2,1,0:T(8,128)(2,1)S(1)} %bitcast.12, bf16[8,2,32,128]{3,2,1,0:T(8,128)(2,1)S(1)} %get-tuple-element.28.refs_2_, bf16[8,2,640,128]{3,2,1,0:T(8,128)(2,1)S(1)} %bitcast.10, f32[2,128,256]{2,1,0:T(8,128)S(1)} %copy-done.2), custom_call_target="tpu_custom_call" | custom-call | tf_op jit(solution)/shard_map/leaf_backward/pallas_call | solution.py:50
  175.4 18.4 %all_to_all.33.refs_0_ = bf16[8,2,32,128]{3,2,1,0:T(8,128)(2,1)S(1)} all-to-all(bf16[8,2,32,128]{3,2,1,0:T(8,128)(2,1)S(1)} %leaf_backward.1), channel_id=1, replica_groups=mesh['layer'=4,'row'=4,'zh'=4,'zl'=4,'core'=2] {'layer','core'}, dimensions={0} | all-to-all | bytes 262144 | tf_op jit(solution)/shard_map/all_to_all | solution.py:368
  193.8 0.8 turn_leaf.1
  (1 shorter events, 0.0 us)
Async XLA Ops:
  7.2 106.3 %all-gather.6.cloned.1.call-start = ((), (), s32[]{:S(2)}) async-start(), calls=%async_computation.6 | async-start | bytes 2703360 | tf_op jit(solution)/shard_map/all_gather | solution.py:432
  11.2 11.8 %collective-permute-start = (f32[2,544,128]{2,1,0:T(8,128)}, f32[2,544,128]{2,1,0:T(8,128)S(1)}, u32[]{:S(2)}, u32[]{:S(2)}) collective-permute-start(f32[2,544,128]{2,1,0:T(8,128)} %get-tuple-element.17), channel_id=1, source_target_pairs={{0,1},{1,0},{2,3},{3,2},{4,5},{5,4},{6,7},{7,6},{8,9},{9,8},{10,11... | collective-permute-start | bytes 1671176 | tf_op jit(solution)/shard_map/ppermute | solution.py:410
  23.0 0.8 copy-start.6
  27.0 55.1 %copy-start.1 = (f32[2,2,544,128]{3,2,1,0:T(8,128)S(1)}, f32[2,2,544,128]{3,2,1,0:T(8,128)}, u32[]{:S(2)}) copy-start(f32[2,2,544,128]{3,2,1,0:T(8,128)} %get-tuple-element.20.refs_1_) | copy-start | bytes 3342340
  41.8 0.9 copy-start.3
  44.4 37.6 %all-to-all-start.1 = ((bf16[16,4,32,128]{3,2,1,0:T(8,128)(2,1)}), bf16[16,4,32,128]{3,2,1,0:T(8,128)(2,1)S(1)}, u32[]{:S(2)}, u32[]{:S(2)}) async-start(bf16[16,4,32,128]{3,2,1,0:T(8,128)(2,1)} %get-tuple-element.19.refs_2_), calls=%async_computation.1 | async-start | bytes 1048576 | tf_op jit(solution)/shard_map/all_to_all | solution.py:368
  55.1 110.1 %all-gather.8.cloned.1.call-start = ((), (), s32[]{:S(2)}) async-start(), calls=%async_computation.7 | async-start | bytes 2949120 | tf_op jit(solution)/shard_map/all_gather | solution.py:474
  83.1 0.6 copy-start.4
  120.8 43.1 %copy-start.5 = (s32[5]{0:T(128)S(1)}, s32[5]{0:T(128)}, u32[]{:S(2)}) copy-start(s32[5]{0:T(128)} %stack.23.refs_0_) | copy-start | bytes 64
  137.5 32.2 %all-to-all-start.4 = ((bf16[16,4,32,128]{3,2,1,0:T(8,128)(2,1)}), bf16[16,4,32,128]{3,2,1,0:T(8,128)(2,1)S(1)}, u32[]{:S(2)}, u32[]{:S(2)}) async-start(bf16[16,4,32,128]{3,2,1,0:T(8,128)(2,1)} %get-tuple-element.27), calls=%async_computation.4 | async-start | bytes 1048576 | tf_op jit(solution)/shard_map/all_to_all | solution.py:368
  169.8 1.7 copy-start
  171.5 0.9 copy-start.2
Sparse Core Ops, SparseCore 0:
  27.1 86.3 all-gather.5
  115.6 32.2 all-gather.7

commit v4 on v3

--- a/solution.py
+++ b/solution.py
@@ -120,7 +120,7 @@
                 sent_ref[j, slot * width : (slot + 1) * width] = update[j * width : (j + 1) * width]
 
 
-def sep_prepare(at_ref, *refs):
+def sep_prepare(*refs):
     sources, (mine_ref, other_ref), landed, sems, turned = refs[:5], refs[5:7], refs[7:12], refs[12], refs[13]
     copies = start_copies(sources, landed, sems)
     li_ref, ll_ref, ui_ref, ul_ref, rhs_ref = landed
@@ -131,10 +131,10 @@
         turned[s] = rhs_ref[s].T
         li, ui = li_ref[s], ui_ref[s]
         blocks = (-mm(li, ll_ref[s]).T, -mm(ui, ul_ref[s]).T, li.T, ui.T)
-        for ref, core in ((mine_ref, at_ref[4]), (other_ref, 1 - at_ref[4])):
+        for ref, core in ((mine_ref, lax.axis_index("core")), (other_ref, 1 - lax.axis_index("core"))):
             for k in range(4):
                 ref[s, k * B : (k + 1) * B] = blocks[k]
-            first = pl.multiple_of((2 * at_ref[0] + core) * width, width)
+            first = pl.multiple_of((2 * lax.axis_index("layer") + core) * width, width)
             ref[s, 4 * B :] = turned[s, pl.ds(first, width)]
 
 
@@ -142,15 +142,15 @@
     return split(maps[0]) + split(maps[1]) + (maps[2].astype(bf16),)
 
 
-def send_half(at_ref, maps, half_ref, whole):
+def send_half(maps, half_ref, whole):
     for m, part in enumerate(map_parts(maps)):
         whole[m] = part
-    half_ref[...] = whole[:, pl.ds(pl.multiple_of(at_ref[4] * (B // 2), B // 2), B // 2)]
-
-
-def chip_maps(at_ref, mine_ref, other_ref, sep_ref, half_ref, wy_ref, whole):
-    sep_ref[at_ref[4]] = mine_ref[...]
-    sep_ref[1 - at_ref[4]] = other_ref[...]
+    half_ref[...] = whole[:, pl.ds(pl.multiple_of(lax.axis_index("core") * (B // 2), B // 2), B // 2)]
+
+
+def chip_maps(mine_ref, other_ref, sep_ref, half_ref, wy_ref, whole):
+    sep_ref[lax.axis_index("core")] = mine_ref[...]
+    sep_ref[1 - lax.axis_index("core")] = other_ref[...]
 
     def block(s, k):
         return sep_ref[s // 2, s % 2, k * B : (k + 1) * B]
@@ -166,7 +166,7 @@
         wy = mm(wy, block(s, 1))
         wy = jnp.concatenate([wy[:B] + mm(reach[s], block(s, 3)), wy[B:]], axis=0)
         wy_ref[:, s * B : (s + 1) * B] = wy
-    send_half(at_ref, (reach[3], wy[B:], wy[:B]), half_ref, whole)
+    send_half((reach[3], wy[B:], wy[:B]), half_ref, whole)
 
 
 def chip_solve(got_ref, sep_ref, bg_ref, local_ref):
@@ -250,7 +250,7 @@
         keep[first + q, 1] = nothing if u is None else u[B : B + width]
 
 
-def row_solve(at_ref, maps_hbm, bg_ref, out_ref, xyz_ref, own_ref, maps_ref, sems, keep_maps, keep):
+def row_solve(maps_hbm, bg_ref, out_ref, xyz_ref, own_ref, maps_ref, sems, keep_maps, keep):
     width = bg_ref.shape[2]
     quads = [pl.ds(8 * h, 8) for h in range(4)]
     copies = start_copies([maps_hbm.at[q] for q in quads], [maps_ref.at[q] for q in quads], sems)
@@ -277,7 +277,7 @@
             out_ref[n, m * B : (m + 1) * B] = sent[m]
         for m in range(4):
             out_ref[n, 5 * B + m * width : 5 * B + (m + 1) * width] = sides[m]
-    high, low = 16 + at_ref[2], 4 * at_ref[2] + at_ref[1]
+    high, low = 16 + lax.axis_index("zh"), 4 * lax.axis_index("zh") + lax.axis_index("zl")
     x, y, z = (keep_maps[low, m] for m in range(3))
     f = mm(jnp.concatenate([keep_maps[high, 0], keep[high, 0]], axis=0), x)
     u = mm(jnp.concatenate([keep_maps[high, 2], keep_maps[high, 1], keep[high, 1]], axis=0), y)
@@ -308,7 +308,7 @@
             u = mm(u, maps[q][1]) + turned[q]
 
 
-def top_solve(at_ref, got_ref, xyz_ref, own_ref, wy_ref, local_ref, sep_ref, low_ref, keep):
+def top_solve(got_ref, xyz_ref, own_ref, wy_ref, local_ref, sep_ref, low_ref, keep):
     width = own_ref.shape[1]
     count = got_ref.shape[0]
     maps, bgs = [], []
@@ -320,7 +320,7 @@
         ]
         bgs.append([side[0] + side[1], side[2] + side[3]])
     chain(maps, bgs, keep)
-    f, u = keep[at_ref[3], 0], keep[at_ref[3], 1]
+    f, u = keep[lax.axis_index("row"), 0], keep[lax.axis_index("row"), 1]
     f, u = (
         mm(f, xyz_ref[0]) + own_ref[0],
         mm(u, xyz_ref[1]) + mm(f, xyz_ref[2]) + own_ref[1],
@@ -357,9 +357,10 @@
         out_ref[k] = whole.astype(f32).T.astype(bf16)
 
 
-def turn_sep(at_ref, got_ref, out_ref):
+def turn_sep(place_ref, got_ref, out_ref, pass_ref):
+    pass_ref[...] = place_ref[...]
     for k in range(2):
-        s = 2 * at_ref[4] + k
+        s = 2 * lax.axis_index("core") + k
         whole = jnp.concatenate([got_ref[j, s] for j in range(got_ref.shape[0])], axis=0)
         out_ref[k] = whole.T
 
@@ -387,9 +388,6 @@
     groups = 2 * layers
     width = 256 // groups
     chips = highs * lows
-    at = jnp.stack(
-        [lax.axis_index(name) for name in ("layer", "zl", "zh", "row", "core")]
-    ).astype(jnp.int32)
 
     along = ("zh", "zl")
     pair = (2, width, B)
@@ -403,10 +401,9 @@
         (blocks, blocks),
         landing(sources) + [pltpu.VMEM((2, 256, B), f32)],
         "sep_prepare",
-        smem=(0,),
-        hbm=range(1, 6),
+        hbm=range(0, 5),
         limit=VMEM_ALL,
-    )(at, *sources)
+    )(*sources)
     theirs = lax.ppermute(others, "core", [(0, 1), (1, 0)])
 
     sources = (leaf_rhs, leaf_lower_inv, leaf_lower)
@@ -425,10 +422,9 @@
         (shaped((2, 2, 4 * B + width, B), f32), half_maps, shaped((2 * B, 4 * B), f32)),
         [pltpu.VMEM((5, B, B), bf16)],
         "chip_maps",
-        smem=(0,),
         limit=VMEM_ALL,
         after=(sent,),
-    )(at, mine, theirs)
+    )(mine, theirs)
     by_chip = lax.all_gather(half, along + ("core",)).reshape((2 * chips,) + half_maps.shape)
 
     got = exchange(sent, across)
@@ -439,7 +435,6 @@
         [pltpu.VMEM((4 * chips, width, B), f32)],
         "scatter_updates",
         smem=(0,),
-        after=(half,),
     )(place, got)
 
     bg, local = call(
@@ -455,18 +450,16 @@
             pltpu.VMEM((20,) + pair, f32),
         ],
         "row_solve",
-        smem=(0,),
-        hbm=(1,),
+        hbm=(0,),
         limit=VMEM_ALL,
-    )(at, by_chip, exchange(bg, along))
+    )(by_chip, exchange(bg, along))
     solved, solved_low = call(
         top_solve,
         (shaped((4, width, B), f32), shaped((chips, 4, width, B), bf16)),
         [pltpu.VMEM((rows,) + pair, f32)],
         "top_solve",
-        smem=(0,),
         limit=VMEM_ALL,
-    )(at, exchange(sent_on, "row"), xyz, own, wy, local)
+    )(exchange(sent_on, "row"), xyz, own, wy, local)
 
     joined = call(
         join_upper, shaped((2, 5 * B, B), bf16), name="join_upper", after=(sums,), limit=VMEM_ALL
@@ -474,13 +467,17 @@
     upper = lax.all_gather(joined, across).reshape((groups, 2, 5 * B, B))
     low = exchange(solved_low, along).reshape(4 * chips, width, B)
     sep_all = lax.all_gather(solved, across).reshape((groups, 4, width, B))
-    sep_part = call(turn_sep, shaped((2, B, 256), f32), name="turn_sep", smem=(0,))(at, sep_all)
+    sep_part, place = call(
+        turn_sep,
+        (shaped((2, B, 256), f32), shaped(place.shape, jnp.int32)),
+        name="turn_sep",
+        after=(upper,),
+    )(place, sep_all)
     back = call(
         leaf_backward,
         shaped((groups, 2, width, B), bf16),
         name="leaf_backward",
         smem=(0,),
-        after=(sep_part,),
     )(place, low, forward, upper)
     leaf_part = call(turn_leaf, shaped((2, B, 256), bf16), name="turn_leaf")(exchange(back, across))
     return (leaf_part, sep_part)

time: 202 us -> 198 us (0.980)
  blocking collectives: 89.8 us -> 85.4 us
  starting transfers between devices: 29.6 us -> 32.7 us
  local copies, waits for them, and re-layouts: 5.65 us -> 3.59 us
    all_to_all x4, blocking collectives: 73.6 us -> 69.7 us  [exchange(): return lax.all_to_all(value, axes, split_axis=0, concat_axis=0, tiled=True)]
    all_to_all x2, starting transfers between devices: 20.8 us -> 23.8 us  [exchange(): return lax.all_to_all(value, axes, split_axis=0, concat_axis=0, tiled=True)]
    unnamed x14 -> x12, local copies, waits for them, and re-layouts: 4.99 us -> 3.59 us
where the time goes in v4:
time: 198 us; the launch traced here: 197 us
  blocking collectives  85.4 us (43%)
  starting transfers between devices  32.7 us (17%)
  waiting for transfers between devices  32.7 us (17%)
  Pallas kernels  28.7 us (14%)
  between operations  14.1 us (7%)
  local copies, waits for them, and re-layouts  3.59 us (2%)
    all_to_all x4, blocking collectives, exchange(): return lax.all_to_all(value, axes, split_axis=0, concat_axis=0, tiled=True)  69.7 us
    all_to_all x2, waiting for transfers between devices, exchange(): return lax.all_to_all(value, axes, split_axis=0, concat_axis=0, tiled=True)  29.7 us
    pallas_call x11, Pallas kernels, run(): pl.pallas_call(body, out_shape=outs, in_specs=[pl.BlockSpec(memory_space=...  28.7 us
    all_to_all x2, starting transfers between devices, exchange(): return lax.all_to_all(value, axes, split_axis=0, concat_axis=0, tiled=True)  23.8 us
    all_gather x1, blocking collectives, on_device(): sep_all = lax.all_gather(solved, across).reshape((groups, 4, width, B))  15.7 us
    ppermute x1, starting transfers between devices, on_device(): theirs = lax.ppermute(others, 'core', [(0, 1), (1, 0)])  8.79 us
  transfers between devices with their start and end apart: 5, of which 3 were waited for; matrix products, arithmetic and copies ran while one was open for 0% of the time, Pallas kernels for 10%

profile of v4, /device:TPU:1, one launch (start us, length us, event | category | flops | bytes accessed | tf_op | source)
XLA Modules:
  0.0 197.2 jit_solution(14773402886349701614)
XLA Ops:
  7.2 0.0 all-gather.6.cloned.1.call-start
  7.2 2.6 %sep_prepare.1 = (f32[2,544,128]{2,1,0:T(8,128)}, f32[2,544,128]{2,1,0:T(8,128)}) custom-call(f32[2,128,128]{2,1,0:T(8,128)} %refs_0_.3, f32[2,128,128]{2,1,0:T(8,128)} %refs_1_.3, f32[2,128,128]{2,1,0:T(8,128)} %refs_2_.2, f32[2,128,128]{2,1,0:T(8,128)} %refs_3_.2, f32[2,128,256]{2,1,0:T(8,128)} %refs_4_.1), custom_call_target="tpu_custom_call" | custom-call | tf_op jit(solution)/shard_map/sep_prepare/pallas_call | solution.py:50
  9.9 8.8 %collective-permute-start = (f32[2,544,128]{2,1,0:T(8,128)}, f32[2,544,128]{2,1,0:T(8,128)S(1)}, u32[]{:S(2)}, u32[]{:S(2)}) collective-permute-start(f32[2,544,128]{2,1,0:T(8,128)} %get-tuple-element.19), channel_id=1, source_target_pairs={{0,1},{1,0},{2,3},{3,2},{4,5},{5,4},{6,7},{7,6},{8,9},{9,8},{10,11... | collective-permute-start | bytes 1671176 | tf_op jit(solution)/shard_map/ppermute | solution.py:407
  18.7 3.0 %leaf_forward.1.refs_2_ = bf16[8,336,128]{2,1,0:T(8,128)(2,1)} custom-call(s32[2,4]{1,0:T(2,128)} %refs_0_.4, bf16[2,128,256]{2,1,0:T(8,128)(2,1)} %refs_1_.4, bf16[2,128,128]{2,1,0:T(8,128)(2,1)} %refs_2_.3, bf16[2,4,128,128]{3,2,1,0:T(8,128)(2,1)} %refs_3_.3, f32[2,544,128]{2,1,0:T(8,128)} %get-tuple-element.18.refs_4_.refs_0_), custom_call_target="tpu_custom_call" | custom-call | tf_op jit(solution)/shard_map/leaf_forward/pallas_call | solution.py:50
  21.7 0.0 collective-permute-done.refs_1_
  21.7 0.0 copy-start.5
  21.7 0.8 copy-done.5
  22.5 3.4 %chip_maps.1 = (f32[2,2,544,128]{3,2,1,0:T(8,128)}, bf16[5,64,128]{2,1,0:T(8,128)(2,1)}, f32[256,512]{1,0:T(8,128)}) custom-call(f32[2,544,128]{2,1,0:T(8,128)} %get-tuple-element.18.refs_4_.refs_0_, f32[2,544,128]{2,1,0:T(8,128)} %copy-done.5, bf16[8,336,128]{2,1,0:T(8,128)(2,1)} %leaf_forward.1.refs_2_), custom_call_target="tpu_custom_call" | custom-call | tf_op jit(solution)/shard_map/chip_maps/pallas_call | solution.py:50
  25.9 0.0 copy-start.3
  25.9 0.0 all-gather.6.cloned.1.call-update
  25.9 14.8 %all_to_all.30.refs_1_ = bf16[8,336,128]{2,1,0:T(8,128)(2,1)S(1)} all-to-all(bf16[8,336,128]{2,1,0:T(8,128)(2,1)} %leaf_forward.1.refs_2_), channel_id=1, replica_groups=mesh['layer'=4,'row'=4,'zh'=4,'zl'=4,'core'=2] {'layer','core'}, dimensions={0} | all-to-all | bytes 1376256 | tf_op jit(solution)/shard_map/all_to_all | solution.py:369
  40.8 1.7 scatter_updates.1
  42.5 10.7 %all-to-all-start.1 = ((bf16[16,4,32,128]{3,2,1,0:T(8,128)(2,1)}), bf16[16,4,32,128]{3,2,1,0:T(8,128)(2,1)S(1)}, u32[]{:S(2)}, u32[]{:S(2)}) async-start(bf16[16,4,32,128]{3,2,1,0:T(8,128)(2,1)} %get-tuple-element.21.refs_2_), calls=%async_computation.1 | async-start | bytes 1048576 | tf_op jit(solution)/shard_map/all_to_all | solution.py:369
  53.1 0.0 all-gather.8.cloned.1.call-start
  53.2 1.9 join_upper.1
  55.0 0.0 all-gather.8.cloned.1.call-update
  55.1 26.1 %all-to-all-done.1.refs_0_ = bf16[16,4,32,128]{3,2,1,0:T(8,128)(2,1)S(1)} async-done(((bf16[16,4,32,128]{3,2,1,0:T(8,128)(2,1)}), bf16[16,4,32,128]{3,2,1,0:T(8,128)(2,1)S(1)}, u32[]{:S(2)}, u32[]{:S(2)}) %all-to-all-start.1) | async-done | bytes 524320 | tf_op jit(solution)/shard_map/all_to_all | solution.py:369
  81.2 0.0 copy-done.3
  81.2 1.0 chip_solve.1
  82.2 0.0 copy-start.4
  82.2 26.4 %all_to_all.31.refs_1_ = bf16[16,2,32,128]{3,2,1,0:T(8,128)(2,1)} all-to-all(bf16[16,2,32,128]{3,2,1,0:T(8,128)(2,1)S(1)} %get-tuple-element.23), channel_id=1, replica_groups=mesh['layer'=4,'row'=4,'zh'=4,'zl'=4,'core'=2] {'zh','zl'}, dimensions={0} | all-to-all | bytes 524288 | tf_op jit(solution)/shard_map/all_to_all | solution.py:369
  108.7 3.0 %all-gather.6.cloned.1.call-done = bf16[160,64,128]{2,1,0:T(8,128)(2,1)} async-done(((bf16[5,64,128]{2,1,0:T(8,128)(2,1)}), bf16[160,64,128]{2,1,0:T(8,128)(2,1)}) %all-gather.6.cloned.1.call-update) | async-done | bytes 2621456 | tf_op jit(solution)/shard_map/all_gather | solution.py:428
  111.7 7.3 %row_solve.1 = (bf16[4,768,128]{2,1,0:T(8,128)(2,1)}, f32[3,128,128]{2,1,0:T(8,128)}, f32[2,32,128]{2,1,0:T(8,128)}) custom-call(bf16[32,5,64,128]{3,2,1,0:T(8,128)(2,1)} %bitcast.11, bf16[16,2,32,128]{3,2,1,0:T(8,128)(2,1)} %all_to_all.31.refs_1_), custom_call_target="tpu_custom_call" | custom-call | tf_op jit(solution)/shard_map/row_solve/pallas_call | solution.py:50
  119.0 12.8 %all_to_all.32.refs_0_ = bf16[4,768,128]{2,1,0:T(8,128)(2,1)} all-to-all(bf16[4,768,128]{2,1,0:T(8,128)(2,1)} %get-tuple-element.24), channel_id=1, replica_groups=mesh['layer'=4,'row'=4,'zh'=4,'zl'=4,'core'=2] {'row'}, dimensions={0} | all-to-all | bytes 1572864 | tf_op jit(solution)/shard_map/all_to_all | solution.py:369
  131.8 0.0 copy-done.4
  131.8 3.2 %top_solve.1 = (f32[4,32,128]{2,1,0:T(8,128)}, bf16[16,4,32,128]{3,2,1,0:T(8,128)(2,1)}) custom-call(bf16[4,768,128]{2,1,0:T(8,128)(2,1)} %all_to_all.32.refs_0_, f32[3,128,128]{2,1,0:T(8,128)} %get-tuple-element.25.refs_1_, f32[2,32,128]{2,1,0:T(8,128)} %get-tuple-element.26.refs_2_, f32[256,512]{1,0:T(8,128)} %get-tuple-element.27.refs_3_, ...), custom_call_target="tpu_custom_call" | custom-call | tf_op jit(solution)/shard_map/top_solve/pallas_call | solution.py:50
  135.1 13.2 %all-to-all-start.4 = ((bf16[16,4,32,128]{3,2,1,0:T(8,128)(2,1)}), bf16[16,4,32,128]{3,2,1,0:T(8,128)(2,1)S(1)}, u32[]{:S(2)}, u32[]{:S(2)}) async-start(bf16[16,4,32,128]{3,2,1,0:T(8,128)(2,1)} %get-tuple-element.31), calls=%async_computation.4 | async-start | bytes 1048576 | tf_op jit(solution)/shard_map/all_to_all | solution.py:369
  148.2 15.7 %all-gather.1 = f32[32,32,128]{2,1,0:T(8,128)} all-gather(f32[4,32,128]{2,1,0:T(8,128)} %get-tuple-element.29), channel_id=3, replica_groups=mesh['layer'=4,'row'=4,'zh'=4,'zl'=4,'core'=2] {'layer','core'}, dimensions={0}, use_global_device_ids=true | all-gather | bytes 589824 | tf_op jit(solution)/shard_map/all_gather | solution.py:469
  163.9 0.0 all-gather.8.cloned.1.call-done
  163.9 0.0 copy-start
  163.9 1.7 copy-done
  165.6 0.0 copy-start.2
  165.6 1.0 copy-done.2
  166.7 0.0 copy-start.1
  166.7 0.8 turn_sep.1
  167.5 3.5 %all-to-all-done.4 = bf16[16,4,32,128]{3,2,1,0:T(8,128)(2,1)S(1)} async-done(((bf16[16,4,32,128]{3,2,1,0:T(8,128)(2,1)}), bf16[16,4,32,128]{3,2,1,0:T(8,128)(2,1)S(1)}, u32[]{:S(2)}, u32[]{:S(2)}) %all-to-all-start.4) | async-done | bytes 524320 | tf_op jit(solution)/shard_map/all_to_all | solution.py:369
  171.0 0.0 copy-done.1
  171.0 3.0 %leaf_backward.1 = bf16[8,2,32,128]{3,2,1,0:T(8,128)(2,1)S(1)} custom-call(s32[8,8]{1,0:T(8,128)S(1)} %get-tuple-element.30.refs_0_, bf16[64,32,128]{2,1,0:T(8,128)(2,1)S(1)} %bitcast.7, bf16[8,2,32,128]{3,2,1,0:T(8,128)(2,1)S(1)} %get-tuple-element.32.refs_2_, bf16[8,2,640,128]{3,2,1,0:T(8,128)(2,1)S(1)} %bitcast.6), custom_call_target="tpu_custom_call" | custom-call | tf_op jit(solution)/shard_map/leaf_backward/pallas_call | solution.py:50
  174.0 15.6 %all_to_all.33.refs_0_ = bf16[8,2,32,128]{3,2,1,0:T(8,128)(2,1)S(1)} all-to-all(bf16[8,2,32,128]{3,2,1,0:T(8,128)(2,1)S(1)} %leaf_backward.1), channel_id=1, replica_groups=mesh['layer'=4,'row'=4,'zh'=4,'zl'=4,'core'=2] {'layer','core'}, dimensions={0} | all-to-all | bytes 262144 | tf_op jit(solution)/shard_map/all_to_all | solution.py:369
  189.6 0.8 turn_leaf.1
  (1 shorter events, 0.0 us)
Async XLA Ops:
  7.2 104.5 %all-gather.6.cloned.1.call-start = ((), (), s32[]{:S(2)}) async-start(), calls=%async_computation.6 | async-start | bytes 2703360 | tf_op jit(solution)/shard_map/all_gather | solution.py:428
  9.9 11.8 %collective-permute-start = (f32[2,544,128]{2,1,0:T(8,128)}, f32[2,544,128]{2,1,0:T(8,128)S(1)}, u32[]{:S(2)}, u32[]{:S(2)}) collective-permute-start(f32[2,544,128]{2,1,0:T(8,128)} %get-tuple-element.19), channel_id=1, source_target_pairs={{0,1},{1,0},{2,3},{3,2},{4,5},{5,4},{6,7},{7,6},{8,9},{9,8},{10,11... | collective-permute-start | bytes 1671176 | tf_op jit(solution)/shard_map/ppermute | solution.py:407
  21.7 0.8 copy-start.5
  25.9 55.3 %copy-start.3 = (f32[2,2,544,128]{3,2,1,0:T(8,128)S(1)}, f32[2,2,544,128]{3,2,1,0:T(8,128)}, u32[]{:S(2)}) copy-start(f32[2,2,544,128]{3,2,1,0:T(8,128)} %get-tuple-element.22.refs_1_) | copy-start | bytes 3342340
  42.5 38.7 %all-to-all-start.1 = ((bf16[16,4,32,128]{3,2,1,0:T(8,128)(2,1)}), bf16[16,4,32,128]{3,2,1,0:T(8,128)(2,1)S(1)}, u32[]{:S(2)}, u32[]{:S(2)}) async-start(bf16[16,4,32,128]{3,2,1,0:T(8,128)(2,1)} %get-tuple-element.21.refs_2_), calls=%async_computation.1 | async-start | bytes 1048576 | tf_op jit(solution)/shard_map/all_to_all | solution.py:369
  53.1 110.7 %all-gather.8.cloned.1.call-start = ((), (), s32[]{:S(2)}) async-start(), calls=%async_computation.7 | async-start | bytes 2949120 | tf_op jit(solution)/shard_map/all_gather | solution.py:467
  82.2 49.6 %copy-start.4 = (f32[4,32,128]{2,1,0:T(8,128)}, f32[4,32,128]{2,1,0:T(8,128)S(1)}, u32[]{:S(2)}) copy-start(f32[4,32,128]{2,1,0:T(8,128)S(1)} %get-tuple-element.28.refs_4_) | copy-start | bytes 196612
  135.1 36.0 %all-to-all-start.4 = ((bf16[16,4,32,128]{3,2,1,0:T(8,128)(2,1)}), bf16[16,4,32,128]{3,2,1,0:T(8,128)(2,1)S(1)}, u32[]{:S(2)}, u32[]{:S(2)}) async-start(bf16[16,4,32,128]{3,2,1,0:T(8,128)(2,1)} %get-tuple-element.31), calls=%async_computation.4 | async-start | bytes 1048576 | tf_op jit(solution)/shard_map/all_to_all | solution.py:369
  163.9 1.7 copy-start
  165.6 1.0 copy-start.2
  166.7 4.4 %copy-start.1 = (bf16[16,640,128]{2,1,0:T(8,128)(2,1)S(1)}, bf16[16,640,128]{2,1,0:T(8,128)(2,1)}, u32[]{:S(2)}) copy-start(bf16[16,640,128]{2,1,0:T(8,128)(2,1)} %all-gather.8.cloned.1.call-done) | copy-start | bytes 7864324
Sparse Core Ops, SparseCore 0:
  26.0 85.6 all-gather.5
  113.8 31.9 all-gather.7

commit v5 on v4

--- a/solution.py
+++ b/solution.py
@@ -148,7 +148,7 @@
     half_ref[...] = whole[:, pl.ds(pl.multiple_of(lax.axis_index("core") * (B // 2), B // 2), B // 2)]
 
 
-def chip_maps(mine_ref, other_ref, sep_ref, half_ref, wy_ref, whole):
+def chip_dependence(mine_ref, other_ref, sep_ref):
     sep_ref[lax.axis_index("core")] = mine_ref[...]
     sep_ref[1 - lax.axis_index("core")] = other_ref[...]
 
@@ -158,15 +158,24 @@
     reach = [block(0, 0)]
     for s in range(1, 4):
         reach.append(mm(reach[-1], block(s, 0)))
-    w = mm(reach[3], block(3, 3))
-    y = block(3, 1)
-    wy = jnp.concatenate([w, y], axis=0)
-    wy_ref[:, 3 * B :] = wy
+    wy = jnp.concatenate([mm(reach[3], block(3, 3)), block(3, 1)], axis=0)
+    wys = [wy]
     for s in (2, 1, 0):
         wy = mm(wy, block(s, 1))
         wy = jnp.concatenate([wy[:B] + mm(reach[s], block(s, 3)), wy[B:]], axis=0)
-        wy_ref[:, s * B : (s + 1) * B] = wy
-    send_half((reach[3], wy[B:], wy[:B]), half_ref, whole)
+        wys.insert(0, wy)
+    return reach[3], wys
+
+
+def chip_maps(mine_ref, other_ref, half_ref, whole, seps):
+    reach, wys = chip_dependence(mine_ref, other_ref, seps)
+    send_half((reach, wys[0][B:], wys[0][:B]), half_ref, whole)
+
+
+def chip_entries(mine_ref, other_ref, half_ref, sep_ref, wy_ref):
+    _, wys = chip_dependence(mine_ref, other_ref, sep_ref)
+    for s in range(4):
+        wy_ref[:, s * B : (s + 1) * B] = wys[s]
 
 
 def chip_solve(got_ref, sep_ref, bg_ref, local_ref):
@@ -270,13 +279,13 @@
         quad_sides.append(side)
     row, side, entering, leaving = compose(quad_maps, quad_sides)
     keep_entries(keep_maps, keep, 16, entering, leaving, width)
-    sent = map_parts(row)
+    sent = [part.astype(bf16) for part in row]
     sides = split(side[0]) + split(side[1])
     for n in range(out_ref.shape[0]):
-        for m in range(5):
+        for m in range(3):
             out_ref[n, m * B : (m + 1) * B] = sent[m]
         for m in range(4):
-            out_ref[n, 5 * B + m * width : 5 * B + (m + 1) * width] = sides[m]
+            out_ref[n, 3 * B + m * width : 3 * B + (m + 1) * width] = sides[m]
     high, low = 16 + lax.axis_index("zh"), 4 * lax.axis_index("zh") + lax.axis_index("zl")
     x, y, z = (keep_maps[low, m] for m in range(3))
     f = mm(jnp.concatenate([keep_maps[high, 0], keep[high, 0]], axis=0), x)
@@ -313,10 +322,9 @@
     count = got_ref.shape[0]
     maps, bgs = [], []
     for q in range(count):
-        part = [got_ref[q, m * B : (m + 1) * B].astype(f32) for m in range(5)]
-        maps.append([part[0] + part[1], part[2] + part[3], part[4]])
+        maps.append([got_ref[q, m * B : (m + 1) * B].astype(f32) for m in range(3)])
         side = [
-            got_ref[q, 5 * B + m * width : 5 * B + (m + 1) * width].astype(f32) for m in range(4)
+            got_ref[q, 3 * B + m * width : 3 * B + (m + 1) * width].astype(f32) for m in range(4)
         ]
         bgs.append([side[0] + side[1], side[2] + side[3]])
     chain(maps, bgs, keep)
@@ -417,14 +425,20 @@
         limit=VMEM_ALL,
         after=(mine,),
     )(targets, *sources)
-    seps, half, wy = call(
+    half = call(
         chip_maps,
-        (shaped((2, 2, 4 * B + width, B), f32), half_maps, shaped((2 * B, 4 * B), f32)),
-        [pltpu.VMEM((5, B, B), bf16)],
+        half_maps,
+        [pltpu.VMEM((5, B, B), bf16), pltpu.VMEM((2, 2, 4 * B + width, B), f32)],
         "chip_maps",
         limit=VMEM_ALL,
         after=(sent,),
     )(mine, theirs)
+    seps, wy = call(
+        chip_entries,
+        (shaped((2, 2, 4 * B + width, B), f32), shaped((2 * B, 4 * B), f32)),
+        name="chip_entries",
+        limit=VMEM_ALL,
+    )(mine, theirs, half)
     by_chip = lax.all_gather(half, along + ("core",)).reshape((2 * chips,) + half_maps.shape)
 
     got = exchange(sent, across)
@@ -442,7 +456,7 @@
     )(exchange(sums, along), seps)
     sent_on, xyz, own = call(
         row_solve,
-        (shaped((rows, 5 * B + 4 * width, B), bf16), maps, shaped(pair, f32)),
+        (shaped((rows, 3 * B + 4 * width, B), bf16), maps, shaped(pair, f32)),
         [
             pltpu.VMEM((2 * chips,) + half_maps.shape, bf16),
             pltpu.SemaphoreType.DMA((4,)),

time: 198 us -> 194 us (0.980)
  blocking collectives: 85.4 us -> 81.8 us
  waiting for transfers between devices: 32.7 us -> 29.7 us
  Pallas kernels: 28.7 us -> 31.5 us
    all_to_all x4, blocking collectives: 69.7 us -> 66.2 us  [exchange(): return lax.all_to_all(value, axes, split_axis=0, concat_axis=0, tiled=True)]
    pallas_call x11 -> x12, Pallas kernels: 28.7 us -> 31.5 us  [run(): pl.pallas_call(body, out_shape=outs, in_specs=[pl.BlockSpec(memory_space=...]
    all_to_all x2, waiting for transfers between devices: 29.7 us -> 27.4 us  [exchange(): return lax.all_to_all(value, axes, split_axis=0, concat_axis=0, tiled=True)]
  transfers between devices with their start and end apart: 5 -> 5, of which waited for: 3 -> 3; matrix products, arithmetic and copies ran while one was open for 0% -> 0% of each run, Pallas kernels for 10% -> 12%
where the time goes in v5:
time: 194 us; the launch traced here: 193 us
  blocking collectives  81.8 us (42%)
  Pallas kernels  31.5 us (16%)
  starting transfers between devices  31 us (16%)
  waiting for transfers between devices  29.7 us (15%)
  between operations  14.1 us (7%)
  local copies, waits for them, and re-layouts  4.83 us (2%)
    all_to_all x4, blocking collectives, exchange(): return lax.all_to_all(value, axes, split_axis=0, concat_axis=0, tiled=True)  66.2 us
    pallas_call x12, Pallas kernels, run(): pl.pallas_call(body, out_shape=outs, in_specs=[pl.BlockSpec(memory_space=...  31.5 us
    all_to_all x2, waiting for transfers between devices, exchange(): return lax.all_to_all(value, axes, split_axis=0, concat_axis=0, tiled=True)  27.4 us
    all_to_all x2, starting transfers between devices, exchange(): return lax.all_to_all(value, axes, split_axis=0, concat_axis=0, tiled=True)  22.2 us
    all_gather x1, blocking collectives, on_device(): sep_all = lax.all_gather(solved, across).reshape((groups, 4, width, B))  15.6 us
    ppermute x1, starting transfers between devices, on_device(): theirs = lax.ppermute(others, 'core', [(0, 1), (1, 0)])  8.79 us
    unnamed x12, local copies, waits for them, and re-layouts  4.83 us
  transfers between devices with their start and end apart: 5, of which 3 were waited for; matrix products, arithmetic and copies ran while one was open for 0% of the time, Pallas kernels for 12%

profile of v5, /device:TPU:1, one launch (start us, length us, event | category | flops | bytes accessed | tf_op | source)
XLA Modules:
  0.0 193.0 jit_solution(3468688824401049666)
XLA Ops:
  7.2 0.0 all-gather.6.cloned.1.call-start
  7.2 2.6 %sep_prepare.1 = (f32[2,544,128]{2,1,0:T(8,128)}, f32[2,544,128]{2,1,0:T(8,128)}) custom-call(f32[2,128,128]{2,1,0:T(8,128)} %refs_0_.3, f32[2,128,128]{2,1,0:T(8,128)} %refs_1_.3, f32[2,128,128]{2,1,0:T(8,128)} %refs_2_.2, f32[2,128,128]{2,1,0:T(8,128)} %refs_3_.2, f32[2,128,256]{2,1,0:T(8,128)} %refs_4_.1), custom_call_target="tpu_custom_call" | custom-call | tf_op jit(solution)/shard_map/sep_prepare/pallas_call | solution.py:50
  9.8 8.8 %collective-permute-start = (f32[2,544,128]{2,1,0:T(8,128)}, f32[2,544,128]{2,1,0:T(8,128)S(1)}, u32[]{:S(2)}, u32[]{:S(2)}) collective-permute-start(f32[2,544,128]{2,1,0:T(8,128)} %get-tuple-element.18), channel_id=1, source_target_pairs={{0,1},{1,0},{2,3},{3,2},{4,5},{5,4},{6,7},{7,6},{8,9},{9,8},{10,11... | collective-permute-start | bytes 1671176 | tf_op jit(solution)/shard_map/ppermute | solution.py:415
  18.6 3.0 %leaf_forward.1.refs_2_ = bf16[8,336,128]{2,1,0:T(8,128)(2,1)} custom-call(s32[2,4]{1,0:T(2,128)} %refs_0_.4, bf16[2,128,256]{2,1,0:T(8,128)(2,1)} %refs_1_.4, bf16[2,128,128]{2,1,0:T(8,128)(2,1)} %refs_2_.3, bf16[2,4,128,128]{3,2,1,0:T(8,128)(2,1)} %refs_3_.3, f32[2,544,128]{2,1,0:T(8,128)} %get-tuple-element.17.refs_4_.refs_0_), custom_call_target="tpu_custom_call" | custom-call | tf_op jit(solution)/shard_map/leaf_forward/pallas_call | solution.py:50
  21.7 0.0 collective-permute-done.refs_1_
  21.7 0.0 copy-start.5
  21.7 0.8 copy-done.5
  22.5 2.9 %chip_maps.1.refs_2_ = bf16[5,64,128]{2,1,0:T(8,128)(2,1)} custom-call(f32[2,544,128]{2,1,0:T(8,128)} %get-tuple-element.17.refs_4_.refs_0_, f32[2,544,128]{2,1,0:T(8,128)} %copy-done.5, bf16[8,336,128]{2,1,0:T(8,128)(2,1)} %leaf_forward.1.refs_2_), custom_call_target="tpu_custom_call" | custom-call | tf_op jit(solution)/shard_map/chip_maps/pallas_call | solution.py:50
  25.4 0.0 all-gather.6.cloned.1.call-update
  25.4 14.7 %all_to_all.30.refs_1_ = bf16[8,336,128]{2,1,0:T(8,128)(2,1)S(1)} all-to-all(bf16[8,336,128]{2,1,0:T(8,128)(2,1)} %leaf_forward.1.refs_2_), channel_id=1, replica_groups=mesh['layer'=4,'row'=4,'zh'=4,'zl'=4,'core'=2] {'layer','core'}, dimensions={0} | all-to-all | bytes 1376256 | tf_op jit(solution)/shard_map/all_to_all | solution.py:377
  40.1 1.8 scatter_updates.1
  41.9 10.7 %all-to-all-start.1 = ((bf16[16,4,32,128]{3,2,1,0:T(8,128)(2,1)}), bf16[16,4,32,128]{3,2,1,0:T(8,128)(2,1)S(1)}, u32[]{:S(2)}, u32[]{:S(2)}) async-start(bf16[16,4,32,128]{3,2,1,0:T(8,128)(2,1)} %get-tuple-element.19.refs_2_), calls=%async_computation.1 | async-start | bytes 1048576 | tf_op jit(solution)/shard_map/all_to_all | solution.py:377
  52.6 0.0 all-gather.8.cloned.1.call-start
  52.6 1.9 join_upper.1
  54.5 0.0 all-gather.8.cloned.1.call-update
  54.5 3.3 %chip_entries.1 = (f32[2,2,544,128]{3,2,1,0:T(8,128)}, f32[256,512]{1,0:T(8,128)}) custom-call(f32[2,544,128]{2,1,0:T(8,128)} %get-tuple-element.17.refs_4_.refs_0_, f32[2,544,128]{2,1,0:T(8,128)} %copy-done.5, bf16[5,64,128]{2,1,0:T(8,128)(2,1)} %chip_maps.1.refs_2_), custom_call_target="tpu_custom_call" | custom-call | tf_op jit(solution)/shard_map/chip_entries/pallas_call | solution.py:50
  57.9 23.9 %all-to-all-done.1.refs_0_ = bf16[16,4,32,128]{3,2,1,0:T(8,128)(2,1)S(1)} async-done(((bf16[16,4,32,128]{3,2,1,0:T(8,128)(2,1)}), bf16[16,4,32,128]{3,2,1,0:T(8,128)(2,1)S(1)}, u32[]{:S(2)}, u32[]{:S(2)}) %all-to-all-start.1) | async-done | bytes 524320 | tf_op jit(solution)/shard_map/all_to_all | solution.py:377
  81.7 0.0 copy-start.3
  81.7 1.2 copy-done.3
  83.0 1.0 chip_solve.1
  84.0 0.0 copy-start.4
  84.0 25.0 %all_to_all.31.refs_1_ = bf16[16,2,32,128]{3,2,1,0:T(8,128)(2,1)} all-to-all(bf16[16,2,32,128]{3,2,1,0:T(8,128)(2,1)S(1)} %get-tuple-element.21), channel_id=1, replica_groups=mesh['layer'=4,'row'=4,'zh'=4,'zl'=4,'core'=2] {'zh','zl'}, dimensions={0} | all-to-all | bytes 524288 | tf_op jit(solution)/shard_map/all_to_all | solution.py:377
  109.0 2.2 %all-gather.6.cloned.1.call-done = bf16[160,64,128]{2,1,0:T(8,128)(2,1)} async-done(((bf16[5,64,128]{2,1,0:T(8,128)(2,1)}), bf16[160,64,128]{2,1,0:T(8,128)(2,1)}) %all-gather.6.cloned.1.call-update) | async-done | bytes 2621456 | tf_op jit(solution)/shard_map/all_gather | solution.py:442
  111.2 7.2 %row_solve.1 = (bf16[4,512,128]{2,1,0:T(8,128)(2,1)}, f32[3,128,128]{2,1,0:T(8,128)}, f32[2,32,128]{2,1,0:T(8,128)}) custom-call(bf16[32,5,64,128]{3,2,1,0:T(8,128)(2,1)} %bitcast.11, bf16[16,2,32,128]{3,2,1,0:T(8,128)(2,1)} %all_to_all.31.refs_1_), custom_call_target="tpu_custom_call" | custom-call | tf_op jit(solution)/shard_map/row_solve/pallas_call | solution.py:50
  118.4 11.5 %all_to_all.32.refs_0_ = bf16[4,512,128]{2,1,0:T(8,128)(2,1)} all-to-all(bf16[4,512,128]{2,1,0:T(8,128)(2,1)} %get-tuple-element.22), channel_id=1, replica_groups=mesh['layer'=4,'row'=4,'zh'=4,'zl'=4,'core'=2] {'row'}, dimensions={0} | all-to-all | bytes 1048576 | tf_op jit(solution)/shard_map/all_to_all | solution.py:377
  129.9 0.0 copy-done.4
  129.9 3.1 %top_solve.1 = (f32[4,32,128]{2,1,0:T(8,128)}, bf16[16,4,32,128]{3,2,1,0:T(8,128)(2,1)}) custom-call(bf16[4,512,128]{2,1,0:T(8,128)(2,1)} %all_to_all.32.refs_0_, f32[3,128,128]{2,1,0:T(8,128)} %get-tuple-element.23.refs_1_, f32[2,32,128]{2,1,0:T(8,128)} %get-tuple-element.24.refs_2_, f32[256,512]{1,0:T(8,128)} %get-tuple-element.25.refs_3_, ...), custom_call_target="tpu_custom_call" | custom-call | tf_op jit(solution)/shard_map/top_solve/pallas_call | solution.py:50
  133.1 11.5 %all-to-all-start.4 = ((bf16[16,4,32,128]{3,2,1,0:T(8,128)(2,1)}), bf16[16,4,32,128]{3,2,1,0:T(8,128)(2,1)S(1)}, u32[]{:S(2)}, u32[]{:S(2)}) async-start(bf16[16,4,32,128]{3,2,1,0:T(8,128)(2,1)} %get-tuple-element.29), calls=%async_computation.4 | async-start | bytes 1048576 | tf_op jit(solution)/shard_map/all_to_all | solution.py:377
  144.6 15.6 %all-gather.1 = f32[32,32,128]{2,1,0:T(8,128)} all-gather(f32[4,32,128]{2,1,0:T(8,128)} %get-tuple-element.27), channel_id=3, replica_groups=mesh['layer'=4,'row'=4,'zh'=4,'zl'=4,'core'=2] {'layer','core'}, dimensions={0}, use_global_device_ids=true | all-gather | bytes 589824 | tf_op jit(solution)/shard_map/all_gather | solution.py:483
  160.2 0.0 all-gather.8.cloned.1.call-done
  160.2 0.0 copy-start
  160.2 1.7 copy-done
  162.0 0.0 copy-start.2
  162.0 1.0 copy-done.2
  163.0 0.0 copy-start.1
  163.0 0.8 turn_sep.1
  163.8 3.6 %all-to-all-done.4 = bf16[16,4,32,128]{3,2,1,0:T(8,128)(2,1)S(1)} async-done(((bf16[16,4,32,128]{3,2,1,0:T(8,128)(2,1)}), bf16[16,4,32,128]{3,2,1,0:T(8,128)(2,1)S(1)}, u32[]{:S(2)}, u32[]{:S(2)}) %all-to-all-start.4) | async-done | bytes 524320 | tf_op jit(solution)/shard_map/all_to_all | solution.py:377
  167.4 0.0 copy-done.1
  167.4 3.0 %leaf_backward.1 = bf16[8,2,32,128]{3,2,1,0:T(8,128)(2,1)S(1)} custom-call(s32[8,8]{1,0:T(8,128)S(1)} %get-tuple-element.28.refs_0_, bf16[64,32,128]{2,1,0:T(8,128)(2,1)S(1)} %bitcast.7, bf16[8,2,32,128]{3,2,1,0:T(8,128)(2,1)S(1)} %get-tuple-element.30.refs_2_, bf16[8,2,640,128]{3,2,1,0:T(8,128)(2,1)S(1)} %bitcast.6), custom_call_target="tpu_custom_call" | custom-call | tf_op jit(solution)/shard_map/leaf_backward/pallas_call | solution.py:50
  170.4 15.0 %all_to_all.33.refs_0_ = bf16[8,2,32,128]{3,2,1,0:T(8,128)(2,1)S(1)} all-to-all(bf16[8,2,32,128]{3,2,1,0:T(8,128)(2,1)S(1)} %leaf_backward.1), channel_id=1, replica_groups=mesh['layer'=4,'row'=4,'zh'=4,'zl'=4,'core'=2] {'layer','core'}, dimensions={0} | all-to-all | bytes 262144 | tf_op jit(solution)/shard_map/all_to_all | solution.py:377
  185.4 0.8 turn_leaf.1
  (1 shorter events, 0.0 us)
Async XLA Ops:
  7.2 104.0 %all-gather.6.cloned.1.call-start = ((), (), s32[]{:S(2)}) async-start(), calls=%async_computation.6 | async-start | bytes 2703360 | tf_op jit(solution)/shard_map/all_gather | solution.py:442
  9.8 11.8 %collective-permute-start = (f32[2,544,128]{2,1,0:T(8,128)}, f32[2,544,128]{2,1,0:T(8,128)S(1)}, u32[]{:S(2)}, u32[]{:S(2)}) collective-permute-start(f32[2,544,128]{2,1,0:T(8,128)} %get-tuple-element.18), channel_id=1, source_target_pairs={{0,1},{1,0},{2,3},{3,2},{4,5},{5,4},{6,7},{7,6},{8,9},{9,8},{10,11... | collective-permute-start | bytes 1671176 | tf_op jit(solution)/shard_map/ppermute | solution.py:415
  21.7 0.8 copy-start.5
  41.9 39.8 %all-to-all-start.1 = ((bf16[16,4,32,128]{3,2,1,0:T(8,128)(2,1)}), bf16[16,4,32,128]{3,2,1,0:T(8,128)(2,1)S(1)}, u32[]{:S(2)}, u32[]{:S(2)}) async-start(bf16[16,4,32,128]{3,2,1,0:T(8,128)(2,1)} %get-tuple-element.19.refs_2_), calls=%async_computation.1 | async-start | bytes 1048576 | tf_op jit(solution)/shard_map/all_to_all | solution.py:377
  52.6 107.6 %all-gather.8.cloned.1.call-start = ((), (), s32[]{:S(2)}) async-start(), calls=%async_computation.7 | async-start | bytes 2949120 | tf_op jit(solution)/shard_map/all_gather | solution.py:481
  81.7 1.3 copy-start.3
  84.0 45.9 %copy-start.4 = (f32[4,32,128]{2,1,0:T(8,128)}, f32[4,32,128]{2,1,0:T(8,128)S(1)}, u32[]{:S(2)}) copy-start(f32[4,32,128]{2,1,0:T(8,128)S(1)} %get-tuple-element.26.refs_4_) | copy-start | bytes 196612
  133.1 34.3 %all-to-all-start.4 = ((bf16[16,4,32,128]{3,2,1,0:T(8,128)(2,1)}), bf16[16,4,32,128]{3,2,1,0:T(8,128)(2,1)S(1)}, u32[]{:S(2)}, u32[]{:S(2)}) async-start(bf16[16,4,32,128]{3,2,1,0:T(8,128)(2,1)} %get-tuple-element.29), calls=%async_computation.4 | async-start | bytes 1048576 | tf_op jit(solution)/shard_map/all_to_all | solution.py:377
  160.2 1.7 copy-start
  162.0 1.0 copy-start.2
  163.0 4.4 %copy-start.1 = (bf16[16,640,128]{2,1,0:T(8,128)(2,1)S(1)}, bf16[16,640,128]{2,1,0:T(8,128)(2,1)}, u32[]{:S(2)}) copy-start(bf16[16,640,128]{2,1,0:T(8,128)(2,1)} %all-gather.8.cloned.1.call-done) | copy-start | bytes 7864324
Sparse Core Ops, SparseCore 0:
  25.5 85.6 all-gather.5
  113.3 31.8 all-gather.7

commit v6 on v5

--- a/solution.py
+++ b/solution.py
@@ -172,13 +172,15 @@
     send_half((reach, wys[0][B:], wys[0][:B]), half_ref, whole)
 
 
-def chip_entries(mine_ref, other_ref, half_ref, sep_ref, wy_ref):
-    _, wys = chip_dependence(mine_ref, other_ref, sep_ref)
+def chip_entries(mine_ref, other_ref, half_ref, wy_ref, seps):
+    _, wys = chip_dependence(mine_ref, other_ref, seps)
     for s in range(4):
         wy_ref[:, s * B : (s + 1) * B] = wys[s]
 
 
-def chip_solve(got_ref, sep_ref, bg_ref, local_ref):
+def chip_solve(got_ref, mine_ref, other_ref, bg_ref, local_ref, sep_ref):
+    sep_ref[lax.axis_index("core")] = mine_ref[...]
+    sep_ref[1 - lax.axis_index("core")] = other_ref[...]
     total = jnp.sum(got_ref[...].astype(f32), axis=0)
 
     def block(s, k):
@@ -433,10 +435,11 @@
         limit=VMEM_ALL,
         after=(sent,),
     )(mine, theirs)
-    seps, wy = call(
+    wy = call(
         chip_entries,
-        (shaped((2, 2, 4 * B + width, B), f32), shaped((2 * B, 4 * B), f32)),
-        name="chip_entries",
+        shaped((2 * B, 4 * B), f32),
+        [pltpu.VMEM((2, 2, 4 * B + width, B), f32)],
+        "chip_entries",
         limit=VMEM_ALL,
     )(mine, theirs, half)
     by_chip = lax.all_gather(half, along + ("core",)).reshape((2 * chips,) + half_maps.shape)
@@ -452,8 +455,11 @@
     )(place, got)
 
     bg, local = call(
-        chip_solve, (shaped((chips,) + pair, bf16), shaped((4, width, B), f32)), name="chip_solve"
-    )(exchange(sums, along), seps)
+        chip_solve,
+        (shaped((chips,) + pair, bf16), shaped((4, width, B), f32)),
+        [pltpu.VMEM((2, 2, 4 * B + width, B), f32)],
+        "chip_solve",
+    )(exchange(sums, along), mine, theirs)
     sent_on, xyz, own = call(
         row_solve,
         (shaped((rows, 3 * B + 4 * width, B), bf16), maps, shaped(pair, f32)),

time: 194 us -> 195 us (level)
  blocking collectives: 81.8 us -> 73.4 us
  waiting for transfers between devices: 29.7 us -> 36.1 us
  starting transfers between devices: 31 us -> 34.7 us
    all_to_all x4 -> x3, blocking collectives: 66.2 us -> 57.3 us  [exchange(): return lax.all_to_all(value, axes, split_axis=0, concat_axis=0, tiled=True)]
    all_to_all x2 -> x3, waiting for transfers between devices: 27.4 us -> 32.3 us  [exchange(): return lax.all_to_all(value, axes, split_axis=0, concat_axis=0, tiled=True)]
    all_to_all x2 -> x3, starting transfers between devices: 22.2 us -> 25.8 us  [exchange(): return lax.all_to_all(value, axes, split_axis=0, concat_axis=0, tiled=True)]
    unnamed x12 -> x16, local copies, waits for them, and re-layouts: 4.83 us -> 4.4 us
  transfers between devices with their start and end apart: 5 -> 6, of which waited for: 3 -> 4; matrix products, arithmetic and copies ran while one was open for 0% -> 0% of each run, Pallas kernels for 12% -> 11%
where the time goes in v6:
time: 195 us; the launch traced here: 194 us
  blocking collectives  73.4 us (38%)
  waiting for transfers between devices  36.1 us (19%)
  starting transfers between devices  34.7 us (18%)
  Pallas kernels  31.1 us (16%)
  between operations  14.1 us (7%)
  local copies, waits for them, and re-layouts  4.4 us (2%)
    all_to_all x3, blocking collectives, exchange(): return lax.all_to_all(value, axes, split_axis=0, concat_axis=0, tiled=True)  57.3 us
    all_to_all x3, waiting for transfers between devices, exchange(): return lax.all_to_all(value, axes, split_axis=0, concat_axis=0, tiled=True)  32.3 us
    pallas_call x12, Pallas kernels, run(): pl.pallas_call(body, out_shape=outs, in_specs=[pl.BlockSpec(memory_space=...  31.1 us
    all_to_all x3, starting transfers between devices, exchange(): return lax.all_to_all(value, axes, split_axis=0, concat_axis=0, tiled=True)  25.8 us
    all_gather x1, blocking collectives, on_device(): sep_all = lax.all_gather(solved, across).reshape((groups, 4, width, B))  16.1 us
    ppermute x1, starting transfers between devices, on_device(): theirs = lax.ppermute(others, 'core', [(0, 1), (1, 0)])  8.79 us
    unnamed x16, local copies, waits for them, and re-layouts  4.4 us
  transfers between devices with their start and end apart: 6, of which 4 were waited for; matrix products, arithmetic and copies ran while one was open for 0% of the time, Pallas kernels for 11%

profile of v6, /device:TPU:1, one launch (start us, length us, event | category | flops | bytes accessed | tf_op | source)
XLA Modules:
  0.0 193.8 jit_solution(10912189217621909420)
XLA Ops:
  7.2 0.0 all-gather.6.cloned.1.call-start
  7.2 2.6 %sep_prepare.1 = (f32[2,544,128]{2,1,0:T(8,128)}, f32[2,544,128]{2,1,0:T(8,128)}) custom-call(f32[2,128,128]{2,1,0:T(8,128)} %refs_0_.3, f32[2,128,128]{2,1,0:T(8,128)} %refs_1_.3, f32[2,128,128]{2,1,0:T(8,128)} %refs_2_.2, f32[2,128,128]{2,1,0:T(8,128)} %refs_3_.2, f32[2,128,256]{2,1,0:T(8,128)} %refs_4_.1), custom_call_target="tpu_custom_call" | custom-call | tf_op jit(solution)/shard_map/sep_prepare/pallas_call | solution.py:50
  9.8 8.8 %collective-permute-start = (f32[2,544,128]{2,1,0:T(8,128)}, f32[2,544,128]{2,1,0:T(8,128)S(1)}, u32[]{:S(2)}, u32[]{:S(2)}) collective-permute-start(f32[2,544,128]{2,1,0:T(8,128)} %get-tuple-element.16), channel_id=1, source_target_pairs={{0,1},{1,0},{2,3},{3,2},{4,5},{5,4},{6,7},{7,6},{8,9},{9,8},{10,11... | collective-permute-start | bytes 1671176 | tf_op jit(solution)/shard_map/ppermute | solution.py:417
  18.6 3.0 %leaf_forward.1.refs_2_ = bf16[8,336,128]{2,1,0:T(8,128)(2,1)} custom-call(s32[2,4]{1,0:T(2,128)} %refs_0_.4, bf16[2,128,256]{2,1,0:T(8,128)(2,1)} %refs_1_.4, bf16[2,128,128]{2,1,0:T(8,128)(2,1)} %refs_2_.3, bf16[2,4,128,128]{3,2,1,0:T(8,128)(2,1)} %refs_3_.3, f32[2,544,128]{2,1,0:T(8,128)} %get-tuple-element.15.refs_4_.refs_0_.refs_1_), custom_call_target="tpu_custom_call" | custom-call | tf_op jit(solution)/shard_map/leaf_forward/pallas_call | solution.py:50
  21.6 0.0 collective-permute-done.refs_1_.refs_2_
  21.6 0.0 copy-start.3
  21.7 0.8 copy-done.3
  22.5 2.9 %chip_maps.1.refs_2_ = bf16[5,64,128]{2,1,0:T(8,128)(2,1)} custom-call(f32[2,544,128]{2,1,0:T(8,128)} %get-tuple-element.15.refs_4_.refs_0_.refs_1_, f32[2,544,128]{2,1,0:T(8,128)} %copy-done.3, bf16[8,336,128]{2,1,0:T(8,128)(2,1)} %leaf_forward.1.refs_2_), custom_call_target="tpu_custom_call" | custom-call | tf_op jit(solution)/shard_map/chip_maps/pallas_call | solution.py:50
  25.4 0.0 copy-start.2
  25.4 0.0 copy-start.4
  25.4 0.0 all-gather.6.cloned.1.call-update
  25.4 14.8 %all_to_all.30.refs_1_ = bf16[8,336,128]{2,1,0:T(8,128)(2,1)S(1)} all-to-all(bf16[8,336,128]{2,1,0:T(8,128)(2,1)} %leaf_forward.1.refs_2_), channel_id=1, replica_groups=mesh['layer'=4,'row'=4,'zh'=4,'zl'=4,'core'=2] {'layer','core'}, dimensions={0} | all-to-all | bytes 1376256 | tf_op jit(solution)/shard_map/all_to_all | solution.py:379
  40.3 1.7 scatter_updates.1
  42.0 10.7 %all-to-all-start.1 = ((bf16[16,4,32,128]{3,2,1,0:T(8,128)(2,1)}), bf16[16,4,32,128]{3,2,1,0:T(8,128)(2,1)S(1)}, u32[]{:S(2)}, u32[]{:S(2)}) async-start(bf16[16,4,32,128]{3,2,1,0:T(8,128)(2,1)} %get-tuple-element.17.refs_2_), calls=%async_computation.1 | async-start | bytes 1048576 | tf_op jit(solution)/shard_map/all_to_all | solution.py:379
  52.7 0.0 all-gather.8.cloned.1.call-start
  52.7 1.8 join_upper.1
  54.6 0.0 all-gather.8.cloned.1.call-update
  54.6 25.4 %all-to-all-done.1.refs_0_ = bf16[16,4,32,128]{3,2,1,0:T(8,128)(2,1)S(1)} async-done(((bf16[16,4,32,128]{3,2,1,0:T(8,128)(2,1)}), bf16[16,4,32,128]{3,2,1,0:T(8,128)(2,1)S(1)}, u32[]{:S(2)}, u32[]{:S(2)}) %all-to-all-start.1) | async-done | bytes 524320 | tf_op jit(solution)/shard_map/all_to_all | solution.py:379
  80.0 0.0 copy-done.2
  80.0 0.0 copy-done.4
  80.0 1.0 chip_solve.1
  81.0 0.0 copy-start.6
  81.1 26.4 %all_to_all.31.refs_1_ = bf16[16,2,32,128]{3,2,1,0:T(8,128)(2,1)} all-to-all(bf16[16,2,32,128]{3,2,1,0:T(8,128)(2,1)S(1)} %get-tuple-element.18), channel_id=1, replica_groups=mesh['layer'=4,'row'=4,'zh'=4,'zl'=4,'core'=2] {'zh','zl'}, dimensions={0} | all-to-all | bytes 524288 | tf_op jit(solution)/shard_map/all_to_all | solution.py:379
  107.4 3.7 %all-gather.6.cloned.1.call-done = bf16[160,64,128]{2,1,0:T(8,128)(2,1)} async-done(((bf16[5,64,128]{2,1,0:T(8,128)(2,1)}), bf16[160,64,128]{2,1,0:T(8,128)(2,1)}) %all-gather.6.cloned.1.call-update) | async-done | bytes 2621456 | tf_op jit(solution)/shard_map/all_gather | solution.py:445
  111.1 7.2 %row_solve.1 = (bf16[4,512,128]{2,1,0:T(8,128)(2,1)}, f32[3,128,128]{2,1,0:T(8,128)}, f32[2,32,128]{2,1,0:T(8,128)}) custom-call(bf16[32,5,64,128]{3,2,1,0:T(8,128)(2,1)} %bitcast.11, bf16[16,2,32,128]{3,2,1,0:T(8,128)(2,1)} %all_to_all.31.refs_1_), custom_call_target="tpu_custom_call" | custom-call | tf_op jit(solution)/shard_map/row_solve/pallas_call | solution.py:50
  118.3 4.2 %all-to-all-start.3 = ((bf16[4,512,128]{2,1,0:T(8,128)(2,1)}), bf16[4,512,128]{2,1,0:T(8,128)(2,1)S(1)}, u32[]{:S(2)}, u32[]{:S(2)}) async-start(bf16[4,512,128]{2,1,0:T(8,128)(2,1)} %get-tuple-element.19), calls=%async_computation.3 | async-start | bytes 1048576 | tf_op jit(solution)/shard_map/all_to_all | solution.py:379
  122.5 3.1 %chip_entries.1.refs_3_ = f32[256,512]{1,0:T(8,128)} custom-call(f32[2,544,128]{2,1,0:T(8,128)} %get-tuple-element.15.refs_4_.refs_0_.refs_1_, f32[2,544,128]{2,1,0:T(8,128)} %copy-done.3, bf16[5,64,128]{2,1,0:T(8,128)(2,1)} %chip_maps.1.refs_2_), custom_call_target="tpu_custom_call" | custom-call | tf_op jit(solution)/shard_map/chip_entries/pallas_call | solution.py:50
  125.6 0.0 copy-done.6
  125.6 3.9 %all-to-all-done.3.refs_0_ = bf16[4,512,128]{2,1,0:T(8,128)(2,1)S(1)} async-done(((bf16[4,512,128]{2,1,0:T(8,128)(2,1)}), bf16[4,512,128]{2,1,0:T(8,128)(2,1)S(1)}, u32[]{:S(2)}, u32[]{:S(2)}) %all-to-all-start.3) | async-done | bytes 524320 | tf_op jit(solution)/shard_map/all_to_all | solution.py:379
  129.4 0.0 copy-start.7
  129.4 0.8 copy-done.7
  130.2 3.2 %top_solve.1 = (f32[4,32,128]{2,1,0:T(8,128)}, bf16[16,4,32,128]{3,2,1,0:T(8,128)(2,1)}) custom-call(bf16[4,512,128]{2,1,0:T(8,128)(2,1)} %copy-done.7, f32[3,128,128]{2,1,0:T(8,128)} %get-tuple-element.20.refs_1_, f32[2,32,128]{2,1,0:T(8,128)} %get-tuple-element.21.refs_2_, f32[256,512]{1,0:T(8,128)} %chip_entries.1.refs_3_, f32[4,32,128]{2,1,0:T(8,128)} %copy-done.6), custom_call_target="tpu_custom_call" | custom-call | tf_op jit(solution)/shard_map/top_solve/pallas_call | solution.py:50
  133.4 11.0 %all-to-all-start.4 = ((bf16[16,4,32,128]{3,2,1,0:T(8,128)(2,1)}), bf16[16,4,32,128]{3,2,1,0:T(8,128)(2,1)S(1)}, u32[]{:S(2)}, u32[]{:S(2)}) async-start(bf16[16,4,32,128]{3,2,1,0:T(8,128)(2,1)} %get-tuple-element.25), calls=%async_computation.4 | async-start | bytes 1048576 | tf_op jit(solution)/shard_map/all_to_all | solution.py:379
  144.4 16.1 %all-gather.1 = f32[32,32,128]{2,1,0:T(8,128)} all-gather(f32[4,32,128]{2,1,0:T(8,128)} %get-tuple-element.23), channel_id=3, replica_groups=mesh['layer'=4,'row'=4,'zh'=4,'zl'=4,'core'=2] {'layer','core'}, dimensions={0}, use_global_device_ids=true | all-gather | bytes 589824 | tf_op jit(solution)/shard_map/all_gather | solution.py:489
  160.5 0.0 all-gather.8.cloned.1.call-done
  160.5 0.0 copy-start
  160.5 1.7 copy-done
  162.2 0.0 copy-start.5
  162.2 1.0 copy-done.5
  163.3 0.0 copy-start.1
  163.3 0.8 turn_sep.1
  164.1 3.1 %all-to-all-done.4 = bf16[16,4,32,128]{3,2,1,0:T(8,128)(2,1)S(1)} async-done(((bf16[16,4,32,128]{3,2,1,0:T(8,128)(2,1)}), bf16[16,4,32,128]{3,2,1,0:T(8,128)(2,1)S(1)}, u32[]{:S(2)}, u32[]{:S(2)}) %all-to-all-start.4) | async-done | bytes 524320 | tf_op jit(solution)/shard_map/all_to_all | solution.py:379
  167.2 0.0 copy-done.1
  167.2 3.0 %leaf_backward.1 = bf16[8,2,32,128]{3,2,1,0:T(8,128)(2,1)S(1)} custom-call(s32[8,8]{1,0:T(8,128)S(1)} %get-tuple-element.24.refs_0_, bf16[64,32,128]{2,1,0:T(8,128)(2,1)S(1)} %bitcast.7, bf16[8,2,32,128]{3,2,1,0:T(8,128)(2,1)S(1)} %get-tuple-element.26.refs_2_, bf16[8,2,640,128]{3,2,1,0:T(8,128)(2,1)S(1)} %bitcast.6), custom_call_target="tpu_custom_call" | custom-call | tf_op jit(solution)/shard_map/leaf_backward/pallas_call | solution.py:50
  170.1 16.1 %all_to_all.32.refs_0_ = bf16[8,2,32,128]{3,2,1,0:T(8,128)(2,1)S(1)} all-to-all(bf16[8,2,32,128]{3,2,1,0:T(8,128)(2,1)S(1)} %leaf_backward.1), channel_id=1, replica_groups=mesh['layer'=4,'row'=4,'zh'=4,'zl'=4,'core'=2] {'layer','core'}, dimensions={0} | all-to-all | bytes 262144 | tf_op jit(solution)/shard_map/all_to_all | solution.py:379
  186.2 0.8 turn_leaf.1
  (1 shorter events, 0.0 us)
Async XLA Ops:
  7.2 104.0 %all-gather.6.cloned.1.call-start = ((), (), s32[]{:S(2)}) async-start(), calls=%async_computation.6 | async-start | bytes 2703360 | tf_op jit(solution)/shard_map/all_gather | solution.py:445
  9.8 11.8 %collective-permute-start = (f32[2,544,128]{2,1,0:T(8,128)}, f32[2,544,128]{2,1,0:T(8,128)S(1)}, u32[]{:S(2)}, u32[]{:S(2)}) collective-permute-start(f32[2,544,128]{2,1,0:T(8,128)} %get-tuple-element.16), channel_id=1, source_target_pairs={{0,1},{1,0},{2,3},{3,2},{4,5},{5,4},{6,7},{7,6},{8,9},{9,8},{10,11... | collective-permute-start | bytes 1671176 | tf_op jit(solution)/shard_map/ppermute | solution.py:417
  21.6 0.8 copy-start.3
  25.4 54.6 %copy-start.2 = (f32[2,544,128]{2,1,0:T(8,128)S(1)}, f32[2,544,128]{2,1,0:T(8,128)}, u32[]{:S(2)}) copy-start(f32[2,544,128]{2,1,0:T(8,128)} %get-tuple-element.15.refs_4_.refs_0_.refs_1_) | copy-start | bytes 1671172
  25.4 54.6 %copy-start.4 = (f32[2,544,128]{2,1,0:T(8,128)S(1)}, f32[2,544,128]{2,1,0:T(8,128)}, u32[]{:S(2)}) copy-start(f32[2,544,128]{2,1,0:T(8,128)} %copy-done.3) | copy-start | bytes 1671172
  42.0 38.0 %all-to-all-start.1 = ((bf16[16,4,32,128]{3,2,1,0:T(8,128)(2,1)}), bf16[16,4,32,128]{3,2,1,0:T(8,128)(2,1)S(1)}, u32[]{:S(2)}, u32[]{:S(2)}) async-start(bf16[16,4,32,128]{3,2,1,0:T(8,128)(2,1)} %get-tuple-element.17.refs_2_), calls=%async_computation.1 | async-start | bytes 1048576 | tf_op jit(solution)/shard_map/all_to_all | solution.py:379
  52.7 107.8 %all-gather.8.cloned.1.call-start = ((), (), s32[]{:S(2)}) async-start(), calls=%async_computation.7 | async-start | bytes 2949120 | tf_op jit(solution)/shard_map/all_gather | solution.py:487
  81.0 44.5 %copy-start.6 = (f32[4,32,128]{2,1,0:T(8,128)}, f32[4,32,128]{2,1,0:T(8,128)S(1)}, u32[]{:S(2)}) copy-start(f32[4,32,128]{2,1,0:T(8,128)S(1)} %get-tuple-element.22.refs_4_) | copy-start | bytes 196612
  118.3 11.1 %all-to-all-start.3 = ((bf16[4,512,128]{2,1,0:T(8,128)(2,1)}), bf16[4,512,128]{2,1,0:T(8,128)(2,1)S(1)}, u32[]{:S(2)}, u32[]{:S(2)}) async-start(bf16[4,512,128]{2,1,0:T(8,128)(2,1)} %get-tuple-element.19), calls=%async_computation.3 | async-start | bytes 1048576 | tf_op jit(solution)/shard_map/all_to_all | solution.py:379
  129.4 0.8 copy-start.7
  133.4 33.8 %all-to-all-start.4 = ((bf16[16,4,32,128]{3,2,1,0:T(8,128)(2,1)}), bf16[16,4,32,128]{3,2,1,0:T(8,128)(2,1)S(1)}, u32[]{:S(2)}, u32[]{:S(2)}) async-start(bf16[16,4,32,128]{3,2,1,0:T(8,128)(2,1)} %get-tuple-element.25), calls=%async_computation.4 | async-start | bytes 1048576 | tf_op jit(solution)/shard_map/all_to_all | solution.py:379
  160.5 1.7 copy-start
  162.2 1.0 copy-start.5
  163.3 3.9 %copy-start.1 = (bf16[16,640,128]{2,1,0:T(8,128)(2,1)S(1)}, bf16[16,640,128]{2,1,0:T(8,128)(2,1)}, u32[]{:S(2)}) copy-start(bf16[16,640,128]{2,1,0:T(8,128)(2,1)} %all-gather.8.cloned.1.call-done) | copy-start | bytes 7864324
Sparse Core Ops, SparseCore 0:
  25.5 85.5 all-gather.5
  113.3 32.1 all-gather.7
